TPU v7x, 128 devices: a whole 4x4x4 slice. The times are simulated.
128 devices in a mesh: head: 8 (over x_hi, y), blk: 16 (over x_lo, z, core).
Axes of the slice: x: 4 (x_hi: 2, x_lo: 2; x = x_hi * 2 + x_lo), y: 4, z: 4, core: 2. Of those that a mesh axis runs over, the one named last changes fastest.
Arguments:
- tokens: bfloat16 [16384, 1024], P(('blk', 'head')), may hold values from -24 to 24
- cotangent: bfloat16 [16384, 1024], P(('blk', 'head')), may hold values from -6 to 6
- segments: int32 [16384], replicated, may hold values from 0 to 6, as said below
- attn_gain: bfloat16 [1024], P(('head', 'blk')), may hold values from 0.5 to 1.5
- w_query: bfloat16 [1024, 2048], P(('head', 'blk')), may hold values from -0.1875 to 0.1875
- key_matrix: bfloat16 [1024, 1024], P(('head', 'blk')), may hold values from -0.1875 to 0.1875
- value_matrix: bfloat16 [1024, 1024], P(('head', 'blk')), may hold values from -0.1875 to 0.1875
- query_gain: bfloat16 [128], P(('head', 'blk')), may hold values from 1 to 2
- key_gain: bfloat16 [128], P(('head', 'blk')), may hold values from 1 to 2
- w_out: bfloat16 [2048, 1024], P(('head', 'blk')), may hold values from -2 to 2
- ffn_gain: bfloat16 [1024], P(('head', 'blk')), may hold values from 0.5 to 1.5
- w_gate: bfloat16 [1024, 3072], P(('head', 'blk')), may hold values from -0.1875 to 0.1875
- w_up: bfloat16 [1024, 3072], P(('head', 'blk')), may hold values from -0.1875 to 0.1875
- w_down: bfloat16 [3072, 1024], P(('head', 'blk')), may hold values from -0.109375 to 0.109375
Outputs:
- output: bfloat16 [16384, 1024], P(('blk', 'head'))
- input_grad: bfloat16 [16384, 1024], P(('blk', 'head'))
- grad_attn_gain: float32 [1024], P(('head', 'blk'))
- grad_query: float32 [1024, 2048], P(('head', 'blk'))
- grad_key: float32 [1024, 1024], P(('head', 'blk'))
- grad_value: float32 [1024, 1024], P(('head', 'blk'))
- grad_query_gain: float32 [128], P(('head', 'blk'))
- grad_key_gain: float32 [128], P(('head', 'blk'))
- grad_out: float32 [2048, 1024], P(('head', 'blk'))
- grad_ffn_gain: float32 [1024], P(('head', 'blk'))
- grad_gate: float32 [1024, 3072], P(('head', 'blk'))
- grad_up: float32 [1024, 3072], P(('head', 'blk'))
- grad_down: float32 [3072, 1024], P(('head', 'blk'))
Inputs may be any that keep to these rules, and one draw needn't show every extreme that they name: `segments`: ids never fall along the sequence; one document starts within the first 1024 tokens and ends within the last 1024 tokens, the others lie inside those two stretches.
All inputs are finite; a program needn't handle non-finite values.
Results may differ from a plain program's by a relative error of at most 0.035.
Values may be sent and summed in bfloat16 or wider, within the bound.
A program may use at most 128 MiB of HBM per device.

v0:
```python
from functools import partial

import jax
import jax.numpy as jnp
from jax import lax
from jax.sharding import PartitionSpec as P

QUERY_HEADS = 16
KEY_VALUE_HEADS = 8
HEAD_SIZE = 128
ATTENTION_SPAN = 1024


norm_eps = 1e-06
rope_base = 1000000.0
tile_most = 512
masked_score = -1e30


def from_behind(x, axis, by):
    peers = lax.axis_size(axis)
    pairs = [(i, i + by) for i in range(peers) if 0 <= i + by < peers]
    return lax.ppermute(x, axis, pairs)


def rms_scale(value_rows):
    return lax.rsqrt(jnp.mean(value_rows * value_rows, axis=-1, keepdims=True) + norm_eps)


def rotary_tables(first_row, row_count):
    places = (first_row + jnp.arange(row_count, dtype=jnp.int32)).astype(jnp.float32)
    inverse_freq = rope_base ** (-jnp.arange(0, HEAD_SIZE, 2, dtype=jnp.float32) / HEAD_SIZE)
    angles = places[:, None] * inverse_freq[None, :]
    angles = jnp.concatenate([angles, angles], axis=-1)
    return (jnp.cos(angles)[:, None, :], jnp.sin(angles)[:, None, :])


def rotate_half(value_rows):
    half_width = value_rows.shape[-1] // 2
    return jnp.concatenate([-value_rows[..., half_width:], value_rows[..., :half_width]], axis=-1)


def head_prep(raw_heads, gain_vec, cos_table, sin_table):
    normed = raw_heads * rms_scale(raw_heads) * gain_vec
    return normed * cos_table + rotate_half(normed) * sin_table


def prep_pair(q_in, k_in, q_gain, k_gain, cos_table, sin_table):
    return (
        head_prep(q_in, q_gain, cos_table, sin_table),
        head_prep(k_in, k_gain, cos_table, sin_table),
    )


def norm_back(d_normed, unit_rows, scale_rows, gain_vec):
    d_unit = d_normed * gain_vec
    return scale_rows * (d_unit - unit_rows * jnp.mean(d_unit * unit_rows, axis=-1, keepdims=True))


def rows_in(value_rows):
    return lax.all_gather(value_rows, "head", axis=0, tiled=True)


def rows_out(value_rows):
    return lax.psum_scatter(
        value_rows.astype(jnp.bfloat16), "head", scatter_dimension=0, tiled=True
    ).astype(jnp.float32)


def permute_cols(value_rows, head_number, blocks_n):
    row_count = value_rows.shape[0]
    return (
        value_rows.reshape(row_count, head_number, blocks_n, -1)
        .transpose(0, 2, 1, 3)
        .reshape(row_count, -1)
    )


def restore_cols(value_rows, head_number, blocks_n):
    row_count = value_rows.shape[0]
    return (
        value_rows.reshape(row_count, blocks_n, head_number, -1)
        .transpose(0, 2, 1, 3)
        .reshape(row_count, -1)
    )


def local(
    tokens,
    cotangent,
    segments,
    attn_gain,
    w_query,
    key_matrix,
    value_matrix,
    query_gain,
    key_gain,
    w_out,
    ffn_gain,
    w_gate,
    w_up,
    w_down,
):
    head_number = lax.axis_size("head")
    blocks_n = lax.axis_size("blk")
    token_rows = tokens.shape[0]
    query_nearby = QUERY_HEADS // head_number
    key_value_nearby = KEY_VALUE_HEADS // head_number
    query_cluster = QUERY_HEADS // KEY_VALUE_HEADS
    block_rows = token_rows * head_number
    block_first = lax.axis_index("blk") * block_rows
    tile_rows = min(tile_most, block_rows)
    tile_count = block_rows // tile_rows
    slab_rows = tile_rows + ATTENTION_SPAN
    cycle_hops = -(-ATTENTION_SPAN // block_rows)
    attn_scale = HEAD_SIZE ** (-0.5)
    seg_padded = jnp.concatenate([jnp.full((cycle_hops * block_rows,), -1, jnp.int32), segments])
    seg_ext = lax.dynamic_slice_in_dim(seg_padded, block_first, (cycle_hops + 1) * block_rows, 0)
    seg_query = lax.dynamic_slice_in_dim(segments, block_first, block_rows, 0)

    def tile_scores(tile_index, q_tile, k_ext):
        offset = tile_index * tile_rows
        slab_start = cycle_hops * block_rows + offset - ATTENTION_SPAN
        k_slab = lax.dynamic_slice_in_dim(k_ext, slab_start, slab_rows, 0)
        seg_keys = lax.dynamic_slice_in_dim(seg_ext, slab_start, slab_rows, 0)
        seg_rows = lax.dynamic_slice_in_dim(seg_query, offset, tile_rows, 0)
        key_gap = (
            jnp.arange(tile_rows, dtype=jnp.int32)[:, None]
            + ATTENTION_SPAN
            - jnp.arange(slab_rows, dtype=jnp.int32)[None, :]
        )
        allowed = (
            (key_gap >= 0) & (key_gap < ATTENTION_SPAN) & (seg_rows[:, None] == seg_keys[None, :])
        )
        scores = (
            jnp.einsum("qkgd,ckd->kgqc", q_tile, k_slab, preferred_element_type=jnp.float32)
            * attn_scale
        )
        scores = jnp.where(allowed[None, None], scores, masked_score)
        return (scores, k_slab, slab_start)

    gains = (
        lax.all_gather(attn_gain, ("head", "blk"), axis=0, tiled=True),
        lax.all_gather(query_gain, ("head", "blk"), axis=0, tiled=True),
        lax.all_gather(key_gain, ("head", "blk"), axis=0, tiled=True),
        lax.all_gather(ffn_gain, ("head", "blk"), axis=0, tiled=True),
    )
    attn_g, qgain_full, kgain_full, ffn_g = gains
    col_parts = (
        lax.all_to_all(w_query, "head", split_axis=1, concat_axis=0, tiled=True),
        lax.all_to_all(key_matrix, "head", split_axis=1, concat_axis=0, tiled=True),
        lax.all_to_all(value_matrix, "head", split_axis=1, concat_axis=0, tiled=True),
        lax.all_to_all(w_gate, "head", split_axis=1, concat_axis=0, tiled=True),
        lax.all_to_all(w_up, "head", split_axis=1, concat_axis=0, tiled=True),
    )
    local_parts = (
        lax.all_gather(col_parts[0], "blk", axis=0, tiled=True),
        lax.all_gather(col_parts[1], "blk", axis=0, tiled=True),
        lax.all_gather(col_parts[2], "blk", axis=0, tiled=True),
        lax.all_gather(col_parts[3], "blk", axis=0, tiled=True),
        lax.all_gather(col_parts[4], "blk", axis=0, tiled=True),
        lax.all_gather(w_out, "blk", axis=0, tiled=True),
        lax.all_gather(w_down, "blk", axis=0, tiled=True),
    )
    query_full, key_full, value_full, gate_full, up_full, out_full, down_full = local_parts
    attn_gf = attn_g.astype(jnp.float32)
    ffn_gf = ffn_g.astype(jnp.float32)
    qgain_f = qgain_full.astype(jnp.float32)
    kgain_f = kgain_full.astype(jnp.float32)
    x_float = tokens.astype(jnp.float32)
    scale_one = rms_scale(x_float)
    x_unit = x_float * scale_one
    input_normalized = (x_unit * attn_gf).astype(jnp.bfloat16)
    x_block = rows_in(permute_cols(input_normalized, head_number, blocks_n))
    q_raw = jnp.dot(x_block, query_full, preferred_element_type=jnp.float32).reshape(
        block_rows, query_nearby, HEAD_SIZE
    )
    key_unrotated = jnp.dot(x_block, key_full, preferred_element_type=jnp.float32).reshape(
        block_rows, key_value_nearby, HEAD_SIZE
    )
    v_loc = (
        jnp.dot(x_block, value_full, preferred_element_type=jnp.float32)
        .astype(jnp.bfloat16)
        .reshape(block_rows, key_value_nearby, HEAD_SIZE)
    )
    cos_table, sin_table = rotary_tables(block_first, block_rows)
    (q_rot, k_rot), prep_back = jax.vjp(
        partial(prep_pair, cos_table=cos_table, sin_table=sin_table),
        q_raw,
        key_unrotated,
        qgain_f,
        kgain_f,
    )
    k_loc = k_rot.astype(jnp.bfloat16)
    earlier = []
    moving_k = k_loc
    moving_v = v_loc
    moving_k, moving_v = from_behind((moving_k, moving_v), "blk", 1)
    earlier = [(moving_k, moving_v)] + earlier
    k_ext = jnp.concatenate([kv_pair[0] for kv_pair in earlier] + [k_loc], axis=0)
    v_ext = jnp.concatenate([kv_pair[1] for kv_pair in earlier] + [v_loc], axis=0)
    q_tiles = q_rot.astype(jnp.bfloat16).reshape(
        tile_count, tile_rows, key_value_nearby, query_cluster, HEAD_SIZE
    )

    def forward_tile(tile_index):
        q_tile = lax.dynamic_index_in_dim(q_tiles, tile_index, 0, keepdims=False)
        scores, k_slab, slab_start = tile_scores(tile_index, q_tile, k_ext)
        v_slab = lax.dynamic_slice_in_dim(v_ext, slab_start, slab_rows, 0)
        row_peak = jnp.max(scores, axis=-1, keepdims=True)
        exp_scores = jnp.exp(scores - row_peak)
        row_total = jnp.sum(exp_scores, axis=-1, keepdims=True)
        attn_probs = (exp_scores / row_total).astype(jnp.bfloat16)
        tile_out = jnp.einsum(
            "kgqc,ckd->qkgd", attn_probs, v_slab, preferred_element_type=jnp.float32
        )
        return (tile_out.astype(jnp.bfloat16), row_peak + jnp.log(row_total))

    attended, log_totals = lax.map(forward_tile, jnp.arange(tile_count, dtype=jnp.int32))
    attended_loc = attended.reshape(block_rows, query_nearby, HEAD_SIZE)
    attn_block = attended_loc.reshape(block_rows, query_nearby * HEAD_SIZE)
    mid_sum = x_float + rows_out(jnp.dot(attn_block, out_full, preferred_element_type=jnp.float32))
    scale_two = rms_scale(mid_sum)
    mid_unit = mid_sum * scale_two
    mid_normed = (mid_unit * ffn_gf).astype(jnp.bfloat16)
    mid_block = rows_in(permute_cols(mid_normed, head_number, blocks_n))
    gate_val = jnp.dot(mid_block, gate_full, preferred_element_type=jnp.float32)
    up_val = jnp.dot(mid_block, up_full, preferred_element_type=jnp.float32)
    gate_sig = jax.nn.sigmoid(gate_val)
    gate_act = gate_val * gate_sig
    hidden = (gate_act * up_val).astype(jnp.bfloat16)
    output = (
        mid_sum + rows_out(jnp.dot(hidden, down_full, preferred_element_type=jnp.float32))
    ).astype(jnp.bfloat16)
    cot_block = rows_in(cotangent)
    grad_down = jnp.einsum("tf,td->fd", hidden, cot_block, preferred_element_type=jnp.float32)
    d_hidden = jnp.einsum("td,fd->tf", cot_block, down_full, preferred_element_type=jnp.float32)
    d_gate = (d_hidden * up_val * gate_sig * (1.0 + gate_val * (1.0 - gate_sig))).astype(
        jnp.bfloat16
    )
    d_up = (d_hidden * gate_act).astype(jnp.bfloat16)
    grad_gate = jnp.einsum("td,tf->df", mid_block, d_gate, preferred_element_type=jnp.float32)
    grad_up = jnp.einsum("td,tf->df", mid_block, d_up, preferred_element_type=jnp.float32)
    mid_partial = jnp.einsum(
        "tf,df->td", d_gate, gate_full, preferred_element_type=jnp.float32
    ) + jnp.einsum("tf,df->td", d_up, up_full, preferred_element_type=jnp.float32)
    d_mid_normed = rows_out(restore_cols(mid_partial, head_number, blocks_n))
    grad_ffn = jnp.sum(d_mid_normed * mid_unit, axis=0)
    d_mid = cotangent.astype(jnp.float32) + norm_back(d_mid_normed, mid_unit, scale_two, ffn_gf)
    branch_block = rows_in(d_mid.astype(jnp.bfloat16))
    grad_wout = jnp.einsum(
        "tk,td->kd", attn_block, branch_block, preferred_element_type=jnp.float32
    )
    d_attended = (
        jnp.einsum("td,kd->tk", branch_block, out_full, preferred_element_type=jnp.float32)
        .astype(jnp.bfloat16)
        .reshape(block_rows, query_nearby, HEAD_SIZE)
    )
    attention_q_tiles, attention_k_ext, attention_v_ext, log_totals = (
        q_tiles,
        k_ext,
        v_ext,
        log_totals,
    )
    d_tiles = d_attended.reshape(tile_count, tile_rows, key_value_nearby, query_cluster, HEAD_SIZE)

    def backward_tile(running, tile_index):
        dk_acc, dv_acc = running
        q_tile = lax.dynamic_index_in_dim(attention_q_tiles, tile_index, 0, keepdims=False)
        d_tile = lax.dynamic_index_in_dim(d_tiles, tile_index, 0, keepdims=False)
        log_tile = lax.dynamic_index_in_dim(log_totals, tile_index, 0, keepdims=False)
        scores, k_slab, slab_start = tile_scores(tile_index, q_tile, attention_k_ext)
        v_slab = lax.dynamic_slice_in_dim(attention_v_ext, slab_start, slab_rows, 0)
        attn_probs = jnp.exp(scores - log_tile)
        dv_part = jnp.einsum(
            "kgqc,qkgd->ckd",
            attn_probs.astype(jnp.bfloat16),
            d_tile,
            preferred_element_type=jnp.float32,
        )
        d_probs = jnp.einsum("qkgd,ckd->kgqc", d_tile, v_slab, preferred_element_type=jnp.float32)
        row_inner = jnp.sum(attn_probs * d_probs, axis=-1, keepdims=True)
        d_scores = (attn_probs * (d_probs - row_inner)).astype(jnp.bfloat16)
        dq_tile = (
            jnp.einsum("kgqc,ckd->qkgd", d_scores, k_slab, preferred_element_type=jnp.float32)
            * attn_scale
        )
        dk_part = (
            jnp.einsum("kgqc,qkgd->ckd", d_scores, q_tile, preferred_element_type=jnp.float32)
            * attn_scale
        )
        dk_acc = lax.dynamic_update_slice_in_dim(
            dk_acc,
            lax.dynamic_slice_in_dim(dk_acc, slab_start, slab_rows, 0) + dk_part,
            slab_start,
            0,
        )
        dv_acc = lax.dynamic_update_slice_in_dim(
            dv_acc,
            lax.dynamic_slice_in_dim(dv_acc, slab_start, slab_rows, 0) + dv_part,
            slab_start,
            0,
        )
        return ((dk_acc, dv_acc), dq_tile.astype(jnp.bfloat16))

    zeros_ext = jnp.zeros(((cycle_hops + 1) * block_rows, key_value_nearby, HEAD_SIZE), jnp.float32)
    (dk_acc, dv_acc), dq_tiles = lax.scan(
        backward_tile, (zeros_ext, zeros_ext), jnp.arange(tile_count, dtype=jnp.int32)
    )
    back_k = from_behind(dk_acc[0 : 0 + block_rows].astype(jnp.bfloat16), "blk", -1).astype(
        jnp.float32
    )
    back_v = from_behind(dv_acc[0 : 0 + block_rows].astype(jnp.bfloat16), "blk", -1).astype(
        jnp.float32
    )
    own_row = cycle_hops * block_rows
    dk_loc = (dk_acc[own_row:] + back_k).astype(jnp.bfloat16)
    dv_loc = (dv_acc[own_row:] + back_v).astype(jnp.bfloat16)
    dq_loc, dk_loc, dv_loc = (dq_tiles.reshape(block_rows, query_nearby, HEAD_SIZE), dk_loc, dv_loc)
    dq_raw, key_gradient_unrotated, grad_qgain, grad_kgain = prep_back(
        (dq_loc.astype(jnp.float32), dk_loc.astype(jnp.float32))
    )
    dq_low = dq_raw.astype(jnp.bfloat16).reshape(block_rows, query_nearby * HEAD_SIZE)
    key_gradient_lower = key_gradient_unrotated.astype(jnp.bfloat16).reshape(
        block_rows, key_value_nearby * HEAD_SIZE
    )
    value_gradient_lower = dv_loc.reshape(block_rows, key_value_nearby * HEAD_SIZE)
    grad_wq = jnp.einsum("td,tk->dk", x_block, dq_low, preferred_element_type=jnp.float32)
    grad_wk = jnp.einsum(
        "td,tk->dk", x_block, key_gradient_lower, preferred_element_type=jnp.float32
    )
    grad_wv = jnp.einsum(
        "td,tk->dk", x_block, value_gradient_lower, preferred_element_type=jnp.float32
    )
    x_partial = jnp.einsum("tk,dk->td", dq_low, query_full, preferred_element_type=jnp.float32)
    x_partial = x_partial + jnp.einsum(
        "tk,dk->td", key_gradient_lower, key_full, preferred_element_type=jnp.float32
    )
    x_partial = x_partial + jnp.einsum(
        "tk,dk->td", value_gradient_lower, value_full, preferred_element_type=jnp.float32
    )
    d_x_normed = rows_out(restore_cols(x_partial, head_number, blocks_n))
    grad_attn = jnp.sum(d_x_normed * x_unit, axis=0)
    input_grad = (d_mid + norm_back(d_x_normed, x_unit, scale_one, attn_gf)).astype(jnp.bfloat16)
    row_sums = (
        lax.psum_scatter(
            grad_wq.astype(jnp.bfloat16), "blk", scatter_dimension=0, tiled=True
        ).astype(jnp.float32),
        lax.psum_scatter(
            grad_wk.astype(jnp.bfloat16), "blk", scatter_dimension=0, tiled=True
        ).astype(jnp.float32),
        lax.psum_scatter(
            grad_wv.astype(jnp.bfloat16), "blk", scatter_dimension=0, tiled=True
        ).astype(jnp.float32),
        lax.psum_scatter(
            grad_gate.astype(jnp.bfloat16), "blk", scatter_dimension=0, tiled=True
        ).astype(jnp.float32),
        lax.psum_scatter(
            grad_up.astype(jnp.bfloat16), "blk", scatter_dimension=0, tiled=True
        ).astype(jnp.float32),
        lax.psum_scatter(
            grad_wout.astype(jnp.bfloat16), "blk", scatter_dimension=0, tiled=True
        ).astype(jnp.float32),
        lax.psum_scatter(
            grad_down.astype(jnp.bfloat16), "blk", scatter_dimension=0, tiled=True
        ).astype(jnp.float32),
    )
    owned = (
        lax.all_to_all(
            row_sums[0].astype(jnp.bfloat16), "head", split_axis=0, concat_axis=1, tiled=True
        ).astype(jnp.float32),
        lax.all_to_all(
            row_sums[1].astype(jnp.bfloat16), "head", split_axis=0, concat_axis=1, tiled=True
        ).astype(jnp.float32),
        lax.all_to_all(
            row_sums[2].astype(jnp.bfloat16), "head", split_axis=0, concat_axis=1, tiled=True
        ).astype(jnp.float32),
        lax.all_to_all(
            row_sums[3].astype(jnp.bfloat16), "head", split_axis=0, concat_axis=1, tiled=True
        ).astype(jnp.float32),
        lax.all_to_all(
            row_sums[4].astype(jnp.bfloat16), "head", split_axis=0, concat_axis=1, tiled=True
        ).astype(jnp.float32),
    )
    gain_sums = (
        lax.psum_scatter(grad_attn, ("head", "blk"), scatter_dimension=0, tiled=True),
        lax.psum_scatter(grad_qgain, ("head", "blk"), scatter_dimension=0, tiled=True),
        lax.psum_scatter(grad_kgain, ("head", "blk"), scatter_dimension=0, tiled=True),
        lax.psum_scatter(grad_ffn, ("head", "blk"), scatter_dimension=0, tiled=True),
    )
    return (
        output,
        input_grad,
        gain_sums[0],
        owned[0],
        owned[1],
        owned[2],
        gain_sums[1],
        gain_sums[2],
        row_sums[5],
        gain_sums[3],
        owned[3],
        owned[4],
        row_sums[6],
    )


def solution(mesh):
    placed = (
        P(("blk", "head"), None),
        P(("blk", "head"), None),
        P(),
        P(("head", "blk")),
        P(("head", "blk"), None),
        P(("head", "blk"), None),
        P(("head", "blk"), None),
        P(("head", "blk")),
        P(("head", "blk")),
        P(("head", "blk"), None),
        P(("head", "blk")),
        P(("head", "blk"), None),
        P(("head", "blk"), None),
        P(("head", "blk"), None),
    )
    return jax.shard_map(
        local,
        mesh=mesh,
        in_specs=placed,
        out_specs=(
            P(("blk", "head"), None),
            P(("blk", "head"), None),
            P(("head", "blk")),
            P(("head", "blk"), None),
            P(("head", "blk"), None),
            P(("head", "blk"), None),
            P(("head", "blk")),
            P(("head", "blk")),
            P(("head", "blk"), None),
            P(("head", "blk")),
            P(("head", "blk"), None),
            P(("head", "blk"), None),
            P(("head", "blk"), None),
        ),
        check_vma=False,
    )
```

profile of v0, /device:TPU:0, one launch (start us, length us, event | category | flops | bytes accessed | tf_op | source)
XLA Modules:
  0.0 1165.0 jit_solution(2880763753025886302)
XLA Ops:
  11.6 68.4 %all-reduce.14 = (bf16[1024]{0:T(1024)(128)(2,1)S(1)}, bf16[128]{0:T(256)(128)(2,1)S(1)}, bf16[128]{0:T(256)(128)(2,1)S(1)}, bf16[1024]{0:T(1024)(128)(2,1)}) all-reduce(bf16[1024]{0:T(1024)(128)(2,1)S(1)} %dynamic-update-slice, bf16[128]{0:T(256)(128)(2,1)S(1)} %dynamic-update-slice.1, ...), channel_id=1, replica_groups=mesh['head'=8,'blk'=16] {'head','blk'}, use_global_device_ids=true, to_apply=%add.5 | all-reduce | flops 2304 | bytes 9216
  82.6 3.9 all-to-all-start
  86.7 9.1 fusion.107
  96.6 18.2 %all_gather.52 = bf16[256,1024]{1,0:T(8,128)(2,1)S(1)} all-gather(bf16[16,1024]{1,0:T(8,128)(2,1)S(1)} %copy-done.47), channel_id=1, replica_groups=mesh['head'=8,'blk'=16] {'blk'}, dimensions={0}, use_global_device_ids=true | all-gather | bytes 557056 | tf_op jit(solution)/shard_map/all_gather | solution.py:162
  114.9 7.8 all-to-all-start.1
  122.7 17.2 %all_gather.47 = bf16[1024,128]{1,0:T(8,128)(2,1)S(1)} all-gather(bf16[64,128]{1,0:T(8,128)(2,1)S(1)} %bitcast.371), channel_id=1, replica_groups=mesh['head'=8,'blk'=16] {'blk'}, dimensions={0}, use_global_device_ids=true | all-gather | bytes 278528 | tf_op jit(solution)/shard_map/all_gather | solution.py:159
  139.9 7.2 all-to-all-start.2
  147.1 18.1 %all_gather.48 = bf16[1024,128]{1,0:T(8,128)(2,1)S(1)} all-gather(bf16[64,128]{1,0:T(8,128)(2,1)S(1)} %bitcast.372), channel_id=1, replica_groups=mesh['head'=8,'blk'=16] {'blk'}, dimensions={0}, use_global_device_ids=true | all-gather | bytes 278528 | tf_op jit(solution)/shard_map/all_gather | solution.py:158
  165.3 17.9 %all_gather.50 = bf16[1024,256]{1,0:T(8,128)(2,1)S(1)} all-gather(bf16[64,256]{1,0:T(8,128)(2,1)S(1)} %bitcast.368), channel_id=1, replica_groups=mesh['head'=8,'blk'=16] {'blk'}, dimensions={0}, use_global_device_ids=true | all-gather | bytes 557056 | tf_op jit(solution)/shard_map/all_gather | solution.py:157
  183.1 3.3 fusion.69
  193.2 3.6 collective-permute-start.1
  203.5 4.0 fusion.72
  212.7 24.0 %while.34 = (s32[]{:T(128)}, bf16[2,512,1,2,128]{4,3,1,0,2:T(2,128)(2,1)S(1)}, f32[2,1,2,512,1]{3,2,4,1,0:T(2,128)S(1)}, s32[2]{0:T(128)S(1)}, bf16[2048,1,128]{...) while((s32[]{:T(128)}, ...), condition=%wide.region_6.7_spmd, body=%wide.region_3.6_spmd.sunk | while | flops 829029888 | bytes 24441124 | solution.py:219
  238.8 75.5 %reduce-scatter.12.cloned.1.call-done = bf16[128,1024]{1,0:T(8,128)(2,1)} async-done(((bf16[1024,1024]{1,0:T(8,128)(2,1)}), bf16[128,1024]{1,0:T(8,128)(2,1)}) %reduce-scatter.12.cloned.1.call-update) | async-done | bytes 262160 | tf_op jit(solution)/shard_map/reduce_scatter | solution.py:65
  318.1 4.0 all-to-all-start.4
  322.0 24.0 %all_gather.57 = bf16[384,1024]{1,0:T(8,128)(2,1)} all-gather(bf16[24,1024]{1,0:T(8,128)(2,1)S(1)} %copy-done.44), channel_id=1, replica_groups=mesh['head'=8,'blk'=16] {'blk'}, dimensions={0}, use_global_device_ids=true | all-gather | bytes 835584 | tf_op jit(solution)/shard_map/all_gather | solution.py:163
  346.1 7.9 all-to-all-start.3
  354.0 21.1 %all_gather.56 = bf16[1024,384]{1,0:T(8,128)(2,1)S(1)} all-gather(bf16[64,384]{1,0:T(8,128)(2,1)S(1)} %bitcast.366), channel_id=1, replica_groups=mesh['head'=8,'blk'=16] {'blk'}, dimensions={0}, use_global_device_ids=true | all-gather | bytes 835584 | tf_op jit(solution)/shard_map/all_gather | solution.py:161
  375.1 19.2 %all_gather.55 = bf16[1024,384]{1,0:T(8,128)(2,1)S(1)} all-gather(bf16[64,384]{1,0:T(8,128)(2,1)S(1)} %bitcast.367), channel_id=1, replica_groups=mesh['head'=8,'blk'=16] {'blk'}, dimensions={0}, use_global_device_ids=true | all-gather | bytes 835584 | tf_op jit(solution)/shard_map/all_gather | solution.py:160
  394.3 4.2 fusion.122
  401.0 27.2 %all-gather.9.cloned.1.call-done = bf16[1024,1024]{1,0:T(8,128)(2,1)} async-done(((bf16[128,1024]{1,0:T(8,128)(2,1)}), bf16[1024,1024]{1,0:T(8,128)(2,1)}) %all-gather.9.cloned.1.call-update) | async-done | bytes 2097168 | tf_op jit(solution)/shard_map/all_gather | solution.py:61
  428.2 5.5 multiply_convert_fusion
  439.1 72.8 %reduce-scatter.16.cloned.1.call-done = bf16[128,1024]{1,0:T(8,128)(2,1)} async-done(((bf16[1024,1024]{1,0:T(8,128)(2,1)}), bf16[128,1024]{1,0:T(8,128)(2,1)}) %reduce-scatter.16.cloned.1.call-update) | async-done | bytes 262160 | tf_op jit(solution)/shard_map/reduce_scatter | solution.py:65
  515.9 3.8 convolution_convert_fusion.3
  519.7 3.8 convolution_convert_fusion.4
  523.8 44.8 %all-gather.11.cloned.1.call-done = bf16[1024,1024]{1,0:T(8,128)(2,1)} async-done(((bf16[128,1024]{1,0:T(8,128)(2,1)}), bf16[1024,1024]{1,0:T(8,128)(2,1)}) %all-gather.11.cloned.1.call-update) | async-done | bytes 2097168 | tf_op jit(solution)/shard_map/all_gather | solution.py:61
  572.1 35.9 %while.35 = (s32[]{:T(128)}, f32[2048,1,128]{0,2,1:T(8,128)S(1)}, f32[2048,1,128]{0,2,1:T(8,128)S(1)}, bf16[2,512,1,2,128]{4,1,0,3,2:T(8,128)(2,1)}, s32[2]{0:T(...) while((s32[]{:T(128)}, f32[2048,1,128]{0,2,1:T(8,128)S(1)}, ...), condition=%wide.region_14.15_spmd, body=%wide.region_12.14_spmd.sunk | while | flops 2032991744 | bytes 56017352 | solution.py:307
  579.9 3.5 fusion.199
  597.9 3.5 fusion.199
  614.7 3.8 convolution_convert_fusion.2
  637.4 3.2 convolution_convert_fusion.6
  640.7 3.2 convolution_convert_fusion.5
  649.6 3.8 convolution_convert_fusion
  653.4 3.4 all-to-all-start.9
  656.8 35.4 %reduce-scatter.28.cloned.1.call-done = bf16[64,384]{1,0:T(8,128)(2,1)} async-done(((bf16[1024,384]{1,0:T(8,128)(2,1)}), bf16[64,384]{1,0:T(8,128)(2,1)}) %reduce-scatter.28.cloned.1.call-update) | async-done | bytes 49168 | tf_op jit(solution)/shard_map/reduce_scatter | solution.py:355
  692.2 14.2 %all_to_all.160 = bf16[8,8,384]{2,1,0:T(8,128)(2,1)S(1)} all-to-all(bf16[8,8,384]{2,1,0:T(8,128)(2,1)} %bitcast.375), channel_id=1, replica_groups=mesh['head'=8,'blk'=16] {'head'}, dimensions={0} | all-to-all | bytes 98304 | tf_op jit(solution)/shard_map/all_to_all | solution.py:378
  706.4 46.8 %reduce-scatter.24.cloned.1.call-done = bf16[64,128]{1,0:T(8,128)(2,1)} async-done(((bf16[1024,128]{1,0:T(8,128)(2,1)}), bf16[64,128]{1,0:T(8,128)(2,1)}) %reduce-scatter.24.cloned.1.call-update) | async-done | bytes 16400 | tf_op jit(solution)/shard_map/reduce_scatter | solution.py:352
  753.2 6.5 all-to-all-start.7
  759.7 55.4 %reduce-scatter.32.cloned.1.call-done = bf16[24,1024]{1,0:T(8,128)(2,1)} async-done(((bf16[384,1024]{1,0:T(8,128)(2,1)}), bf16[24,1024]{1,0:T(8,128)(2,1)}) %reduce-scatter.32.cloned.1.call-update) | async-done | bytes 49168 | tf_op jit(solution)/shard_map/reduce_scatter | solution.py:364
  817.9 59.0 %reduce-scatter.22.cloned.1.call-done = bf16[64,128]{1,0:T(8,128)(2,1)} async-done(((bf16[1024,128]{1,0:T(8,128)(2,1)}), bf16[64,128]{1,0:T(8,128)(2,1)}) %reduce-scatter.22.cloned.1.call-update) | async-done | bytes 16400 | tf_op jit(solution)/shard_map/reduce_scatter | solution.py:349
  876.9 6.6 all-to-all-start.6
  884.1 7.1 all-to-all-done.6
  891.2 47.4 %reduce-scatter.20.cloned.1.call-done = bf16[64,256]{1,0:T(8,128)(2,1)} async-done(((bf16[1024,256]{1,0:T(8,128)(2,1)}), bf16[64,256]{1,0:T(8,128)(2,1)}) %reduce-scatter.20.cloned.1.call-update) | async-done | bytes 32784 | tf_op jit(solution)/shard_map/reduce_scatter | solution.py:346
  938.6 6.4 all-to-all-start.5
  945.7 54.5 %reduce-scatter.26.cloned.1.call-done = bf16[16,1024]{1,0:T(8,128)(2,1)} async-done(((bf16[256,1024]{1,0:T(8,128)(2,1)}), bf16[16,1024]{1,0:T(8,128)(2,1)}) %reduce-scatter.26.cloned.1.call-update) | async-done | bytes 32784 | tf_op jit(solution)/shard_map/reduce_scatter | solution.py:361
  1002.2 75.3 %reduce-scatter.18.cloned.1.call-done = bf16[128,1024]{1,0:T(8,128)(2,1)} async-done(((bf16[1024,1024]{1,0:T(8,128)(2,1)}), bf16[128,1024]{1,0:T(8,128)(2,1)}) %reduce-scatter.18.cloned.1.call-update) | async-done | bytes 262160 | tf_op jit(solution)/shard_map/reduce_scatter | solution.py:65
  1078.8 68.3 %all-reduce.13 = (f32[1024]{0:T(1024)S(1)}, f32[128]{0:T(128)S(1)}, f32[128]{0:T(128)S(1)}, f32[1024]{0:T(1024)S(1)}) all-reduce(f32[1024]{0:T(1024)S(1)} %get-tuple-element.547, f32[128]{0:T(128)S(1)} %get-tuple-element.543, f32[128]{0:T(128)S(1)} %get-tuple-element.541, ...), channel_id=6, replica_groups=mesh['head'=8,'blk'=16] {'head','blk'}, use_global_device_ids=true, to_apply=%region_20.21.clone | all-reduce | flops 2304 | bytes 18432
  1149.5 6.3 reduce-scatter.14.cloned.1.call-done
  (331 shorter events, 131.8 us)
Async XLA Ops:
  7.2 89.4 %copy-start.47 = (bf16[16,1024]{1,0:T(8,128)(2,1)S(1)}, bf16[16,1024]{1,0:T(8,128)(2,1)}, u32[]{:S(2)}) copy-start(bf16[16,1024]{1,0:T(8,128)(2,1)} %param.27) | copy-start | bytes 98308
  7.2 107.6 %copy-start.39 = (s32[16384]{0:T(1024)S(1)}, s32[16384]{0:T(1024)}, u32[]{:S(2)}) copy-start(s32[16384]{0:T(1024)} %param.20) | copy-start | bytes 196612
  7.2 175.9 %all-gather.5.cloned.1.call-start = ((), (), s32[]{:S(2)}) async-start(), calls=%async_computation.21 | async-start | bytes 2359296 | tf_op jit(solution)/shard_map/all_gather | solution.py:61
  9.7 113.1 %copy-start.57 = (f32[128]{0:T(128)}, f32[128]{0:T(128)S(1)}, u32[]{:S(2)}) copy-start(f32[128]{0:T(128)S(1)} %add_rsqrt_fusion.1) | copy-start | bytes 1540
  82.6 32.3 %all-to-all-start = ((bf16[8,8,128]{2,0,1:T(8,128)(2,1)}), bf16[8,8,128]{2,0,1:T(8,128)(2,1)S(1)}, u32[]{:S(2)}, u32[]{:S(2)}) async-start(bf16[8,8,128]{2,0,1:T(8,128)(2,1)} %bitcast.377), calls=%async_computation | async-start | bytes 32768 | tf_op jit(solution)/shard_map/all_to_all | solution.py:152
  114.8 121.8 %copy-start.23 = (bf16[256,1024]{1,0:T(8,128)(2,1)}, bf16[256,1024]{1,0:T(8,128)(2,1)S(1)}, u32[]{:S(2)}) copy-start(bf16[256,1024]{1,0:T(8,128)(2,1)S(1)} %all_gather.52) | copy-start | bytes 1572868
  114.9 88.6 %copy-start.55 = (f32[128]{0:T(128)}, f32[128]{0:T(128)S(1)}, u32[]{:S(2)}) copy-start(f32[128]{0:T(128)S(1)} %convert_element_type.292) | copy-start | bytes 1540
  114.9 25.0 %all-to-all-start.1 = ((bf16[8,8,128]{2,0,1:T(8,128)(2,1)}), bf16[8,8,128]{2,0,1:T(8,128)(2,1)S(1)}, u32[]{:S(2)}, u32[]{:S(2)}) async-start(bf16[8,8,128]{2,0,1:T(8,128)(2,1)} %bitcast.45), calls=%async_computation.1 | async-start | bytes 32768 | tf_op jit(solution)/shard_map/all_to_all | solution.py:151
  139.9 25.4 %all-to-all-start.2 = ((bf16[8,8,256]{2,0,1:T(8,128)(2,1)}), bf16[8,8,256]{2,0,1:T(8,128)(2,1)S(1)}, u32[]{:S(2)}, u32[]{:S(2)}) async-start(bf16[8,8,256]{2,0,1:T(8,128)(2,1)} %bitcast.52), calls=%async_computation.2 | async-start | bytes 65536 | tf_op jit(solution)/shard_map/all_to_all | solution.py:150
  147.1 167.2 %reduce-scatter.12.cloned.1.call-start = ((), (), s32[]{:S(2)}) async-start(), calls=%async_computation.22 | async-start | bytes 2359296 | tf_op jit(solution)/shard_map/reduce_scatter | solution.py:65
  186.4 24.4 %collective-permute-start = (bf16[1024,1,128]{2,0,1:T(8,128)(2,1)}, bf16[1024,1,128]{2,0,1:T(8,128)(2,1)}, u32[]{:S(2)}, u32[]{:S(2)}) collective-permute-start(bf16[1024,1,128]{2,0,1:T(8,128)(2,1)} %fusion.69), channel_id=1, source_target_pairs={{0,1},{1,2},{2,3},{3,4},{4,5},{5,6},{6,7},{7,8},{8,9},{9,10},{10,1... | collective-permute-start | bytes 786440 | tf_op jit(solution)/shard_map/ppermute | solution.py:23
  193.2 16.4 %collective-permute-start.1 = (bf16[1024,1,128]{0,2,1:T(8,128)(2,1)S(1)}, bf16[1024,1,128]{0,2,1:T(8,128)(2,1)}, u32[]{:S(2)}, u32[]{:S(2)}) collective-permute-start(bf16[1024,1,128]{0,2,1:T(8,128)(2,1)S(1)} %get-tuple-element.619), channel_id=1, source_target_pairs={{0,1},{1,2},{2,3},{3,4},{4,5},{5,6},{6,7},{7,8},{8,9},{9,10},{10,1... | collective-permute-start | bytes 786440 | tf_op jit(solution)/shard_map/ppermute | solution.py:23
  236.6 79.9 %copy-start.26 = (bf16[2,512,1,2,128]{4,3,1,0,2:T(2,128)(2,1)}, bf16[2,512,1,2,128]{4,3,1,0,2:T(2,128)(2,1)S(1)}, u32[]{:S(2)}) copy-start(bf16[2,512,1,2,128]{4,3,1,0,2:T(2,128)(2,1)S(1)} %get-tuple-element.431) | copy-start | bytes 1572868
  236.7 77.6 %copy-start.7 = (bf16[128,1024]{1,0:T(8,128)(2,1)S(1)}, bf16[128,1024]{1,0:T(8,128)(2,1)}, u32[]{:S(2)}) copy-start(bf16[128,1024]{1,0:T(8,128)(2,1)} %param.18) | copy-start | bytes 786436
  238.8 83.3 %copy-start.44 = (bf16[24,1024]{1,0:T(8,128)(2,1)S(1)}, bf16[24,1024]{1,0:T(8,128)(2,1)}, u32[]{:S(2)}) copy-start(bf16[24,1024]{1,0:T(8,128)(2,1)} %param.31) | copy-start | bytes 147460
  238.8 155.5 %all-gather.7.cloned.1.call-start = ((), (), s32[]{:S(2)}) async-start(), calls=%async_computation.23 | async-start | bytes 2359296 | tf_op jit(solution)/shard_map/all_gather | solution.py:61
  315.4 198.4 %copy-start.51 = (f32[128]{0:T(128)}, f32[128]{0:T(128)S(1)}, u32[]{:S(2)}) copy-start(f32[128]{0:T(128)S(1)} %add_rsqrt_fusion) | copy-start | bytes 1540
  317.5 110.7 %all-gather.9.cloned.1.call-start = ((), (), s32[]{:S(2)}) async-start(), calls=%async_computation.25 | async-start | bytes 2359296 | tf_op jit(solution)/shard_map/all_gather | solution.py:61
  318.1 28.0 %all-to-all-start.4 = ((bf16[8,8,384]{2,0,1:T(8,128)(2,1)}), bf16[8,8,384]{2,0,1:T(8,128)(2,1)S(1)}, u32[]{:S(2)}, u32[]{:S(2)}) async-start(bf16[8,8,384]{2,0,1:T(8,128)(2,1)} %bitcast.62), calls=%async_computation.5 | async-start | bytes 98304 | tf_op jit(solution)/shard_map/all_to_all | solution.py:154
  346.1 29.0 %all-to-all-start.3 = ((bf16[8,8,384]{2,0,1:T(8,128)(2,1)}), bf16[8,8,384]{2,0,1:T(8,128)(2,1)S(1)}, u32[]{:S(2)}, u32[]{:S(2)}) async-start(bf16[8,8,384]{2,0,1:T(8,128)(2,1)} %bitcast.59), calls=%async_computation.4 | async-start | bytes 98304 | tf_op jit(solution)/shard_map/all_to_all | solution.py:153
  353.9 158.0 %reduce-scatter.16.cloned.1.call-start = ((), (), s32[]{:S(2)}) async-start(), calls=%async_computation.26 | async-start | bytes 2359296 | tf_op jit(solution)/shard_map/reduce_scatter | solution.py:65
  436.5 75.5 %copy-start.9 = (bf16[128,1024]{1,0:T(8,128)(2,1)S(1)}, bf16[128,1024]{1,0:T(8,128)(2,1)}, u32[]{:S(2)}) copy-start(bf16[128,1024]{1,0:T(8,128)(2,1)} %reduce-scatter.12.cloned.1.call-done) | copy-start | bytes 786436
  436.5 77.4 %copy-start.16 = (bf16[128,1024]{1,0:T(8,128)(2,1)S(1)}, bf16[128,1024]{1,0:T(8,128)(2,1)}, u32[]{:S(2)}) copy-start(bf16[128,1024]{1,0:T(8,128)(2,1)} %param.19) | copy-start | bytes 786436
  439.1 76.8 %copy-start.36 = (bf16[1024,384]{1,0:T(8,128)(2,1)S(1)}, bf16[1024,384]{1,0:T(8,128)(2,1)}, u32[]{:S(2)}) copy-start(bf16[1024,384]{1,0:T(8,128)(2,1)} %copy-done.35) | copy-start | bytes 2359300
  439.1 129.6 %all-gather.11.cloned.1.call-start = ((), (), s32[]{:S(2)}) async-start(), calls=%async_computation.27 | async-start | bytes 2359296 | tf_op jit(solution)/shard_map/all_gather | solution.py:61
  515.8 137.6 %reduce-scatter.30.cloned.1.call-start = ((), (), s32[]{:S(2)}) async-start(), calls=%async_computation.34 | async-start | bytes 835584 | tf_op jit(solution)/shard_map/reduce_scatter | solution.py:358
  519.7 172.5 %reduce-scatter.28.cloned.1.call-start = ((), (), s32[]{:S(2)}) async-start(), calls=%async_computation.33 | async-start | bytes 835584 | tf_op jit(solution)/shard_map/reduce_scatter | solution.py:355
  523.6 229.6 %reduce-scatter.24.cloned.1.call-start = ((), (), s32[]{:S(2)}) async-start(), calls=%async_computation.31 | async-start | bytes 278528 | tf_op jit(solution)/shard_map/reduce_scatter | solution.py:352
  608.1 3.4 collective-permute-start.3
  614.6 200.5 %reduce-scatter.32.cloned.1.call-start = ((), (), s32[]{:S(2)}) async-start(), calls=%async_computation.35 | async-start | bytes 835584 | tf_op jit(solution)/shard_map/reduce_scatter | solution.py:364
  618.5 258.4 %reduce-scatter.22.cloned.1.call-start = ((), (), s32[]{:S(2)}) async-start(), calls=%async_computation.30 | async-start | bytes 278528 | tf_op jit(solution)/shard_map/reduce_scatter | solution.py:349
  619.3 8.2 collective-permute-start.2
  635.0 303.6 %reduce-scatter.20.cloned.1.call-start = ((), (), s32[]{:S(2)}) async-start(), calls=%async_computation.29 | async-start | bytes 557056 | tf_op jit(solution)/shard_map/reduce_scatter | solution.py:346
  640.6 359.6 %reduce-scatter.26.cloned.1.call-start = ((), (), s32[]{:S(2)}) async-start(), calls=%async_computation.32 | async-start | bytes 557056 | tf_op jit(solution)/shard_map/reduce_scatter | solution.py:361
  643.9 433.6 %reduce-scatter.18.cloned.1.call-start = ((), (), s32[]{:S(2)}) async-start(), calls=%async_computation.28 | async-start | bytes 2359296 | tf_op jit(solution)/shard_map/reduce_scatter | solution.py:65
  649.5 428.1 %copy-start.43 = (f32[1024]{0:T(1024)S(1)}, f32[1024]{0:T(1024)}, u32[]{:S(2)}) copy-start(f32[1024]{0:T(1024)} %copy-done.42) | copy-start | bytes 12292
  649.5 428.1 %copy-start.58 = (f32[128]{0:T(128)S(1)}, f32[128]{0:T(128)}, u32[]{:S(2)}) copy-start(f32[128]{0:T(128)} %copy-done.57) | copy-start | bytes 1540
  649.5 429.3 %copy-start.50 = (f32[1024]{0:T(1024)S(1)}, f32[1024]{0:T(1024)}, u32[]{:S(2)}) copy-start(f32[1024]{0:T(1024)} %get-tuple-element.545) | copy-start | bytes 12292
  649.5 506.3 %copy-start.10 = (bf16[128,1024]{1,0:T(8,128)(2,1)S(1)}, bf16[128,1024]{1,0:T(8,128)(2,1)}, u32[]{:S(2)}) copy-start(bf16[128,1024]{1,0:T(8,128)(2,1)} %reduce-scatter.12.cloned.1.call-done) | copy-start | bytes 786436
  649.5 506.3 %copy-start.17 = (bf16[128,1024]{1,0:T(8,128)(2,1)S(1)}, bf16[128,1024]{1,0:T(8,128)(2,1)}, u32[]{:S(2)}) copy-start(bf16[128,1024]{1,0:T(8,128)(2,1)} %param.19) | copy-start | bytes 786436
  649.5 506.3 %copy-start.18 = (bf16[128,1024]{1,0:T(8,128)(2,1)S(1)}, bf16[128,1024]{1,0:T(8,128)(2,1)}, u32[]{:S(2)}) copy-start(bf16[128,1024]{1,0:T(8,128)(2,1)} %reduce-scatter.16.cloned.1.call-done) | copy-start | bytes 786436
  649.5 506.3 %copy-start.52 = (f32[128]{0:T(128)S(1)}, f32[128]{0:T(128)}, u32[]{:S(2)}) copy-start(f32[128]{0:T(128)} %copy-done.51) | copy-start | bytes 1540
  649.5 506.3 %copy-start.60 = (f32[128]{0:T(128)S(1)}, f32[128]{0:T(128)}, u32[]{:S(2)}) copy-start(f32[128]{0:T(128)} %copy-done.59) | copy-start | bytes 1540
  649.5 506.2 %reduce-scatter.14.cloned.1.call-start = ((), (), s32[]{:S(2)}) async-start(), calls=%async_computation.24 | async-start | bytes 2359296 | tf_op jit(solution)/shard_map/reduce_scatter | solution.py:65
  653.4 38.7 %all-to-all-start.9 = ((bf16[8,8,384]{2,1,0:T(8,128)(2,1)}), bf16[8,8,384]{2,1,0:T(8,128)(2,1)S(1)}, u32[]{:S(2)}, u32[]{:S(2)}) async-start(bf16[8,8,384]{2,1,0:T(8,128)(2,1)} %bitcast.374), calls=%async_computation.19 | async-start | bytes 98304 | tf_op jit(solution)/shard_map/all_to_all | solution.py:381
  753.2 123.7 %all-to-all-start.7 = ((bf16[8,8,128]{2,1,0:T(8,128)(2,1)}), bf16[8,8,128]{2,1,0:T(8,128)(2,1)S(1)}, u32[]{:S(2)}, u32[]{:S(2)}) async-start(bf16[8,8,128]{2,1,0:T(8,128)(2,1)} %bitcast.378), calls=%async_computation.14 | async-start | bytes 32768 | tf_op jit(solution)/shard_map/all_to_all | solution.py:375
  876.9 14.3 %all-to-all-start.6 = ((bf16[8,8,128]{2,1,0:T(8,128)(2,1)}), bf16[8,8,128]{2,1,0:T(8,128)(2,1)S(1)}, u32[]{:S(2)}, u32[]{:S(2)}) async-start(bf16[8,8,128]{2,1,0:T(8,128)(2,1)} %bitcast.379), calls=%async_computation.12 | async-start | bytes 32768 | tf_op jit(solution)/shard_map/all_to_all | solution.py:372
  938.6 62.9 %all-to-all-start.5 = ((bf16[8,8,256]{2,1,0:T(8,128)(2,1)}), bf16[8,8,256]{2,1,0:T(8,128)(2,1)S(1)}, u32[]{:S(2)}, u32[]{:S(2)}) async-start(bf16[8,8,256]{2,1,0:T(8,128)(2,1)} %bitcast.376), calls=%async_computation.10 | async-start | bytes 65536 | tf_op jit(solution)/shard_map/all_to_all | solution.py:369
  (48 other events, 368.2 us)
Sparse Core Ops, SparseCore 0:
  82.7 50.5 all-gather.4
  238.9 75.3 reduce-scatter.11
  317.6 54.7 all-gather.6
  374.6 53.5 all-gather.8
  439.2 72.7 reduce-scatter.15
  515.9 52.6 all-gather.10
  571.0 59.0 reduce-scatter.29
  632.6 59.5 reduce-scatter.27
  694.5 58.5 reduce-scatter.23
  755.5 59.5 reduce-scatter.31
  818.1 58.7 reduce-scatter.21
  879.2 59.3 reduce-scatter.19
  941.0 59.1 reduce-scatter.25
  1004.2 73.3 reduce-scatter.17
  1081.6 74.1 reduce-scatter.13
where the time goes:
time: 1170 us
  waiting for transfers between devices  612 us (52%)
  blocking collectives  287 us (25%)
  matrix products  81.7 us (7%)
  starting transfers between devices  63.9 us (5%)
  other arithmetic  61 us (5%)
  local copies, waits for them, and re-layouts  32.9 us (3%)
  between operations  16.7 us (1%)
    reduce_scatter x4, waiting for transfers between devices, rows_out(): lax.psum_scatter(value_rows.astype(jnp.bfloat16), 'head', scatter_dimensi...  230 us
    unnamed x2, blocking collectives  137 us
    all_gather x4, waiting for transfers between devices, rows_in(): return lax.all_gather(value_rows, 'head', axis=0, tiled=True)  72 us
    reduce_scatter x1, waiting for transfers between devices, local(): lax.psum_scatter(grad_wk.astype(jnp.bfloat16), 'blk', scatter_dimension=0...  59 us
    reduce_scatter x1, waiting for transfers between devices, local(): lax.psum_scatter(grad_down.astype(jnp.bfloat16), 'blk', scatter_dimension...  55.4 us
    reduce_scatter x1, waiting for transfers between devices, local(): lax.psum_scatter(grad_wout.astype(jnp.bfloat16), 'blk', scatter_dimension...  54.5 us
    reduce_scatter x1, waiting for transfers between devices, local(): lax.psum_scatter(grad_wq.astype(jnp.bfloat16), 'blk', scatter_dimension=0...  47.4 us
    reduce_scatter x1, waiting for transfers between devices, local(): lax.psum_scatter(grad_wv.astype(jnp.bfloat16), 'blk', scatter_dimension=0...  46.8 us
  transfers between devices with their start and end apart: 28, of which 15 were waited for; matrix products, arithmetic and copies ran while one was open for 10% of the time, Pallas kernels for 0%

commit v1 on v0

v1 whole, which is shorter than its diff:
```python
import functools

import jax
import jax.numpy as jnp
import numpy as np
from jax import lax
from jax.experimental import pallas as pl
from jax.experimental.pallas import tpu as pltpu
from jax.sharding import PartitionSpec as P

HEAD_SIZE = 128
SPAN = 1024
CHUNK = 512
EPS = 1e-06
ROPE_BASE = 1000000.0
MASKED = -1e30
MESH = pl.DeviceIdType.MESH
BF = jnp.bfloat16
F32 = jnp.float32
VMEM = pl.BlockSpec(memory_space=pltpu.VMEM)
HBM = pl.BlockSpec(memory_space=pl.ANY)
DMA = pltpu.SemaphoreType.DMA
VMEM_LIMIT = 58 * 2**20


def coords():
    h = lax.axis_index("head")
    b = lax.axis_index("blk")
    x = 2 * lax.div(h, 4) + lax.div(b, 8)
    return x, lax.rem(h, 4), lax.rem(lax.div(b, 2), 4), lax.rem(b, 2)


def device(x, y, z, c):
    return (lax.div(x, 2) * 4 + y, lax.rem(x, 2) * 8 + z * 2 + c)


def wrap4(v):
    return lax.rem(v + 8, 4)


def send(src, dst, send_sem, recv_sem, to):
    copy = pltpu.make_async_remote_copy(
        src_ref=src, dst_ref=dst, send_sem=send_sem, recv_sem=recv_sem, device_id=to, device_id_type=MESH
    )
    copy.start()
    return copy


def arrived(dst, sem, anyone):
    pltpu.make_async_remote_copy(
        src_ref=dst, dst_ref=dst, send_sem=sem, recv_sem=sem, device_id=anyone, device_id_type=MESH
    ).wait_recv()


def meet(peers):
    barrier = pltpu.get_barrier_semaphore()
    for peer in peers:
        pl.semaphore_signal(barrier, inc=1, device_id=peer, device_id_type=MESH)
    pl.semaphore_wait(barrier, len(peers))


def params(collective_id):
    return pltpu.CompilerParams(
        collective_id=collective_id, has_side_effects=True, vmem_limit_bytes=VMEM_LIMIT
    )


def gather_kernel(
    tok, cot, wq, wk, wv, wg, wu, gains, wo, wd,
    xs, cs, wa, wb, wof, wdf,
    sa, sb, ysend, yrecv, lsem, p1s, p1r, p2s, p2r, cos, cor,
):
    x, y, z, c = coords()
    for r in range(4):
        for g in range(2):
            h = g * 4 + r
            sa[r, :, g * 256 : g * 256 + 256] = wq[:, h * 256 : h * 256 + 256]
            sa[r, :, 512 + g * 128 : 640 + g * 128] = wk[:, h * 128 : h * 128 + 128]
            sa[r, :, 768 + g * 128 : 896 + g * 128] = wv[:, h * 128 : h * 128 + 128]
            sb[r, :, g * 384 : g * 384 + 384] = wg[:, h * 384 : h * 384 + 384]
            sb[r, :, 768 + g * 384 : 1152 + g * 384] = wu[:, h * 384 : h * 384 + 384]
        sa[r, :, 1024:1152] = gains[...]

    d = 1 - c

    def along(j, k):
        return wrap4(x + j * d + k * c), wrap4(z + j * c + k * d)

    def to(j, k):
        px, pz = along(j, k)
        return device(px, y, pz, c)

    across = device(x, y, z, 1 - c)
    ring = [device(x, wrap4(y + k), z, c) for k in range(1, 4)]
    meet(ring + [to(k, 0) for k in range(1, 4)] + [to(0, k) for k in range(1, 4)] + [across])

    def slot(ref, wide, px, pz, core):
        b = lax.rem(px, 2) * 8 + pz * 2 + core
        if wide:
            return ref.at[lax.div(px, 2), :, b]
        return ref.at[lax.div(px, 2), b]

    def piece(n, j, k):
        px, pz = along(-j, -k)
        ref, wide = arrays[n]
        return slot(ref, wide, px, pz, c)

    def piece_across(n, j, k):
        px, pz = wrap4(x - j * c - k * d), wrap4(z - j * d - k * c)
        ref, wide = arrays[n]
        return slot(ref, wide, px, pz, 1 - c)

    arrays = [(wa, True), (wof, False), (wb, True), (wdf, False)]
    sends = []
    locals_ = []
    b = lax.rem(x, 2) * 8 + z * 2 + c
    xh = lax.div(x, 2)

    def keep(src, dst, n):
        copy = pltpu.make_async_copy(src, dst, lsem.at[n])
        copy.start()
        return copy

    def ring_out(n, src_of, dst):
        for k in range(1, 4):
            sends.append(send(src_of(wrap4(y + k)), dst(y), ysend.at[n, k - 1], yrecv.at[n, k - 1], ring[k - 1]))
        return keep(src_of(y), dst(y), n)

    def ring_in(n, dst):
        for k in range(1, 4):
            arrived(dst(wrap4(y - k)), yrecv.at[n, k - 1], ring[0])

    at_a = lambda r: wa.at[xh, r, b]
    at_b = lambda r: wb.at[xh, r, b]
    own_a = ring_out(0, lambda r: sa.at[r], at_a)
    own_x = ring_out(2, lambda r: tok, lambda r: xs.at[r])
    own_b = ring_out(1, lambda r: sb.at[r], at_b)
    own_c = ring_out(3, lambda r: cot, lambda r: cs.at[r])
    own_o = keep(wo, slot(wof, False, x, z, c), 4)
    own_d = keep(wd, slot(wdf, False, x, z, c), 5)

    def own_sends(n, src):
        for k in range(1, 4):
            sends.append(send(src, piece(n, 0, 0), p1s.at[n, k - 1], p1r.at[n, k - 1], to(k, 0)))
        for k in range(1, 4):
            sends.append(send(src, piece(n, 0, 0), p2s.at[n, 0, k - 1], p2r.at[n, 0, k - 1], to(0, k)))
        sends.append(send(src, piece(n, 0, 0), cos.at[n, 0, 0], cor.at[n, 0, 0], across))

    def pass_on(n, j):
        arrived(piece(n, j, 0), p1r.at[n, j - 1], across)
        for k in range(1, 4):
            sends.append(
                send(piece(n, j, 0), piece(n, j, 0), p2s.at[n, j, k - 1], p2r.at[n, j, k - 1], to(0, k))
            )
        sends.append(send(piece(n, j, 0), piece(n, j, 0), cos.at[n, j, 0], cor.at[n, j, 0], across))

    def pass_across(n, j, k):
        arrived(piece(n, j, k), p2r.at[n, j, k - 1], across)
        sends.append(send(piece(n, j, k), piece(n, j, k), cos.at[n, j, k], cor.at[n, j, k], across))

    own_sends(1, wo)
    ring_in(0, at_a)
    own_a.wait()
    own_sends(0, piece(0, 0, 0))
    for j in range(1, 4):
        pass_on(0, j)
        pass_on(1, j)
    own_sends(3, wd)
    ring_in(1, at_b)
    own_b.wait()
    own_sends(2, piece(2, 0, 0))
    for n in (0, 1):
        for j in range(4):
            for k in range(1, 4):
                pass_across(n, j, k)
    for j in range(1, 4):
        pass_on(2, j)
        pass_on(3, j)
    for n in (2, 3):
        for j in range(4):
            for k in range(1, 4):
                pass_across(n, j, k)
    ring_in(2, lambda r: xs.at[r])
    ring_in(3, lambda r: cs.at[r])
    for n in range(4):
        for j in range(4):
            for k in range(4):
                arrived(piece_across(n, j, k), cor.at[n, j, k], across)
    for copy in (own_x, own_c, own_o, own_d):
        copy.wait()
    for copy in sends:
        copy.wait_send()


def gather_all(tok, cot, wq, wk, wv, wg, wu, gains, wo, wd):
    sds = jax.ShapeDtypeStruct
    return pl.pallas_call(
        gather_kernel,
        out_shape=(
            sds((4, 128, 1024), BF),
            sds((4, 128, 1024), BF),
            sds((2, 4, 16, 8, 1152), BF),
            sds((2, 4, 16, 8, 1536), BF),
            sds((2, 16, 16, 1024), BF),
            sds((2, 16, 24, 1024), BF),
        ),
        in_specs=[HBM, HBM] + [VMEM] * 6 + [HBM, HBM],
        out_specs=(HBM,) * 6,
        scratch_shapes=[
            pltpu.VMEM((4, 8, 1152), BF),
            pltpu.VMEM((4, 8, 1536), BF),
            DMA((4, 3)),
            DMA((4, 3)),
            DMA((6,)),
            DMA((4, 3)),
            DMA((4, 3)),
            DMA((4, 4, 3)),
            DMA((4, 4, 3)),
            DMA((4, 4, 4)),
            DMA((4, 4, 4)),
        ],
        compiler_params=params(0),
        name="gather_all",
    )(tok, cot, wq, wk, wv, wg, wu, gains, wo, wd)


def ring_gather_kernel(src, out, ssem, rsem, lsem):
    x, y, z, c = coords()
    ring = [device(x, wrap4(y + k), z, c) for k in range(1, 4)]
    meet(ring)
    copies = [send(src, out.at[y], ssem.at[k], rsem.at[k], ring[k]) for k in range(3)]
    own = pltpu.make_async_copy(src, out.at[y], lsem)
    own.start()
    for k in range(3):
        arrived(out.at[wrap4(y - k - 1)], rsem.at[k], ring[0])
    own.wait()
    for copy in copies:
        copy.wait_send()


def ring_gather(rows, collective_id):
    return pl.pallas_call(
        ring_gather_kernel,
        out_shape=jax.ShapeDtypeStruct((4,) + rows.shape, rows.dtype),
        in_specs=[HBM],
        out_specs=HBM,
        scratch_shapes=[DMA((3,)), DMA((3,)), DMA],
        compiler_params=params(collective_id),
        name="ring_gather",
    )(rows)


def ring_sum_kernel(part, out, land, ssem, rsem):
    x, y, z, c = coords()
    ring = [device(x, wrap4(y + k), z, c) for k in range(1, 4)]
    meet(ring)
    copies = [
        send(part.at[wrap4(y + k + 1)], land.at[k], ssem.at[k], rsem.at[k], ring[k]) for k in range(3)
    ]
    for copy in copies:
        copy.wait()
    total = part[y].astype(F32)
    for k in range(3):
        total = total + land[k].astype(F32)
    out[...] = total


def ring_sum(part, collective_id):
    rows, cols = part.shape[1:]
    return pl.pallas_call(
        ring_sum_kernel,
        out_shape=jax.ShapeDtypeStruct((rows, cols), F32),
        in_specs=[VMEM],
        out_specs=VMEM,
        scratch_shapes=[pltpu.VMEM((3, rows, cols), BF), DMA((3,)), DMA((3,))],
        compiler_params=params(collective_id),
        name="ring_sum",
    )(part)


def chunk_device(step):
    h = lax.axis_index("head")
    chunk = lax.rem(2 * lax.axis_index("blk") + lax.div(h, 4) + step + 32, 32)
    return (lax.rem(chunk, 2) * 4 + lax.rem(h, 4), lax.div(chunk, 2))


def halo_kernel(kv, out, ssem, rsem, lsem):
    meet([chunk_device(s) for s in (-2, -1, 1, 2)])
    far = send(kv, out.at[0], ssem.at[0], rsem.at[0], chunk_device(2))
    near = send(kv, out.at[1], ssem.at[1], rsem.at[1], chunk_device(1))
    own = pltpu.make_async_copy(kv, out.at[2], lsem)
    own.start()
    far.wait()
    near.wait()
    own.wait()


def halo(kv, collective_id):
    return pl.pallas_call(
        halo_kernel,
        out_shape=jax.ShapeDtypeStruct((3,) + kv.shape, kv.dtype),
        in_specs=[HBM],
        out_specs=HBM,
        scratch_shapes=[DMA((2,)), DMA((2,)), DMA],
        compiler_params=params(collective_id),
        name="halo",
    )(kv)


def halo_back_kernel(dkv, out, land, ssem, rsem):
    meet([chunk_device(s) for s in (-2, -1, 1, 2)])
    far = send(dkv.at[0], land.at[0], ssem.at[0], rsem.at[0], chunk_device(-2))
    near = send(dkv.at[1], land.at[1], ssem.at[1], rsem.at[1], chunk_device(-1))
    far.wait()
    near.wait()
    out[...] = dkv[2].astype(F32) + land[0].astype(F32) + land[1].astype(F32)


def halo_back(dkv, collective_id):
    return pl.pallas_call(
        halo_back_kernel,
        out_shape=jax.ShapeDtypeStruct(dkv.shape[1:], F32),
        in_specs=[VMEM],
        out_specs=VMEM,
        scratch_shapes=[pltpu.VMEM((2,) + dkv.shape[1:], BF), DMA((2,)), DMA((2,))],
        compiler_params=params(collective_id),
        name="halo_back",
    )(dkv)


GRADS = ((8, 1152, 4), (8, 1536, 4), (16, 1024, 1), (24, 1024, 1))


def grads_kernel(ga, gb, go, gd, oq, ok, ov, og, ou, oo, od, ogain, *scratch):
    n_arr = len(GRADS)
    rc, lc, sa, lb, sb, l2, sd, ry = [scratch[i * n_arr : (i + 1) * n_arr] for i in range(8)]
    csem, crec, lsem, p2s, p2r, p1s, p1r, ys, yr = scratch[8 * n_arr :]
    x, y, z, c = coords()
    d = 1 - c

    def to(j, k):
        return device(wrap4(x + j * d + k * c), y, wrap4(z + j * c + k * d), c)

    across = device(x, y, z, 1 - c)
    ring = [device(x, wrap4(y + k), z, c) for k in range(1, 4)]
    meet(ring + [to(k, 0) for k in range(1, 4)] + [to(0, k) for k in range(1, 4)] + [across])
    p1 = x * d + z * c
    p2 = x * c + z * d
    ins = (ga, gb, go, gd)
    over, kept = [], []
    for n in range(n_arr):
        over.append(send(ins[n].at[:, 1 - c], rc[n], csem.at[n], crec.at[n], across))
        own = pltpu.make_async_copy(ins[n].at[:, c], lc[n], lsem.at[n])
        own.start()
        kept.append(own)

    first, second, third = [], [], []
    for n, (rows, cols, cut) in enumerate(GRADS):
        over[n].wait_recv()
        kept[n].wait()

        def add_cores(i, _, n=n, cut=cut):
            a2, a1, r = lax.div(i, 4 * cut), lax.rem(lax.div(i, cut), 4), lax.rem(i, cut)
            px, pz = a1 * d + a2 * c, a1 * c + a2 * d
            at = ((lax.div(px, 2) * cut + r) * 2 + lax.rem(px, 2)) * 4 + pz
            sa[n][a2, a1, r] = (rc[n][at].astype(F32) + lc[n][at].astype(F32)).astype(BF)
            return 0

        lax.fori_loop(0, 16 * cut, add_cores, 0)
        for k in range(1, 4):
            first.append(
                send(sa[n].at[wrap4(p2 + k)], lb[n].at[k - 1], p2s.at[n, k - 1], p2r.at[n, k - 1], to(0, k))
            )
    for n, (rows, cols, cut) in enumerate(GRADS):
        for k in range(3):
            first[3 * n + k].wait_recv()

        def add_second(i, _, n=n, cut=cut):
            a1, r = lax.div(i, cut), lax.rem(i, cut)
            total = sa[n][p2, a1, r].astype(F32)
            for k in range(3):
                total = total + lb[n][k, a1, r].astype(F32)
            sb[n][a1, r] = total.astype(BF)
            return 0

        lax.fori_loop(0, 4 * cut, add_second, 0)
        for k in range(1, 4):
            second.append(
                send(sb[n].at[wrap4(p1 + k)], l2[n].at[k - 1], p1s.at[n, k - 1], p1r.at[n, k - 1], to(k, 0))
            )
    for n, (rows, cols, cut) in enumerate(GRADS):
        for k in range(3):
            second[3 * n + k].wait_recv()
        for r in range(cut):
            total = sb[n][p1, r].astype(F32)
            for k in range(3):
                total = total + l2[n][k, r].astype(F32)
            if cut == 1:
                (oo if n == 2 else od)[...] = total
            else:
                sd[n][r] = total.astype(BF)
        if cut > 1:
            for k in range(1, 4):
                third.append(
                    send(sd[n].at[wrap4(y + k)], ry[n].at[y], ys.at[n, k - 1], yr.at[n, k - 1], ring[k - 1])
                )
            ry[n][y] = sd[n][y]
    for copy in third:
        copy.wait_recv()
    gain = jnp.zeros((8, 128), F32)
    for r in range(4):
        for g in range(2):
            h = g * 4 + r
            oq[:, h * 256 : h * 256 + 256] = ry[0][r, :, g * 256 : g * 256 + 256].astype(F32)
            ok[:, h * 128 : h * 128 + 128] = ry[0][r, :, 512 + g * 128 : 640 + g * 128].astype(F32)
            ov[:, h * 128 : h * 128 + 128] = ry[0][r, :, 768 + g * 128 : 896 + g * 128].astype(F32)
            og[:, h * 384 : h * 384 + 384] = ry[1][r, :, g * 384 : g * 384 + 384].astype(F32)
            ou[:, h * 384 : h * 384 + 384] = ry[1][r, :, 768 + g * 384 : 1152 + g * 384].astype(F32)
        gain = gain + ry[0][r, :, 1024:1152].astype(F32)
    ogain[...] = gain
    for copy in over + first + second + third:
        copy.wait_send()


def grads_out(ga, gb, go, gd):
    sds = jax.ShapeDtypeStruct
    scratch = []
    for lead in (
        lambda cut: (16 * cut,),
        lambda cut: (16 * cut,),
        lambda cut: (4, 4, cut),
        lambda cut: (3, 4, cut),
        lambda cut: (4, cut),
        lambda cut: (3, cut),
        lambda cut: (cut,),
        lambda cut: (cut,),
    ):
        for rows, cols, cut in GRADS:
            scratch.append(pltpu.VMEM(lead(cut) + (rows, cols), BF))
    n = len(GRADS)
    scratch += [DMA((n,)), DMA((n,)), DMA((n,))] + [DMA((n, 3))] * 6
    return pl.pallas_call(
        grads_kernel,
        out_shape=(
            sds((8, 2048), F32),
            sds((8, 1024), F32),
            sds((8, 1024), F32),
            sds((8, 3072), F32),
            sds((8, 3072), F32),
            sds((16, 1024), F32),
            sds((24, 1024), F32),
            sds((8, 128), F32),
        ),
        in_specs=[HBM] * 4,
        out_specs=(VMEM,) * 8,
        scratch_shapes=scratch,
        compiler_params=params(1),
        name="grads_out",
    )(ga, gb, go, gd)


def rms_scale(rows):
    return lax.rsqrt(jnp.mean(rows * rows, axis=-1, keepdims=True) + EPS)


def norm_back(d_normed, unit, scale, gain):
    d_unit = d_normed * gain
    return scale * (d_unit - unit * jnp.mean(d_unit * unit, axis=-1, keepdims=True))


def rope_tables():
    freq = ROPE_BASE ** (-np.arange(0, HEAD_SIZE, 2, dtype=np.float64) / HEAD_SIZE)
    freq = np.concatenate([freq, freq])
    inner = np.arange(CHUNK)[:, None] * freq[None, :]
    outer = (np.arange(32) * CHUNK)[:, None] * freq[None, :]
    return [f(a).astype(np.float32) for a in (inner, outer) for f in (np.cos, np.sin)]


def rotate_half(rows):
    half = rows.shape[-1] // 2
    return jnp.concatenate([-rows[..., half:], rows[..., :half]], axis=-1)


def head_prep(raw, gain, cos, sin):
    normed = raw * rms_scale(raw) * gain
    return normed * cos + rotate_half(normed) * sin


def dot(a, b, ca, cb):
    return lax.dot_general(a, b, (((ca,), (cb,)), ((), ())), preferred_element_type=F32)


def local(
    tokens, cotangent, segments, attn_gain, w_query, key_matrix, value_matrix, query_gain, key_gain,
    w_out, ffn_gain, w_gate, w_up, w_down,
):
    y = lax.rem(lax.axis_index("head"), 4)
    chunk = 2 * lax.axis_index("blk") + lax.div(lax.axis_index("head"), 4)
    own_gains = jnp.concatenate(
        [
            attn_gain[:, None],
            ffn_gain[:, None],
            jnp.broadcast_to(query_gain[None, :], (8, 1)),
            jnp.broadcast_to(key_gain[None, :], (8, 1)),
            jnp.zeros((8, 124), BF),
        ],
        axis=1,
    )
    xs, cs, wa, wb, wo, wd = gather_all(
        tokens, cotangent, w_query, key_matrix, value_matrix, w_gate, w_up, own_gains, w_out, w_down
    )
    wa = wa.reshape(1024, 1152)
    wb = wb.reshape(1024, 1536)
    wo = wo.reshape(512, 1024)
    wd = wd.reshape(768, 1024)
    cot = cs.reshape(CHUNK, 1024)
    gains = wa[:, 1024:1028].astype(F32)
    attn_g, ffn_g = gains[:, 0], gains[:, 1]
    q_gain, k_gain = gains[::8, 2], gains[::8, 3]

    x = xs.reshape(CHUNK, 1024).astype(F32)
    scale_one = rms_scale(x)
    x_normed = (x * scale_one * attn_g).astype(BF)
    raw = dot(x_normed, wa[:, :1024], 1, 0)
    q_raw = raw[:, :512].reshape(CHUNK, 4, HEAD_SIZE)
    k_raw = raw[:, 512:768].reshape(CHUNK, 2, HEAD_SIZE)
    v = raw[:, 768:1024].astype(BF)
    in_cos, in_sin, out_cos, out_sin = rope_tables()
    c0 = lax.dynamic_slice_in_dim(jnp.asarray(out_cos), chunk, 1, 0)
    s0 = lax.dynamic_slice_in_dim(jnp.asarray(out_sin), chunk, 1, 0)
    cos = (c0 * in_cos - s0 * in_sin)[:, None, :]
    sin = (s0 * in_cos + c0 * in_sin)[:, None, :]

    def prep(q, k, qg, kg):
        return head_prep(q, qg, cos, sin), head_prep(k, kg, cos, sin)

    (q_rot, k_rot), prep_back = jax.vjp(prep, q_raw, k_raw, q_gain, k_gain)
    q = q_rot.astype(BF)
    k = k_rot.astype(BF).reshape(CHUNK, 256)
    kv = halo(jnp.concatenate([k, v], axis=1), 2).reshape(3 * CHUNK, 512)
    k_ext = kv[:, :256].reshape(3 * CHUNK, 2, HEAD_SIZE)
    v_ext = kv[:, 256:].reshape(3 * CHUNK, 2, HEAD_SIZE)
    q4 = q.reshape(CHUNK, 2, 2, HEAD_SIZE)

    padded = jnp.concatenate([jnp.full((2 * CHUNK,), -1, jnp.int32), segments])
    seg_keys = lax.dynamic_slice_in_dim(padded, chunk * CHUNK, 3 * CHUNK, 0)
    seg_rows = seg_keys[2 * CHUNK :]
    begins = jnp.sum((seg_keys[None, :] < seg_rows[:, None]).astype(jnp.int32), axis=1)
    row = jnp.arange(CHUNK, dtype=jnp.int32)
    low = jnp.maximum(begins, row + 1)
    column = jnp.arange(3 * CHUNK, dtype=jnp.int32)[None, :]
    allowed = (column >= low[:, None]) & (column <= row[:, None] + SPAN)
    attn_scale = HEAD_SIZE ** (-0.5)
    scores = jnp.einsum("qkgd,ckd->kgqc", q4, k_ext, preferred_element_type=F32) * attn_scale
    scores = jnp.where(allowed[None, None], scores, MASKED)
    peak = jnp.max(scores, axis=-1, keepdims=True)
    weight = jnp.exp(scores - peak)
    total = jnp.sum(weight, axis=-1, keepdims=True)
    soft = weight / total
    probs = soft.astype(BF)
    attended = jnp.einsum("kgqc,ckd->qkgd", probs, v_ext, preferred_element_type=F32)
    attended = attended.astype(BF).reshape(CHUNK, 512)

    part = dot(attended, wo, 1, 0).astype(BF).reshape(4, 128, 1024)
    x_own = tokens.astype(F32)
    mid_sum = x_own + ring_sum(part, 3)
    scale_two = rms_scale(mid_sum)
    mid_unit = mid_sum * scale_two
    mid = ring_gather((mid_unit * ffn_g).astype(BF), 4).reshape(CHUNK, 1024)
    gate_up = dot(mid, wb, 1, 0)
    gate, up = gate_up[:, :768], gate_up[:, 768:]
    sig = jax.nn.sigmoid(gate)
    act = gate * sig
    hidden = (act * up).astype(BF)
    out_part = dot(hidden, wd, 1, 0).astype(BF).reshape(4, 128, 1024)
    output = (mid_sum + ring_sum(out_part, 5)).astype(BF)
    d_hidden = dot(cot, wd, 1, 1)
    d_gate = (d_hidden * up * sig * (1.0 + gate * (1.0 - sig))).astype(BF)
    d_up = (d_hidden * act).astype(BF)
    d_gu = jnp.concatenate([d_gate, d_up], axis=1)
    d_mid_normed = ring_sum(dot(d_gu, wb, 1, 1).astype(BF).reshape(4, 128, 1024), 6)
    d_mid = cotangent.astype(F32) + norm_back(d_mid_normed, mid_unit, scale_two, ffn_g)
    d_branch = ring_gather(d_mid.astype(BF), 7).reshape(CHUNK, 1024)
    d_att = dot(d_branch, wo, 1, 1).astype(BF)
    d4 = d_att.reshape(CHUNK, 2, 2, HEAD_SIZE)

    d_v = jnp.einsum("kgqc,qkgd->ckd", probs, d4, preferred_element_type=F32)
    d_probs = jnp.einsum("qkgd,ckd->kgqc", d4, v_ext, preferred_element_type=F32)
    inner = jnp.sum(soft * d_probs, axis=-1, keepdims=True)
    d_scores = (soft * (d_probs - inner)).astype(BF)
    d_q = jnp.einsum("kgqc,ckd->qkgd", d_scores, k_ext, preferred_element_type=F32) * attn_scale
    d_k = jnp.einsum("kgqc,qkgd->ckd", d_scores, q4, preferred_element_type=F32) * attn_scale
    d_kv = jnp.concatenate([d_k.reshape(3 * CHUNK, 256), d_v.reshape(3 * CHUNK, 256)], axis=1)
    d_kv = halo_back(d_kv.astype(BF).reshape(3, CHUNK, 512), 8)
    d_kv = d_kv.astype(BF)
    d_q_raw, d_k_raw, g_qg, g_kg = prep_back(
        (
            d_q.astype(BF).astype(F32).reshape(CHUNK, 4, HEAD_SIZE),
            d_kv[:, :256].astype(F32).reshape(CHUNK, 2, HEAD_SIZE),
        )
    )
    d_qkv = jnp.concatenate(
        [
            d_q_raw.astype(BF).reshape(CHUNK, 512),
            d_k_raw.astype(BF).reshape(CHUNK, 256),
            d_kv[:, 256:],
        ],
        axis=1,
    )
    d_x_normed = ring_sum(dot(d_qkv, wa[:, :1024], 1, 1).astype(BF).reshape(4, 128, 1024), 9)
    scale_own = rms_scale(x_own)
    unit_own = x_own * scale_own
    input_grad = (d_mid + norm_back(d_x_normed, unit_own, scale_own, attn_g)).astype(BF)

    g_attn = jnp.sum(d_x_normed * unit_own, axis=0)
    g_ffn = jnp.sum(d_mid_normed * mid_unit, axis=0)
    g_gains = jnp.concatenate(
        [
            g_attn[:, None],
            g_ffn[:, None],
            jnp.repeat(g_qg, 8)[:, None],
            jnp.repeat(g_kg, 8)[:, None],
            jnp.zeros((1024, 124), F32),
        ],
        axis=1,
    ).astype(BF)
    ga = jnp.concatenate([dot(x_normed, d_qkv, 0, 0).astype(BF), g_gains], axis=1)
    gb = dot(mid, d_gu, 0, 0).astype(BF)
    go = dot(attended, d_branch, 0, 0).astype(BF)
    gd = dot(hidden, cot, 0, 0).astype(BF)
    oq, ok, ov, og, ou, oo, od, ogain = grads_out(
        ga.reshape(64, 2, 8, 1152),
        gb.reshape(64, 2, 8, 1536),
        go.reshape(16, 2, 16, 1024),
        gd.reshape(16, 2, 24, 1024),
    )
    return (
        output,
        input_grad,
        ogain[:, 0],
        oq,
        ok,
        ov,
        ogain[0, 2:3],
        ogain[0, 3:4],
        oo,
        ogain[:, 1],
        og,
        ou,
        od,
    )


def solution(mesh):
    rows = P(("blk", "head"), None)
    cut = P(("head", "blk"), None)
    vec = P(("head", "blk"))
    return jax.shard_map(
        local,
        mesh=mesh,
        in_specs=(rows, rows, P(), vec, cut, cut, cut, vec, vec, cut, vec, cut, cut, cut),
        out_specs=(rows, rows, vec, cut, cut, cut, vec, vec, cut, vec, cut, cut, cut),
        check_vma=False,
    )
```

time: 1170 us -> 410 us (0.35)
  the two profiles are of different devices: /device:TPU:0 before, /device:TPU:1 now
where the time goes in v1:
time: 410 us; the launch traced here: 402 us
  Pallas kernels  232 us (57%)
  matrix products  65.4 us (16%)
  local copies, waits for them, and re-layouts  57 us (14%)
  other arithmetic  44.2 us (11%)
    pallas_call x4, Pallas kernels, ring_sum(): pl.pallas_call(ring_sum_kernel, out_shape=jax.ShapeDtypeStruct((rows, col...  67 us
    pallas_call x1, Pallas kernels, grads_out(): pl.pallas_call(grads_kernel, out_shape=(sds((8, 2048), F32), sds((8, 1024...  50.7 us
    pallas_call x1, Pallas kernels, gather_all(): pl.pallas_call(gather_kernel, out_shape=(sds((4, 128, 1024), BF), sds((4,...  47.9 us
    dot_general x12, matrix products, dot(): lax.dot_general(a, b, (((ca,), (cb,)), ((), ())), preferred_element_type=...  29.8 us
    pallas_call x2, Pallas kernels, ring_gather(): pl.pallas_call(ring_gather_kernel, out_shape=jax.ShapeDtypeStruct((4,) +...  29.3 us
    pallas_call x1, Pallas kernels, halo(): pl.pallas_call(halo_kernel, out_shape=jax.ShapeDtypeStruct((3,) + kv.shap...  19.6 us
    pallas_call x1, Pallas kernels, halo_back(): pl.pallas_call(halo_back_kernel, out_shape=jax.ShapeDtypeStruct(dkv.shape...  17.6 us
    unnamed x89, local copies, waits for them, and re-layouts  15 us

profile of v1, /device:TPU:1, one launch (start us, length us, event | category | flops | bytes accessed | tf_op | source)
XLA Modules:
  0.0 401.9 jit_solution(473592221199543805)
XLA Ops:
  9.3 1.7 fusion.12
  11.1 47.9 %gather_all.1 = (bf16[4,128,1024]{2,1,0:T(8,128)(2,1)}, bf16[4,128,1024]{2,1,0:T(8,128)(2,1)}, bf16[2,4,16,8,1152]{4,3,2,1,0:T(8,128)(2,1)}, bf16[2,4,16,8,1536]...) custom-call(bf16[128,1024]{1,0:T(8,128)(2,1)} %tok.1, ...), custom_call_target="tpu_custom_call" | custom-call | tf_op jit(solution)/shard_map/gather_all/pallas_call | solution.py:197
  59.0 1.6 multiply_reduce_fusion
  62.5 3.2 fusion.29
  72.9 1.9 pad_maximum_fusion.5.kv
  76.5 19.6 %halo.1 = bf16[3,512,512]{2,1,0:T(8,128)(2,1)} custom-call(bf16[512,512]{1,0:T(8,128)(2,1)} %pad_maximum_fusion.5.kv), custom_call_target="tpu_custom_call" | custom-call | tf_op jit(solution)/shard_map/halo/pallas_call | solution.py:299
  96.1 1.5 fusion.69
  99.0 11.4 %fusion.74 = (f32[2,2,512]{2,1,0:T(2,128)S(1)}, f32[2,2,512,1536]{2,3,1,0:T(8,128)}) fusion(pred[512,1536]{0,1:T(8,128)(4,1)} %fusion.12, bf16[1536,2,128,1]{0,2,3,1:T(8,128)(2,1)} %bitcast.174, bf16[512,2,2,128]{0,3,2,1:T(8,128)(2,1)} %fusion.44), kind=kOutput, calls=%fused_computation.144 | convolution fusion | flops 817890816 | bytes 14688256 | tf_op jit(solution)/shard_map/sub | solution.py:557
  110.4 5.7 %fusion.37 = bf16[2,128,2,512]{3,1,2,0:T(8,128)(2,1)S(1)} fusion(bf16[1536,2,128,1]{0,2,3,1:T(8,128)(2,1)S(1)} %bitcast.191, f32[2,2,512,1536]{2,3,1,0:T(8,128)} %get-tuple-element.80, f32[2,2,512]{2,1,0:T(2,128)S(1)} %get-tuple-element.79), kind=kOutput, calls=%fused_computation.54 | convolution fusion | flops 811859968 | bytes 13901824 | tf_op jit(solution)/shard_map/kgqc,ckd->qkgd/dot_general | solution.py:561
  116.1 1.7 convolution_convert_fusion.6
  117.8 21.1 %ring_sum.4 = f32[128,1024]{1,0:T(8,128)} custom-call(bf16[4,128,1024]{2,1,0:T(8,128)(2,1)} %bitcast.189), custom_call_target="tpu_custom_call" | custom-call | tf_op jit(solution)/shard_map/ring_sum/pallas_call | solution.py:270
  141.0 14.2 %ring_gather.2 = bf16[4,128,1024]{2,1,0:T(8,128)(2,1)} custom-call(bf16[128,1024]{1,0:T(8,128)(2,1)} %multiply_convert_fusion.3.src), custom_call_target="tpu_custom_call" | custom-call | tf_op jit(solution)/shard_map/ring_gather/pallas_call | solution.py:242
  155.2 4.1 %fusion.75 = f32[512,1536]{1,0:T(8,128)S(1)} fusion(bf16[512,1024]{1,0:T(8,128)(2,1)} %bitcast.182, bf16[1024,1536]{1,0:T(8,128)(2,1)} %bitcast.217), kind=kOutput, calls=%fused_computation.145 | convolution fusion | flops 1610612736 | bytes 7340032 | tf_op jit(solution)/shard_map/dot_general | solution.py:490
  159.5 1.6 multiply_convert_fusion.1
  161.2 2.0 convolution_convert_fusion.3
  164.3 2.8 convolution_convert_fusion.4
  167.1 17.0 %ring_sum.6 = f32[128,1024]{1,0:T(8,128)} custom-call(bf16[4,128,1024]{2,1,0:T(8,128)(2,1)} %bitcast.188), custom_call_target="tpu_custom_call" | custom-call | tf_op jit(solution)/shard_map/ring_sum/pallas_call | solution.py:270
  184.2 17.0 %ring_sum.5 = f32[128,1024]{1,0:T(8,128)} custom-call(bf16[4,128,1024]{2,1,0:T(8,128)(2,1)} %bitcast.186), custom_call_target="tpu_custom_call" | custom-call | tf_op jit(solution)/shard_map/ring_sum/pallas_call | solution.py:270
  203.6 3.5 convolution_convert_fusion
  207.1 2.1 convolution_convert_fusion.2
  209.2 15.1 %ring_gather.3 = bf16[4,128,1024]{2,1,0:T(8,128)(2,1)} custom-call(bf16[128,1024]{1,0:T(8,128)(2,1)} %fusion.67.src), custom_call_target="tpu_custom_call" | custom-call | tf_op jit(solution)/shard_map/ring_gather/pallas_call | solution.py:242
  224.3 2.0 convolution_convert_fusion.7
  226.4 1.7 convolution_convert_fusion.5
  228.1 7.7 %fusion.22 = bf16[1536,2,128]{0,2,1:T(8,128)(2,1)} fusion(bf16[512,2,2,128]{0,3,2,1:T(8,128)(2,1)S(1)} %bitcast.227, f32[2,2,512,1536]{2,3,1,0:T(8,128)} %get-tuple-element.80, f32[2,2,512]{2,1,0:T(2,128)S(1)} %get-tuple-element.79), kind=kOutput, calls=%fused_computation.28 | convolution fusion | flops 811991040 | bytes 13901824 | tf_op jit(solution)/shard_map/kgqc,qkgd->ckd/dot_general | solution.py:587
  235.8 2.2 copy.152
  239.5 6.9 %fusion.1 = (f32[2,2,512]{2,1,0:T(2,128)S(1)}, f32[2,1536,512,2]{2,1,3,0:T(8,128)S(1)}) fusion(f32[2,2,512,1536]{2,3,1,0:T(8,128)} %get-tuple-element.80, f32[2,2,512]{2,1,0:T(2,128)S(1)} %get-tuple-element.79, bf16[1536,2,128,1]{0,2,3,1:T(8,128)(2,1)} %bitcast.192, bf16[512,2,2,128]{0,3,2,1:T(8,128)(2,1)} %bitcast.228), kind=kOutput, calls=%fused_computation.3 | convolution fusion | flops 814741504 | bytes 26492928 | tf_op jit(solution)/shard_map/qkgd,ckd->kgqc/dot_general | solution.py:588
  246.3 7.1 %fusion.3 = bf16[2,2,512,1536]{2,3,1,0:T(8,128)(2,1)S(1)} fusion(f32[2,1536,512,2]{2,1,3,0:T(8,128)S(1)} %get-tuple-element.82, f32[2,2,512]{2,1,0:T(2,128)S(1)} %get-tuple-element.81, f32[2,2,512,1536]{2,3,1,0:T(8,128)} %get-tuple-element.80, f32[2,2,512]{2,1,0:T(2,128)S(1)} %get-tuple-element.79), kind=kLoop, calls=%fused_computation.5 | loop fusion | flops 12582912 | bytes 31473664 | tf_op jit(solution)/shard_map/convert_element_type | solution.py:590
  254.5 3.0 fusion.21
  257.6 3.0 copy.150
  260.6 3.1 concatenate.49
  263.7 2.6 pad_maximum_fusion.1.dkv
  266.4 17.6 %halo_back.1 = f32[512,512]{1,0:T(8,128)} custom-call(bf16[3,512,512]{2,1,0:T(8,128)(2,1)} %pad_maximum_fusion.1.dkv), custom_call_target="tpu_custom_call" | custom-call | tf_op jit(solution)/shard_map/halo_back/pallas_call | solution.py:320
  286.2 2.1 reshape.323
  288.3 1.8 copy.156
  292.4 3.5 multiply_reduce_fusion.4
  298.0 4.2 %fusion.56 = bf16[512,2,128]{2,1,0:T(2,128)(2,1)} fusion(f32[512,2,128]{2,1,0:T(2,128)S(1)} %reshape.291, f32[512,2,128]{2,1,0:T(2,128)} %get-tuple-element.52, f32[512,2]{1,0:T(8,128)} %copy.154, f32[128]{0:T(128)S(1)} %bitcast.214, f32[512,2]{1,0:T(8,128)S(1)} %copy.136), kind=kLoop, calls=%fused_computation.84 | loop fusion | flops 786432 | bytes 1319424 | tf_op jit(solution)/shard_map/convert_element_type | solution.py:605
  306.9 2.3 fusion.32
  309.2 2.6 convolution_convert_fusion.1
  311.8 11.8 %ring_sum.7 = f32[128,1024]{1,0:T(8,128)} custom-call(bf16[4,128,1024]{2,1,0:T(8,128)(2,1)} %bitcast.187), custom_call_target="tpu_custom_call" | custom-call | tf_op jit(solution)/shard_map/ring_sum/pallas_call | solution.py:270
  325.0 2.1 fusion.53
  327.3 7.9 %concatenate.53 = bf16[1024,1152]{0,1:T(8,128)(2,1)S(1)} concatenate(bf16[1024,1024]{0,1:T(8,128)(2,1)} %convolution_convert_fusion.1, bf16[1024,1]{0,1:T(2,128)(2,1)S(1)} %broadcast_in_dim.90, bf16[1024,1]{0,1:T(2,128)(2,1)S(1)} %broadcast_in_dim.91, bf16[1024,1]{0,1:T(2,128)(2,1)S(1)} %broadcast_in_dim_reshape.8, bf16[1024,1]{0,1:T(2,128)(2,1)S(1)} %broadcast_in_dim_reshape.9, ...), dimensions={1} | concatenate | bytes 4718592 | tf_op jit(solution)/shard_map/concatenate | solution.py:627
  335.3 2.6 copy.157
  337.8 50.7 %grads_out.1 = (f32[8,2048]{1,0:T(8,128)}, f32[8,1024]{1,0:T(8,128)}, f32[8,1024]{1,0:T(8,128)}, f32[8,3072]{1,0:T(8,128)}, f32[8,3072]{1,0:T(8,128)}, /*index=5...) custom-call(bf16[64,2,8,1152]{3,2,1,0:T(8,128)(2,1)} %bitcast.171, bf16[64,2,8,1536]{3,2,1,0:T(8,128)(2,1)} %bitcast.173, ...), custom_call_target="tpu_custom_call" | custom-call | tf_op jit(solution)/shard_map/grads_out/pallas_call | solution.py:442
  389.9 1.5 slice_reduce_fusion
  395.6 1.5 copy.196
  397.1 1.5 copy.197
  398.6 1.5 copy.198
  400.2 1.5 copy.199
  (161 shorter events, 45.5 us)
Async XLA Ops:
  8.0 67.2 %copy-start.6 = (f32[512,128]{0,1:T(8,128)}, f32[512,128]{0,1:T(8,128)S(1)}, u32[]{:S(2)}) copy-start(f32[512,128]{0,1:T(8,128)S(1)} %get-tuple-element.64) | copy-start | bytes 786436
  8.1 67.2 %copy-start.8 = (f32[512,128]{0,1:T(8,128)}, f32[512,128]{0,1:T(8,128)S(1)}, u32[]{:S(2)}) copy-start(f32[512,128]{0,1:T(8,128)S(1)} %get-tuple-element.65) | copy-start | bytes 786436
  8.2 2.9 copy-start.12
  8.3 62.2 %copy-start.14 = (f32[512,128]{1,0:T(8,128)}, f32[512,128]{1,0:T(8,128)S(1)}, u32[]{:S(2)}) copy-start(f32[512,128]{1,0:T(8,128)S(1)} %copy.138) | copy-start | bytes 786436
  59.0 3.2 copy-start.3
  62.5 3.2 copy-start.20
  65.8 1.4 copy-start.4
  69.3 1.9 copy-start.5
  69.3 1.9 copy-start.18
  71.2 1.3 slice-start
  99.0 11.4 %copy-start.24 = (bf16[1536,256]{0,1:T(8,128)(2,1)}, bf16[1536,256]{0,1:T(8,128)(2,1)S(1)}, u32[]{:S(2)}) copy-start(bf16[1536,256]{0,1:T(8,128)(2,1)S(1)} %copy.139) | copy-start | bytes 2359300
  110.4 5.7 %copy-start.29 = (bf16[2,16,16,1024]{3,2,1,0:T(8,128)(2,1)S(1)}, bf16[2,16,16,1024]{3,2,1,0:T(8,128)(2,1)}, u32[]{:S(2)}) copy-start(bf16[2,16,16,1024]{3,2,1,0:T(8,128)(2,1)} %get-tuple-element.29) | copy-start | bytes 3145732
  116.1 22.8 %copy-start.9 = (bf16[128,1024]{1,0:T(8,128)(2,1)S(1)}, bf16[128,1024]{1,0:T(8,128)(2,1)}, u32[]{:S(2)}) copy-start(bf16[128,1024]{1,0:T(8,128)(2,1)} %tok.1) | copy-start | bytes 786436
  155.1 4.2 %copy-start.28 = (bf16[2,16,24,1024]{3,2,1,0:T(8,128)(2,1)S(1)}, bf16[2,16,24,1024]{3,2,1,0:T(8,128)(2,1)}, u32[]{:S(2)}) copy-start(bf16[2,16,24,1024]{3,2,1,0:T(8,128)(2,1)} %get-tuple-element.31) | copy-start | bytes 4718596
  155.2 4.2 %copy-start.31 = (bf16[4,128,1024]{2,1,0:T(8,128)(2,1)S(1)}, bf16[4,128,1024]{2,1,0:T(8,128)(2,1)}, u32[]{:S(2)}) copy-start(bf16[4,128,1024]{2,1,0:T(8,128)(2,1)} %get-tuple-element.32) | copy-start | bytes 3145732
  161.2 2.0 copy-start.34
  161.2 2.0 copy-start.36
  161.2 2.0 copy-start.38
  161.2 3.1 copy-start.27
  167.1 35.5 %copy-start.15 = (bf16[128,1024]{1,0:T(8,128)(2,1)S(1)}, bf16[128,1024]{1,0:T(8,128)(2,1)}, u32[]{:S(2)}) copy-start(bf16[128,1024]{1,0:T(8,128)(2,1)} %cot.1) | copy-start | bytes 786436
  184.2 18.5 %copy-start = (f32[128,1024]{1,0:T(8,128)S(1)}, f32[128,1024]{1,0:T(8,128)}, u32[]{:S(2)}) copy-start(f32[128,1024]{1,0:T(8,128)} %ring_sum.6) | copy-start | bytes 1572868
  184.2 19.4 %copy-start.22 = (bf16[4,128,1024]{2,1,0:T(8,128)(2,1)S(1)}, bf16[4,128,1024]{2,1,0:T(8,128)(2,1)}, u32[]{:S(2)}) copy-start(bf16[4,128,1024]{2,1,0:T(8,128)(2,1)} %ring_gather.2) | copy-start | bytes 3145732
  184.2 19.4 %copy-start.37 = (bf16[512,768]{1,0:T(8,128)(2,1)S(1)}, bf16[512,768]{1,0:T(8,128)(2,1)}, u32[]{:S(2)}) copy-start(bf16[512,768]{1,0:T(8,128)(2,1)} %copy-done.36) | copy-start | bytes 2359300
  201.3 2.3 copy-start.39
  203.6 3.5 copy-start.32
  203.6 3.5 copy-start.35
  207.1 17.2 %copy-start.30 = (bf16[2,16,16,1024]{3,2,1,0:T(8,128)(2,1)S(1)}, bf16[2,16,16,1024]{3,2,1,0:T(8,128)(2,1)}, u32[]{:S(2)}) copy-start(bf16[2,16,16,1024]{3,2,1,0:T(8,128)(2,1)} %get-tuple-element.29) | copy-start | bytes 3145732
  224.3 2.1 copy-start.23
  226.4 1.7 copy-start.33
  246.3 7.1 %copy-start.11 = (bf16[1536,256]{0,1:T(8,128)(2,1)S(1)}, bf16[1536,256]{0,1:T(8,128)(2,1)}, u32[]{:S(2)}) copy-start(bf16[1536,256]{0,1:T(8,128)(2,1)} %copy.177) | copy-start | bytes 2359300
  253.5 1.0 copy-start.19
  290.1 2.2 copy-start.2
  290.1 2.2 copy-start.13
  303.4 1.3 copy-start.7
  305.2 1.0 copy-start.25
  305.2 1.8 copy-start.26
  306.9 2.3 copy-start.21
  309.2 14.5 %copy-start.10 = (bf16[128,1024]{1,0:T(8,128)(2,1)S(1)}, bf16[128,1024]{1,0:T(8,128)(2,1)}, u32[]{:S(2)}) copy-start(bf16[128,1024]{1,0:T(8,128)(2,1)} %tok.1) | copy-start | bytes 786436
  311.8 13.2 %copy-start.1 = (f32[128,1024]{1,0:T(8,128)S(1)}, f32[128,1024]{1,0:T(8,128)}, u32[]{:S(2)}) copy-start(f32[128,1024]{1,0:T(8,128)} %ring_sum.6) | copy-start | bytes 1572868
  311.8 13.2 %copy-start.16 = (bf16[128,1024]{1,0:T(8,128)(2,1)S(1)}, bf16[128,1024]{1,0:T(8,128)(2,1)}, u32[]{:S(2)}) copy-start(bf16[128,1024]{1,0:T(8,128)(2,1)} %cot.1) | copy-start | bytes 786436
  311.8 13.2 %copy-start.17 = (f32[128,1024]{1,0:T(8,128)S(1)}, f32[128,1024]{1,0:T(8,128)}, u32[]{:S(2)}) copy-start(f32[128,1024]{1,0:T(8,128)} %ring_sum.5) | copy-start | bytes 1572868

commit v2 on v1

--- a/solution.py
+++ b/solution.py
@@ -224,32 +224,6 @@
     )(tok, cot, wq, wk, wv, wg, wu, gains, wo, wd)
 
 
-def ring_gather_kernel(src, out, ssem, rsem, lsem):
-    x, y, z, c = coords()
-    ring = [device(x, wrap4(y + k), z, c) for k in range(1, 4)]
-    meet(ring)
-    copies = [send(src, out.at[y], ssem.at[k], rsem.at[k], ring[k]) for k in range(3)]
-    own = pltpu.make_async_copy(src, out.at[y], lsem)
-    own.start()
-    for k in range(3):
-        arrived(out.at[wrap4(y - k - 1)], rsem.at[k], ring[0])
-    own.wait()
-    for copy in copies:
-        copy.wait_send()
-
-
-def ring_gather(rows, collective_id):
-    return pl.pallas_call(
-        ring_gather_kernel,
-        out_shape=jax.ShapeDtypeStruct((4,) + rows.shape, rows.dtype),
-        in_specs=[HBM],
-        out_specs=HBM,
-        scratch_shapes=[DMA((3,)), DMA((3,)), DMA],
-        compiler_params=params(collective_id),
-        name="ring_gather",
-    )(rows)
-
-
 def ring_sum_kernel(part, out, land, ssem, rsem):
     x, y, z, c = coords()
     ring = [device(x, wrap4(y + k), z, c) for k in range(1, 4)]
@@ -328,135 +302,327 @@
     )(dkv)
 
 
-GRADS = ((8, 1152, 4), (8, 1536, 4), (16, 1024, 1), (24, 1024, 1))
-
-
-def grads_kernel(ga, gb, go, gd, oq, ok, ov, og, ou, oo, od, ogain, *scratch):
-    n_arr = len(GRADS)
-    rc, lc, sa, lb, sb, l2, sd, ry = [scratch[i * n_arr : (i + 1) * n_arr] for i in range(8)]
-    csem, crec, lsem, p2s, p2r, p1s, p1r, ys, yr = scratch[8 * n_arr :]
-    x, y, z, c = coords()
-    d = 1 - c
-
-    def to(j, k):
-        return device(wrap4(x + j * d + k * c), y, wrap4(z + j * c + k * d), c)
-
-    across = device(x, y, z, 1 - c)
-    ring = [device(x, wrap4(y + k), z, c) for k in range(1, 4)]
-    meet(ring + [to(k, 0) for k in range(1, 4)] + [to(0, k) for k in range(1, 4)] + [across])
-    p1 = x * d + z * c
-    p2 = x * c + z * d
-    ins = (ga, gb, go, gd)
-    over, kept = [], []
-    for n in range(n_arr):
-        over.append(send(ins[n].at[:, 1 - c], rc[n], csem.at[n], crec.at[n], across))
-        own = pltpu.make_async_copy(ins[n].at[:, c], lc[n], lsem.at[n])
-        own.start()
-        kept.append(own)
-
-    first, second, third = [], [], []
-    for n, (rows, cols, cut) in enumerate(GRADS):
-        over[n].wait_recv()
-        kept[n].wait()
-
-        def add_cores(i, _, n=n, cut=cut):
+class Sums:
+    def __init__(self, grad, rows, cols, cut, refs):
+        self.grad, self.rows, self.cols, self.cut = grad, rows, cols, cut
+        (self.rc, self.sa, self.lb, self.sb, self.l2, self.sd, self.ry, self.ss, self.rs) = refs
+        x, y, z, c = coords()
+        self.y, self.c, self.d = y, c, 1 - c
+        d = self.d
+        self.across = device(x, y, z, d)
+        self.ring = [device(x, wrap4(y + k), z, c) for k in range(1, 4)]
+        self.to_first = [device(wrap4(x + k * d), y, wrap4(z + k * c), c) for k in range(1, 4)]
+        self.to_second = [device(wrap4(x + k * c), y, wrap4(z + k * d), c) for k in range(1, 4)]
+        self.p1 = x * d + z * c
+        self.p2 = x * c + z * d
+        self.sends = []
+
+    @staticmethod
+    def scratch(rows, cols, cut):
+        buffers = [(16 * cut,), (4, 4, cut), (3, 4, cut), (4, cut), (3, cut), (cut,), (cut,)]
+        return [pltpu.VMEM(lead + (rows, cols), BF) for lead in buffers] + [DMA((10,)), DMA((10,))]
+
+    def start(self):
+        self.over = send(self.grad.at[:, self.d], self.rc, self.ss.at[9], self.rs.at[9], self.across)
+        self.sends.append(self.over)
+
+    def cores(self):
+        self.over.wait_recv()
+        c, d, cut = self.c, self.d, self.cut
+
+        def add(i, _):
             a2, a1, r = lax.div(i, 4 * cut), lax.rem(lax.div(i, cut), 4), lax.rem(i, cut)
             px, pz = a1 * d + a2 * c, a1 * c + a2 * d
             at = ((lax.div(px, 2) * cut + r) * 2 + lax.rem(px, 2)) * 4 + pz
-            sa[n][a2, a1, r] = (rc[n][at].astype(F32) + lc[n][at].astype(F32)).astype(BF)
+            self.sa[a2, a1, r] = (self.rc[at].astype(F32) + self.grad[at, c].astype(F32)).astype(BF)
             return 0
 
-        lax.fori_loop(0, 16 * cut, add_cores, 0)
-        for k in range(1, 4):
-            first.append(
-                send(sa[n].at[wrap4(p2 + k)], lb[n].at[k - 1], p2s.at[n, k - 1], p2r.at[n, k - 1], to(0, k))
-            )
-    for n, (rows, cols, cut) in enumerate(GRADS):
-        for k in range(3):
-            first[3 * n + k].wait_recv()
-
-        def add_second(i, _, n=n, cut=cut):
-            a1, r = lax.div(i, cut), lax.rem(i, cut)
-            total = sa[n][p2, a1, r].astype(F32)
+        lax.fori_loop(0, 16 * cut, add, 0)
+        self.hop = [
+            send(self.sa.at[wrap4(self.p2 + k + 1)], self.lb.at[k], self.ss.at[k], self.rs.at[k], self.to_second[k])
+            for k in range(3)
+        ]
+        self.sends += self.hop
+
+    def second(self):
+        for copy in self.hop:
+            copy.wait_recv()
+
+        def add(i, _):
+            a1, r = lax.div(i, self.cut), lax.rem(i, self.cut)
+            total = self.sa[self.p2, a1, r].astype(F32)
             for k in range(3):
-                total = total + lb[n][k, a1, r].astype(F32)
-            sb[n][a1, r] = total.astype(BF)
+                total = total + self.lb[k, a1, r].astype(F32)
+            self.sb[a1, r] = total.astype(BF)
             return 0
 
-        lax.fori_loop(0, 4 * cut, add_second, 0)
-        for k in range(1, 4):
-            second.append(
-                send(sb[n].at[wrap4(p1 + k)], l2[n].at[k - 1], p1s.at[n, k - 1], p1r.at[n, k - 1], to(k, 0))
-            )
-    for n, (rows, cols, cut) in enumerate(GRADS):
-        for k in range(3):
-            second[3 * n + k].wait_recv()
-        for r in range(cut):
-            total = sb[n][p1, r].astype(F32)
+        lax.fori_loop(0, 4 * self.cut, add, 0)
+        self.hop = [
+            send(self.sb.at[wrap4(self.p1 + k + 1)], self.l2.at[k], self.ss.at[3 + k], self.rs.at[3 + k], self.to_first[k])
+            for k in range(3)
+        ]
+        self.sends += self.hop
+
+    def first(self, out=None):
+        for copy in self.hop:
+            copy.wait_recv()
+        for r in range(self.cut):
+            total = self.sb[self.p1, r].astype(F32)
             for k in range(3):
-                total = total + l2[n][k, r].astype(F32)
-            if cut == 1:
-                (oo if n == 2 else od)[...] = total
+                total = total + self.l2[k, r].astype(F32)
+            if out is not None:
+                out[...] = total
             else:
-                sd[n][r] = total.astype(BF)
-        if cut > 1:
-            for k in range(1, 4):
-                third.append(
-                    send(sd[n].at[wrap4(y + k)], ry[n].at[y], ys.at[n, k - 1], yr.at[n, k - 1], ring[k - 1])
-                )
-            ry[n][y] = sd[n][y]
-    for copy in third:
-        copy.wait_recv()
+                self.sd[r] = total.astype(BF)
+        if out is None:
+            y = self.y
+            self.hop = [
+                send(self.sd.at[wrap4(y + k + 1)], self.ry.at[y], self.ss.at[6 + k], self.rs.at[6 + k], self.ring[k])
+                for k in range(3)
+            ]
+            self.sends += self.hop
+            self.ry[y] = self.sd[y]
+
+    def owners(self):
+        for copy in self.hop:
+            copy.wait_recv()
+
+    def done(self):
+        for copy in self.sends:
+            copy.wait_send()
+
+
+def greet_all():
+    x, y, z, c = coords()
+    peers = [device(x, wrap4(y + k), z, c) for k in range(1, 4)]
+    peers += [device(wrap4(x + k), y, z, c) for k in range(1, 4)]
+    peers += [device(x, y, wrap4(z + k), c) for k in range(1, 4)]
+    meet(peers + [device(x, y, z, 1 - c)])
+
+
+def grads_kernel(ga, go, oq, ok, ov, oo, ogain, *scratch):
+    a = Sums(ga, 8, 1152, 4, scratch[:9])
+    o = Sums(go, 16, 1024, 1, scratch[9:18])
+    greet_all()
+    for s in (a, o):
+        s.start()
+    for s in (a, o):
+        s.cores()
+    for s in (a, o):
+        s.second()
+    a.first()
+    o.first(oo)
+    a.owners()
     gain = jnp.zeros((8, 128), F32)
     for r in range(4):
         for g in range(2):
             h = g * 4 + r
-            oq[:, h * 256 : h * 256 + 256] = ry[0][r, :, g * 256 : g * 256 + 256].astype(F32)
-            ok[:, h * 128 : h * 128 + 128] = ry[0][r, :, 512 + g * 128 : 640 + g * 128].astype(F32)
-            ov[:, h * 128 : h * 128 + 128] = ry[0][r, :, 768 + g * 128 : 896 + g * 128].astype(F32)
-            og[:, h * 384 : h * 384 + 384] = ry[1][r, :, g * 384 : g * 384 + 384].astype(F32)
-            ou[:, h * 384 : h * 384 + 384] = ry[1][r, :, 768 + g * 384 : 1152 + g * 384].astype(F32)
-        gain = gain + ry[0][r, :, 1024:1152].astype(F32)
+            oq[:, h * 256 : h * 256 + 256] = a.ry[r, :, g * 256 : g * 256 + 256].astype(F32)
+            ok[:, h * 128 : h * 128 + 128] = a.ry[r, :, 512 + g * 128 : 640 + g * 128].astype(F32)
+            ov[:, h * 128 : h * 128 + 128] = a.ry[r, :, 768 + g * 128 : 896 + g * 128].astype(F32)
+        gain = gain + a.ry[r, :, 1024:1152].astype(F32)
     ogain[...] = gain
-    for copy in over + first + second + third:
-        copy.wait_send()
-
-
-def grads_out(ga, gb, go, gd):
+    a.done()
+    o.done()
+
+
+def grads_out(ga, go):
     sds = jax.ShapeDtypeStruct
-    scratch = []
-    for lead in (
-        lambda cut: (16 * cut,),
-        lambda cut: (16 * cut,),
-        lambda cut: (4, 4, cut),
-        lambda cut: (3, 4, cut),
-        lambda cut: (4, cut),
-        lambda cut: (3, cut),
-        lambda cut: (cut,),
-        lambda cut: (cut,),
-    ):
-        for rows, cols, cut in GRADS:
-            scratch.append(pltpu.VMEM(lead(cut) + (rows, cols), BF))
-    n = len(GRADS)
-    scratch += [DMA((n,)), DMA((n,)), DMA((n,))] + [DMA((n, 3))] * 6
     return pl.pallas_call(
         grads_kernel,
         out_shape=(
             sds((8, 2048), F32),
             sds((8, 1024), F32),
             sds((8, 1024), F32),
+            sds((16, 1024), F32),
+            sds((8, 128), F32),
+        ),
+        in_specs=[VMEM] * 2,
+        out_specs=(VMEM,) * 5,
+        scratch_shapes=Sums.scratch(8, 1152, 4) + Sums.scratch(16, 1024, 1),
+        compiler_params=params(1),
+        name="grads_out",
+    )(ga, go)
+
+
+def middle_kernel(
+    att, tok, cot, wo, wb, wd, gain,
+    out, dmid, datt, gffn, go, og, ou, od,
+    part, land1, acc, unit, mid, dhid, dgu, hid, dpart, land2, dbr, opart, land3, gbs, gds, ssem, rsem,
+    *scratch,
+):
+    x, y, z, c = coords()
+    ring = [device(x, wrap4(y + k), z, c) for k in range(1, 4)]
+    sb = Sums(gbs, 8, 1536, 4, scratch[:9])
+    sd = Sums(gds, 24, 1024, 1, scratch[9:18])
+    greet_all()
+    sends = []
+
+    def ring_send(n, k, src, dst):
+        sends.append(send(src, dst, ssem.at[n, k - 1], rsem.at[n, k - 1], ring[k - 1]))
+
+    def ring_wait(n, k, dst):
+        arrived(dst, rsem.at[n, k - 1], ring[0])
+
+    for k in (2, 1, 3, 0):
+        p = dot(att[wrap4(y + k)], wo[...], 1, 0)
+        if k:
+            part[k - 1] = p.astype(BF)
+            ring_send(0, k, part.at[k - 1], land1.at[k - 1])
+        else:
+            acc[...] = p + tok[...].astype(F32)
+    for r in range(4):
+        dhid[r] = dot(cot[r], wd[...], 1, 1)
+    for k in (1, 3, 2):
+        ring_wait(0, k, land1.at[k - 1])
+    total = acc[...]
+    for k in range(3):
+        total = total + land1[k].astype(F32)
+    acc[...] = total
+    scale = rms_scale(total)
+    unit[...] = total * scale
+    mid[y] = (total * scale * gain[...]).astype(BF)
+    for k in (2, 1, 3):
+        ring_send(1, k, mid.at[y], mid.at[y])
+
+    for k in (0, 1, 3, 2):
+        r = wrap4(y - k)
+        if k:
+            ring_wait(1, k, mid.at[r])
+        gu = dot(mid[r], wb[...], 1, 0)
+        gate, up = gu[:, :768], gu[:, 768:]
+        sig = 1.0 / (1.0 + jnp.exp(-gate))
+        act = gate * sig
+        dh = dhid[r]
+        hid[r] = (act * up).astype(BF)
+        dgu[r, :, :768] = (dh * up * sig * (1.0 + gate * (1.0 - sig))).astype(BF)
+        dgu[r, :, 768:] = (dh * act).astype(BF)
+        p = dot(dgu[r], wb[...], 1, 1)
+        if k:
+            dpart[k - 1] = p.astype(BF)
+            ring_send(2, 4 - k, dpart.at[k - 1], land2.at[3 - k])
+        else:
+            dmid[...] = p
+
+    for k in (1, 3, 2):
+        ring_wait(2, k, land2.at[k - 1])
+    total = dmid[...]
+    for k in range(3):
+        total = total + land2[k].astype(F32)
+    gffn[...] = jnp.sum(total * unit[...], axis=0, keepdims=True)
+    total = total * gain[...]
+    mean = jnp.mean(total * unit[...], axis=-1, keepdims=True)
+    total = cot[y].astype(F32) + rms_scale(acc[...]) * (total - unit[...] * mean)
+    dmid[...] = total
+    dbr[y] = total.astype(BF)
+    for k in (2, 1, 3):
+        ring_send(3, k, dbr.at[y], dbr.at[y])
+
+    def gate_up_rows(f, _):
+        cols = pl.ds(pl.multiple_of(f * 128, 128), 128)
+        rows = mid[:, :, cols].reshape(CHUNK, 128)
+        g = dot(rows, dgu[...].reshape(CHUNK, 1536), 0, 0)
+        gbs[pl.ds(f * 8, 8)] = g.reshape(8, 2, 8, 1536).astype(BF)
+        return 0
+
+    lax.fori_loop(0, 8, gate_up_rows, 0)
+    sb.start()
+
+    def down_rows(f, _):
+        cols = pl.ds(pl.multiple_of(f * 384, 384), 384)
+        rows = hid[:, :, cols].reshape(CHUNK, 384)
+        g = dot(rows, cot[...].reshape(CHUNK, 1024), 0, 0)
+        gds[pl.ds(f * 8, 8)] = g.reshape(8, 2, 24, 1024).astype(BF)
+        return 0
+
+    lax.fori_loop(0, 2, down_rows, 0)
+    sd.start()
+    for k in (2, 1, 3, 0):
+        p = dot(hid[wrap4(y + k)], wd[...], 1, 0)
+        if k:
+            opart[k - 1] = p.astype(BF)
+            ring_send(4, k, opart.at[k - 1], land3.at[k - 1])
+        else:
+            acc[...] = acc[...] + p
+    sb.cores()
+    sd.cores()
+    for k in (0, 1, 3, 2):
+        r = wrap4(y - k)
+        if k:
+            ring_wait(3, k, dbr.at[r])
+        datt[r] = dot(dbr[r], wo[...], 1, 1).astype(BF)
+
+    def out_rows(f, _):
+        cols = pl.ds(pl.multiple_of(f * 256, 256), 256)
+        rows = att[:, :, cols].reshape(CHUNK, 256)
+        g = dot(rows, dbr[...].reshape(CHUNK, 1024), 0, 0)
+        go[pl.ds(f * 8, 8)] = g.reshape(8, 2, 16, 1024).astype(BF)
+        return 0
+
+    lax.fori_loop(0, 2, out_rows, 0)
+    for k in (1, 3, 2):
+        ring_wait(4, k, land3.at[k - 1])
+    total = acc[...]
+    for k in range(3):
+        total = total + land3[k].astype(F32)
+    out[...] = total.astype(BF)
+    sb.second()
+    sd.second()
+    sb.first()
+    sd.first(od)
+    sb.owners()
+    for r in range(4):
+        for g in range(2):
+            h = g * 4 + r
+            og[:, h * 384 : h * 384 + 384] = sb.ry[r, :, g * 384 : g * 384 + 384].astype(F32)
+            ou[:, h * 384 : h * 384 + 384] = sb.ry[r, :, 768 + g * 384 : 1152 + g * 384].astype(F32)
+    sb.done()
+    sd.done()
+    for copy in sends:
+        copy.wait_send()
+
+
+def middle(att, tok, cot, wo, wb, wd, gain):
+    sds = jax.ShapeDtypeStruct
+    block = (128, 1024)
+    return pl.pallas_call(
+        middle_kernel,
+        out_shape=(
+            sds(block, BF),
+            sds(block, F32),
+            sds((4, 128, 512), BF),
+            sds((1, 1024), F32),
+            sds((16, 2, 16, 1024), BF),
             sds((8, 3072), F32),
             sds((8, 3072), F32),
-            sds((16, 1024), F32),
             sds((24, 1024), F32),
-            sds((8, 128), F32),
         ),
-        in_specs=[HBM] * 4,
+        in_specs=[VMEM] * 7,
         out_specs=(VMEM,) * 8,
-        scratch_shapes=scratch,
-        compiler_params=params(1),
-        name="grads_out",
-    )(ga, gb, go, gd)
+        scratch_shapes=[
+            pltpu.VMEM((3,) + block, BF),
+            pltpu.VMEM((3,) + block, BF),
+            pltpu.VMEM(block, F32),
+            pltpu.VMEM(block, F32),
+            pltpu.VMEM((4,) + block, BF),
+            pltpu.VMEM((4, 128, 768), F32),
+            pltpu.VMEM((4, 128, 1536), BF),
+            pltpu.VMEM((4, 128, 768), BF),
+            pltpu.VMEM((3,) + block, BF),
+            pltpu.VMEM((3,) + block, BF),
+            pltpu.VMEM((4,) + block, BF),
+            pltpu.VMEM((3,) + block, BF),
+            pltpu.VMEM((3,) + block, BF),
+            pltpu.VMEM((64, 2, 8, 1536), BF),
+            pltpu.VMEM((16, 2, 24, 1024), BF),
+            DMA((5, 3)),
+            DMA((5, 3)),
+        ]
+        + Sums.scratch(8, 1536, 4)
+        + Sums.scratch(24, 1024, 1),
+        compiler_params=params(3),
+        name="middle",
+    )(att, tok, cot, wo, wb, wd, gain)
 
 
 def rms_scale(rows):
@@ -513,7 +679,6 @@
     wb = wb.reshape(1024, 1536)
     wo = wo.reshape(512, 1024)
     wd = wd.reshape(768, 1024)
-    cot = cs.reshape(CHUNK, 1024)
     gains = wa[:, 1024:1028].astype(F32)
     attn_g, ffn_g = gains[:, 0], gains[:, 1]
     q_gain, k_gain = gains[::8, 2], gains[::8, 3]
@@ -561,27 +726,10 @@
     attended = jnp.einsum("kgqc,ckd->qkgd", probs, v_ext, preferred_element_type=F32)
     attended = attended.astype(BF).reshape(CHUNK, 512)
 
-    part = dot(attended, wo, 1, 0).astype(BF).reshape(4, 128, 1024)
     x_own = tokens.astype(F32)
-    mid_sum = x_own + ring_sum(part, 3)
-    scale_two = rms_scale(mid_sum)
-    mid_unit = mid_sum * scale_two
-    mid = ring_gather((mid_unit * ffn_g).astype(BF), 4).reshape(CHUNK, 1024)
-    gate_up = dot(mid, wb, 1, 0)
-    gate, up = gate_up[:, :768], gate_up[:, 768:]
-    sig = jax.nn.sigmoid(gate)
-    act = gate * sig
-    hidden = (act * up).astype(BF)
-    out_part = dot(hidden, wd, 1, 0).astype(BF).reshape(4, 128, 1024)
-    output = (mid_sum + ring_sum(out_part, 5)).astype(BF)
-    d_hidden = dot(cot, wd, 1, 1)
-    d_gate = (d_hidden * up * sig * (1.0 + gate * (1.0 - sig))).astype(BF)
-    d_up = (d_hidden * act).astype(BF)
-    d_gu = jnp.concatenate([d_gate, d_up], axis=1)
-    d_mid_normed = ring_sum(dot(d_gu, wb, 1, 1).astype(BF).reshape(4, 128, 1024), 6)
-    d_mid = cotangent.astype(F32) + norm_back(d_mid_normed, mid_unit, scale_two, ffn_g)
-    d_branch = ring_gather(d_mid.astype(BF), 7).reshape(CHUNK, 1024)
-    d_att = dot(d_branch, wo, 1, 1).astype(BF)
+    output, d_mid, d_att, g_ffn, go, og, ou, od = middle(
+        attended.reshape(4, 128, 512), tokens, cs, wo, wb, wd, ffn_g[None, :]
+    )
     d4 = d_att.reshape(CHUNK, 2, 2, HEAD_SIZE)
 
     d_v = jnp.einsum("kgqc,qkgd->ckd", probs, d4, preferred_element_type=F32)
@@ -613,11 +761,10 @@
     input_grad = (d_mid + norm_back(d_x_normed, unit_own, scale_own, attn_g)).astype(BF)
 
     g_attn = jnp.sum(d_x_normed * unit_own, axis=0)
-    g_ffn = jnp.sum(d_mid_normed * mid_unit, axis=0)
     g_gains = jnp.concatenate(
         [
             g_attn[:, None],
-            g_ffn[:, None],
+            g_ffn[0][:, None],
             jnp.repeat(g_qg, 8)[:, None],
             jnp.repeat(g_kg, 8)[:, None],
             jnp.zeros((1024, 124), F32),
@@ -625,15 +772,7 @@
         axis=1,
     ).astype(BF)
     ga = jnp.concatenate([dot(x_normed, d_qkv, 0, 0).astype(BF), g_gains], axis=1)
-    gb = dot(mid, d_gu, 0, 0).astype(BF)
-    go = dot(attended, d_branch, 0, 0).astype(BF)
-    gd = dot(hidden, cot, 0, 0).astype(BF)
-    oq, ok, ov, og, ou, oo, od, ogain = grads_out(
-        ga.reshape(64, 2, 8, 1152),
-        gb.reshape(64, 2, 8, 1536),
-        go.reshape(16, 2, 16, 1024),
-        gd.reshape(16, 2, 24, 1024),
-    )
+    oq, ok, ov, oo, ogain = grads_out(ga.reshape(64, 2, 8, 1152), go)
     return (
         output,
         input_grad,

time: 410 us -> 358 us (0.87)
  the two profiles are of different devices: /device:TPU:1 before, /device:TPU:0 now
where the time goes in v2:
time: 358 us; the launch traced here: 351 us
  Pallas kernels  223 us (62%)
  local copies, waits for them, and re-layouts  48.2 us (13%)
  matrix products  42.9 us (12%)
  other arithmetic  34.4 us (10%)
    pallas_call x1, Pallas kernels, middle(): pl.pallas_call(middle_kernel, out_shape=(sds(block, BF), sds(block, F32),...  92.1 us
    pallas_call x1, Pallas kernels, gather_all(): pl.pallas_call(gather_kernel, out_shape=(sds((4, 128, 1024), BF), sds((4,...  46.4 us
    pallas_call x1, Pallas kernels, grads_out(): pl.pallas_call(grads_kernel, out_shape=(sds((8, 2048), F32), sds((8, 1024...  28.3 us
    pallas_call x1, Pallas kernels, halo_back(): pl.pallas_call(halo_back_kernel, out_shape=jax.ShapeDtypeStruct(dkv.shape...  23.3 us
    pallas_call x1, Pallas kernels, halo(): pl.pallas_call(halo_kernel, out_shape=jax.ShapeDtypeStruct((3,) + kv.shap...  19.9 us
    pallas_call x1, Pallas kernels, ring_sum(): pl.pallas_call(ring_sum_kernel, out_shape=jax.ShapeDtypeStruct((rows, col...  12.9 us
    unnamed x54, local copies, waits for them, and re-layouts  12.2 us
    sub x1, matrix products, local(): weight = jnp.exp(scores - peak)  11.1 us

profile of v2, /device:TPU:0, one launch (start us, length us, event | category | flops | bytes accessed | tf_op | source)
XLA Modules:
  0.0 351.2 jit_solution(10103943960666251420)
XLA Ops:
  1.4 1.2 multiply_subtract_fusion
  6.0 46.4 %gather_all.1 = (bf16[4,128,1024]{2,1,0:T(8,128)(2,1)}, bf16[4,128,1024]{2,1,0:T(8,128)(2,1)}, bf16[2,4,16,8,1152]{4,3,2,1,0:T(8,128)(2,1)}, bf16[2,4,16,8,1536]...) custom-call(bf16[128,1024]{1,0:T(8,128)(2,1)} %tok.3, ...), custom_call_target="tpu_custom_call" | custom-call | tf_op jit(solution)/shard_map/gather_all/pallas_call | solution.py:197
  52.4 1.1 slice.90
  53.7 1.5 multiply_reduce_fusion
  55.2 1.5 fusion.26
  56.8 1.3 fusion.29
  58.1 1.3 copy-done.3
  60.6 1.2 fusion.46
  66.4 1.2 fusion.59
  68.5 19.9 %halo.1 = bf16[3,512,512]{2,1,0:T(8,128)(2,1)} custom-call(bf16[512,512]{1,0:T(8,128)(2,1)} %pad_maximum_fusion.2.kv), custom_call_target="tpu_custom_call" | custom-call | tf_op jit(solution)/shard_map/halo/pallas_call | solution.py:273
  88.5 2.4 fusion.68
  90.8 2.3 copy.187
  93.8 1.7 fusion.12
  95.5 11.1 %fusion.72 = (f32[2,2,512]{2,1,0:T(2,128)S(1)}, f32[2,2,512,1536]{2,3,1,0:T(8,128)}) fusion(pred[512,1536]{0,1:T(8,128)(4,1)} %fusion.12, bf16[1536,2,128,1]{0,2,3,1:T(8,128)(2,1)} %bitcast.154, bf16[512,2,2,128]{0,3,2,1:T(8,128)(2,1)} %fusion.46), kind=kOutput, calls=%fused_computation.121 | convolution fusion | flops 817890816 | bytes 14688256 | tf_op jit(solution)/shard_map/sub | solution.py:722
  106.6 1.2 copy.147
  107.8 6.7 %fusion.41 = bf16[512,2,2,128]{0,3,2,1:T(8,128)(2,1)} fusion(bf16[1536,2,128,1]{0,2,3,1:T(8,128)(2,1)} %bitcast.164, f32[2,2,512,1536]{2,3,1,0:T(8,128)} %get-tuple-element.78, f32[2,2,512]{2,1,0:T(2,128)S(1)} %get-tuple-element.77), kind=kOutput, calls=%fused_computation.45 | convolution fusion | flops 811859968 | bytes 13901824 | tf_op jit(solution)/shard_map/kgqc,ckd->qkgd/dot_general | solution.py:726
  114.5 1.2 reshape.278
  115.6 1.1 copy.182.att
  117.4 92.1 %middle.1 = (bf16[128,1024]{1,0:T(8,128)(2,1)}, f32[128,1024]{1,0:T(8,128)}, bf16[4,128,512]{2,1,0:T(8,128)(2,1)}, f32[1,1024]{1,0:T(1,128)}, bf16[16,2,16,1024]...) custom-call(bf16[4,128,512]{2,1,0:T(8,128)(2,1)} %copy.182.att, ...), custom_call_target="tpu_custom_call" | custom-call | tf_op jit(solution)/shard_map/middle/pallas_call | solution.py:588
  209.5 1.2 reshape.257
  210.6 1.4 copy.160
  212.1 6.9 %fusion.1 = (f32[2,2,512]{2,1,0:T(2,128)S(1)}, f32[2,1536,512,2]{2,1,3,0:T(8,128)S(1)}) fusion(f32[2,2,512,1536]{2,3,1,0:T(8,128)} %get-tuple-element.78, f32[2,2,512]{2,1,0:T(2,128)S(1)} %get-tuple-element.77, bf16[1536,2,128,1]{0,2,3,1:T(8,128)(2,1)} %bitcast.165, bf16[512,2,2,128]{0,3,2,1:T(8,128)(2,1)} %copy.160), kind=kOutput, calls=%fused_computation.3 | convolution fusion | flops 814741504 | bytes 26492928 | tf_op jit(solution)/shard_map/qkgd,ckd->kgqc/dot_general | solution.py:736
  219.0 7.2 %fusion.3 = bf16[2,2,512,1536]{2,3,1,0:T(8,128)(2,1)S(1)} fusion(f32[2,1536,512,2]{2,1,3,0:T(8,128)S(1)} %get-tuple-element.80, f32[2,2,512]{2,1,0:T(2,128)S(1)} %get-tuple-element.79, f32[2,2,512,1536]{2,3,1,0:T(8,128)} %get-tuple-element.78, f32[2,2,512]{2,1,0:T(2,128)S(1)} %get-tuple-element.77), kind=kLoop, calls=%fused_computation.5 | loop fusion | flops 12582912 | bytes 31473664 | tf_op jit(solution)/shard_map/convert_element_type | solution.py:738
  226.1 1.0 fusion.40
  227.9 1.1 fusion.44
  229.0 2.1 fusion.21
  232.3 7.7 %fusion.22 = bf16[1536,2,128]{0,2,1:T(8,128)(2,1)} fusion(bf16[512,2,2,128]{0,3,2,1:T(8,128)(2,1)S(1)} %copy-done.11, f32[2,2,512,1536]{2,3,1,0:T(8,128)} %get-tuple-element.78, f32[2,2,512]{2,1,0:T(2,128)S(1)} %get-tuple-element.77), kind=kOutput, calls=%fused_computation.27 | convolution fusion | flops 811991040 | bytes 13901824 | tf_op jit(solution)/shard_map/kgqc,qkgd->ckd/dot_general | solution.py:735
  240.0 2.2 copy.162
  242.3 1.4 concatenate.46
  243.7 2.4 pad_maximum_fusion.dkv
  246.1 23.3 %halo_back.1 = f32[512,512]{1,0:T(8,128)} custom-call(bf16[3,512,512]{2,1,0:T(8,128)(2,1)} %pad_maximum_fusion.dkv), custom_call_target="tpu_custom_call" | custom-call | tf_op jit(solution)/shard_map/halo_back/pallas_call | solution.py:294
  269.5 1.3 convert_element_type.88
  272.9 2.8 multiply_reduce_fusion.4
  275.7 1.1 copy.163
  276.9 1.8 fusion.58
  279.1 3.8 %convolution_convert_fusion = bf16[1024,1024]{0,1:T(8,128)(2,1)} fusion(bf16[512,1024]{1,0:T(8,128)(2,1)S(1)} %copy-done.9, bf16[512,256]{0,1:T(8,128)(2,1)S(1)} %copy.166, bf16[512,256]{0,1:T(8,128)(2,1)S(1)} %bitcast.168, bf16[512,512]{0,1:T(8,128)(2,1)} %bitcast.166), kind=kOutput, calls=%fused_computation.32 | convolution fusion | flops 1077936128 | bytes 4194304 | tf_op jit(solution)/shard_map/dot_general | solution.py:656
  282.9 2.3 fusion.31
  285.2 12.9 %ring_sum.1 = f32[128,1024]{1,0:T(8,128)} custom-call(bf16[4,128,1024]{2,1,0:T(8,128)(2,1)} %bitcast.163), custom_call_target="tpu_custom_call" | custom-call | tf_op jit(solution)/shard_map/ring_sum/pallas_call | solution.py:244
  298.3 1.3 fusion.56
  300.0 7.9 %concatenate.49 = bf16[1024,1152]{0,1:T(8,128)(2,1)S(1)} concatenate(bf16[1024,1024]{0,1:T(8,128)(2,1)} %convolution_convert_fusion, bf16[1024,1]{0,1:T(2,128)(2,1)S(1)} %broadcast_in_dim.84, bf16[1024,1]{0,1:T(2,128)(2,1)S(1)} %convert_bitcast_fusion, bf16[1024,1]{0,1:T(2,128)(2,1)S(1)} %broadcast_in_dim_reshape.8, bf16[1024,1]{0,1:T(2,128)(2,1)S(1)} %broadcast_in_dim_reshape.9, ...), dimensions={1} | concatenate | bytes 4718592 | tf_op jit(solution)/shard_map/concatenate | solution.py:774
  308.0 2.6 copy.167
  310.6 28.3 %grads_out.1 = (f32[8,2048]{1,0:T(8,128)}, f32[8,1024]{1,0:T(8,128)}, f32[8,1024]{1,0:T(8,128)}, f32[16,1024]{1,0:T(8,128)}, f32[8,128]{1,0:T(8,128)}) custom-call(bf16[64,2,8,1152]{3,2,1,0:T(8,128)(2,1)} %bitcast.151, bf16[16,2,16,1024]{3,2,1,0:T(8,128)(2,1)} %get-tuple-element.42.go), custom_call_target="tpu_custom_call" | custom-call | tf_op jit(solution)/shard_map/grads_out/pallas_call | solution.py:431
  338.9 1.3 fusion.71
  340.2 1.5 slice_reduce_fusion
  343.4 1.5 copy.205
  344.8 1.4 copy.206
  346.2 1.4 copy.207
  347.6 1.5 copy.208
  (114 shorter events, 19.4 us)
Async XLA Ops:
  52.4 4.3 %copy-start.19 = (bf16[2,4,16,8,1152]{4,3,2,1,0:T(8,128)(2,1)S(1)}, bf16[2,4,16,8,1152]{4,3,2,1,0:T(8,128)(2,1)}, u32[]{:S(2)}) copy-start(bf16[2,4,16,8,1152]{4,3,2,1,0:T(8,128)(2,1)} %get-tuple-element.33) | copy-start | bytes 7077892
  56.8 1.3 copy-start.8
  58.1 1.4 copy-start.3
  60.4 1.5 slice-start
  65.6 22.8 %copy-start.5 = (f32[512,128]{1,0:T(8,128)}, f32[512,128]{1,0:T(8,128)S(1)}, u32[]{:S(2)}) copy-start(f32[512,128]{1,0:T(8,128)S(1)} %copy.145) | copy-start | bytes 786436
  65.6 2.0 copy-start.4
  68.5 24.6 %copy-start.15 = (s32[16384]{0:T(1024)S(1)}, s32[16384]{0:T(1024)}, u32[]{:S(2)}) copy-start(s32[16384]{0:T(1024)} %param.20) | copy-start | bytes 196612
  218.9 7.2 %copy-start.2 = (bf16[1536,256]{0,1:T(8,128)(2,1)S(1)}, bf16[1536,256]{0,1:T(8,128)(2,1)}, u32[]{:S(2)}) copy-start(bf16[1536,256]{0,1:T(8,128)(2,1)} %copy.187) | copy-start | bytes 2359300
  227.4 1.6 copy-start.7
  231.1 1.1 copy-start.11
  270.7 2.1 copy-start.6
  272.8 6.1 %copy-start.10 = (bf16[512,256]{1,0:T(8,128)(2,1)S(1)}, bf16[512,256]{1,0:T(8,128)(2,1)}, u32[]{:S(2)}) copy-start(bf16[512,256]{1,0:T(8,128)(2,1)} %get-tuple-element.72) | copy-start | bytes 786436
  272.9 6.2 %copy-start.9 = (bf16[512,1024]{1,0:T(8,128)(2,1)S(1)}, bf16[512,1024]{1,0:T(8,128)(2,1)}, u32[]{:S(2)}) copy-start(bf16[512,1024]{1,0:T(8,128)(2,1)} %copy-done.8) | copy-start | bytes 3145732
  279.1 3.8 %copy-start.13 = (bf16[512,4,128]{0,2,1:T(8,128)(2,1)S(1)}, bf16[512,4,128]{0,2,1:T(8,128)(2,1)}, u32[]{:S(2)}) copy-start(bf16[512,4,128]{0,2,1:T(8,128)(2,1)} %fusion.44) | copy-start | bytes 1572868
  279.1 3.8 %copy-start.20 = (bf16[2,4,16,8,1152]{4,3,2,1,0:T(8,128)(2,1)S(1)}, bf16[2,4,16,8,1152]{4,3,2,1,0:T(8,128)(2,1)}, u32[]{:S(2)}) copy-start(bf16[2,4,16,8,1152]{4,3,2,1,0:T(8,128)(2,1)} %get-tuple-element.33) | copy-start | bytes 7077892
  282.9 15.2 %copy-start = (bf16[128,1024]{1,0:T(8,128)(2,1)S(1)}, bf16[128,1024]{1,0:T(8,128)(2,1)}, u32[]{:S(2)}) copy-start(bf16[128,1024]{1,0:T(8,128)(2,1)} %tok.3) | copy-start | bytes 786436
  282.9 17.1 %copy-start.21 = (f32[1,1024]{1,0:T(1,128)S(1)}, f32[1,1024]{1,0:T(1,128)}, u32[]{:S(2)}) copy-start(f32[1,1024]{1,0:T(1,128)} %get-tuple-element.41) | copy-start | bytes 12292
  308.0 33.7 %copy-start.1 = (f32[128,1024]{1,0:T(8,128)S(1)}, f32[128,1024]{1,0:T(8,128)}, u32[]{:S(2)}) copy-start(f32[128,1024]{1,0:T(8,128)} %ring_sum.1) | copy-start | bytes 1572868
  310.6 31.2 %copy-start.12 = (f32[128,1024]{1,0:T(8,128)S(1)}, f32[128,1024]{1,0:T(8,128)}, u32[]{:S(2)}) copy-start(f32[128,1024]{1,0:T(8,128)} %get-tuple-element.39) | copy-start | bytes 1572868
  310.6 32.1 %copy-start.14 = (bf16[128,1024]{1,0:T(8,128)(2,1)S(1)}, bf16[128,1024]{1,0:T(8,128)(2,1)}, u32[]{:S(2)}) copy-start(bf16[128,1024]{1,0:T(8,128)(2,1)} %get-tuple-element.98) | copy-start | bytes 786436
  310.6 38.5 %copy-start.18 = (f32[8,3072]{1,0:T(8,128)S(1)}, f32[8,3072]{1,0:T(8,128)}, u32[]{:S(2)}) copy-start(f32[8,3072]{1,0:T(8,128)} %get-tuple-element.108) | copy-start | bytes 294916
  310.6 39.1 %copy-start.17 = (f32[8,3072]{1,0:T(8,128)S(1)}, f32[8,3072]{1,0:T(8,128)}, u32[]{:S(2)}) copy-start(f32[8,3072]{1,0:T(8,128)} %get-tuple-element.109) | copy-start | bytes 294916
  310.6 39.8 %copy-start.16 = (f32[24,1024]{1,0:T(8,128)S(1)}, f32[24,1024]{1,0:T(8,128)}, u32[]{:S(2)}) copy-start(f32[24,1024]{1,0:T(8,128)} %get-tuple-element.110) | copy-start | bytes 294916

commit v3 on v2

v3 whole, which is shorter than its diff:
```python
import math

import jax
import jax.numpy as jnp
import numpy as np
from jax import lax
from jax.experimental import pallas as pl
from jax.experimental.pallas import tpu as pltpu
from jax.sharding import PartitionSpec as P

HEAD_SIZE = 128
SPAN = 1024
CHUNK = 512
EPS = 1e-06
ROPE_BASE = 1000000.0
MASKED = -1e30
MESH = pl.DeviceIdType.MESH
BF = jnp.bfloat16
F32 = jnp.float32
VMEM = pl.BlockSpec(memory_space=pltpu.VMEM)
HBM = pl.BlockSpec(memory_space=pl.ANY)
DMA = pltpu.SemaphoreType.DMA
VMEM_LIMIT = 58 * 2**20


def coords():
    h = lax.axis_index("head")
    b = lax.axis_index("blk")
    x = 2 * lax.div(h, 4) + lax.div(b, 8)
    return x, lax.rem(h, 4), lax.rem(lax.div(b, 2), 4), lax.rem(b, 2)


def device(x, y, z, c):
    return (lax.div(x, 2) * 4 + y, lax.rem(x, 2) * 8 + z * 2 + c)


def wrap4(v):
    return lax.rem(v + 8, 4)


def send(src, dst, send_sem, recv_sem, to):
    copy = pltpu.make_async_remote_copy(
        src_ref=src, dst_ref=dst, send_sem=send_sem, recv_sem=recv_sem, device_id=to, device_id_type=MESH
    )
    copy.start()
    return copy


def arrived(dst, sem, anyone):
    pltpu.make_async_remote_copy(
        src_ref=dst, dst_ref=dst, send_sem=sem, recv_sem=sem, device_id=anyone, device_id_type=MESH
    ).wait_recv()


def meet(peers):
    barrier = pltpu.get_barrier_semaphore()
    for peer in peers:
        pl.semaphore_signal(barrier, inc=1, device_id=peer, device_id_type=MESH)
    pl.semaphore_wait(barrier, len(peers))


def params(collective_id):
    return pltpu.CompilerParams(
        collective_id=collective_id, has_side_effects=True, vmem_limit_bytes=VMEM_LIMIT
    )


def chunk_number():
    return 2 * lax.axis_index("blk") + lax.div(lax.axis_index("head"), 4)


def chunk_device(step):
    chunk = lax.rem(chunk_number() + step + 32, 32)
    return (lax.rem(chunk, 2) * 4 + lax.rem(lax.axis_index("head"), 4), lax.div(chunk, 2))


def greet_all(chunks=False):
    x, y, z, c = coords()
    peers = [device(x, wrap4(y + k), z, c) for k in range(1, 4)]
    peers += [device(wrap4(x + k), y, z, c) for k in range(1, 4)]
    peers += [device(x, y, wrap4(z + k), c) for k in range(1, 4)]
    peers += [device(x, y, z, 1 - c)]
    if chunks:
        peers += [chunk_device(s) for s in (-2, -1, 1, 2)]
    meet(peers)


def dot(a, b, ca, cb):
    return lax.dot_general(a, b, (((ca,), (cb,)), ((), ())), preferred_element_type=F32)


def rms_scale(rows):
    return lax.rsqrt(jnp.mean(rows * rows, axis=-1, keepdims=True) + EPS)


def rope_tables():
    freq = ROPE_BASE ** (-np.arange(0, HEAD_SIZE, 2, dtype=np.float64) / HEAD_SIZE)
    freq = np.concatenate([freq, freq])
    sign = np.where(np.arange(HEAD_SIZE) < 64, -1.0, 1.0)
    inner = np.arange(CHUNK)[:, None] * freq[None, :]
    outer = (np.arange(32) * CHUNK)[:, None] * freq[None, :]
    tables = [f(a) * s for a in (inner, outer) for f, s in ((np.cos, 1.0), (np.sin, sign))]
    return [jnp.asarray(t.astype(np.float32)) for t in tables]


def rope_here(ic, isn, oc, osn, cos, sin):
    n = chunk_number()
    c0, s0 = oc[pl.ds(n, 1), :], osn[pl.ds(n, 1), :]
    cos[...] = c0 * ic[...] - s0 * isn[...]
    sin[...] = s0 * ic[...] + c0 * isn[...]


def rope(rows, cos, sin):
    return rows * cos + pltpu.roll(rows, 64, 1) * sin


def rope_back(rows, cos, sin):
    return rows * cos + pltpu.roll(rows * sin, 64, 1)


def prep_back(d, raw, gain, cos, sin):
    scale = rms_scale(raw)
    unit = raw * scale
    d = rope_back(d, cos, sin)
    d_gain = jnp.sum(d * unit, axis=0, keepdims=True)
    d = d * gain
    return scale * (d - unit * jnp.mean(d * unit, axis=-1, keepdims=True)), d_gain


REACH = (((0, 512), (256, 256)), ((0, 512), (0, 512)), ((0, 256), (0, 512)))
EXP_SCALE = HEAD_SIZE ** (-0.5) * math.log2(math.e)


def allowed(low, slot, t):
    first, count = REACH[slot][t]
    place = lax.broadcasted_iota(jnp.int32, (count, 512), 0) + (slot * CHUNK + first)
    ok = place >= low[t]
    if slot == 2:
        query = lax.rem(lax.broadcasted_iota(jnp.int32, (1, 512), 1), 256) + (t * 256 + SPAN)
        ok = ok & (place <= query)
    return ok


def attend(q, kvx, low, peak, total, acc, slot, fresh):
    def group(g, _):
        for t in range(2):
            first, count = REACH[slot][t]
            keys = kvx[g, slot, first : first + count]
            values = kvx[2 + g, slot, first : first + count]
            s = dot(keys, q[g, t], 1, 1)
            s = jnp.where(allowed(low, slot, t), s, MASKED)
            top = jnp.max(s, axis=0, keepdims=True)
            if not fresh:
                before = peak[g, t]
                top = jnp.maximum(top, before)
                fade = jnp.exp2((before - top) * EXP_SCALE)
            p = jnp.exp2((s - top) * EXP_SCALE)
            add = jnp.sum(p, axis=0, keepdims=True)
            o = dot(values, p.astype(BF), 0, 0)
            if not fresh:
                add = add + total[g, t] * fade
                o = o + acc[g, t] * fade
            peak[g, t] = top
            total[g, t] = add
            acc[g, t] = o
        return 0

    lax.fori_loop(0, 2, group, 0)


def attend_back(q, kvx, low, lse, do, inner, dq, dkv, slot, fresh):
    def group(g, _):
        for t in range(2):
            first, count = REACH[slot][t]
            rows = slice(first, first + count)
            keys = kvx[g, slot, rows]
            values = kvx[2 + g, slot, rows]
            s = dot(keys, q[g, t], 1, 1)
            p = jnp.where(allowed(low, slot, t), jnp.exp2(s * EXP_SCALE - lse[g, t]), 0.0)
            dp = dot(values, do[g, t], 1, 1)
            ds = (p * (dp - inner[g, t])).astype(BF)
            dv = dot(p.astype(BF), do[g, t], 1, 0)
            dk = dot(ds, q[g, t], 1, 0)
            whole = count == CHUNK
            if whole and (t == 0 or slot == 2):
                other = slice(0, 256)
                if t == 0:
                    dkv[g, slot] = dk
                    dkv[2 + g, slot] = dv
                else:
                    dkv[g, slot, other] = dkv[g, slot, other] + dk[other]
                    dkv[2 + g, slot, other] = dkv[2 + g, slot, other] + dv[other]
                    dkv[g, slot, 256:] = dk[256:]
                    dkv[2 + g, slot, 256:] = dv[256:]
            elif t == 0:
                dkv[g, slot, rows] = dk
                dkv[2 + g, slot, rows] = dv
            else:
                dkv[g, slot, rows] = dkv[g, slot, rows] + dk
                dkv[2 + g, slot, rows] = dkv[2 + g, slot, rows] + dv
            d = dot(keys, ds, 0, 0)
            dq[g, t] = d if fresh else dq[g, t] + d
        return 0

    lax.fori_loop(0, 2, group, 0)


class Pieces:
    def __init__(self, ref, wide, ssem, rsem):
        self.ref, self.wide, self.ssem, self.rsem = ref, wide, ssem, rsem
        self.x, self.y, self.z, self.c = x, y, z, c = coords()
        self.d = 1 - c
        self.across = device(x, y, z, 1 - c)
        self.ring = [device(x, wrap4(y + k), z, c) for k in range(1, 4)]
        self.sends = []

    @staticmethod
    def semaphores():
        return [DMA((34,)), DMA((34,))]

    def slot(self, px, pz, core):
        b = lax.rem(px, 2) * 8 + pz * 2 + core
        if self.wide:
            return self.ref.at[lax.div(px, 2), :, b]
        return self.ref.at[lax.div(px, 2), b]

    def piece(self, j, k):
        c, d = self.c, self.d
        return self.slot(wrap4(self.x - j * d - k * c), wrap4(self.z - j * c - k * d), c)

    def piece_across(self, j, k):
        c, d = self.c, self.d
        return self.slot(wrap4(self.x - j * c - k * d), wrap4(self.z - j * d - k * c), d)

    def send(self, src, dst, n, to):
        self.sends.append(send(src, dst, self.ssem.at[n], self.rsem.at[n], to))

    def first(self, k):
        return device(wrap4(self.x + k * self.d), self.y, wrap4(self.z + k * self.c), self.c)

    def second(self, k):
        return device(wrap4(self.x + k * self.c), self.y, wrap4(self.z + k * self.d), self.c)

    def to_ring(self, parts):
        self.b = lax.rem(self.x, 2) * 8 + self.z * 2 + self.c
        xh = lax.div(self.x, 2)
        self.at_ring = lambda r: self.ref.at[xh, r, self.b]
        for k in range(1, 4):
            self.send(parts.at[wrap4(self.y + k)], self.at_ring(self.y), 30 + k, self.ring[k - 1])
        self.ref[xh, self.y, self.b] = parts[self.y]

    def from_ring(self):
        for k in range(1, 4):
            arrived(self.at_ring(wrap4(self.y - k)), self.rsem.at[30 + k], self.across)

    def own(self, src=None):
        src = self.piece(0, 0) if src is None else src
        for k in (2, 1, 3):
            self.send(src, self.piece(0, 0), k - 1, self.first(k))
        for k in (2, 1, 3):
            self.send(src, self.piece(0, 0), 2 + k, self.second(k))
        self.send(src, self.piece(0, 0), 15, self.across)

    def pass_on(self, j):
        here = self.piece(j, 0)
        arrived(here, self.rsem.at[j - 1], self.across)
        for k in (2, 1, 3):
            self.send(here, here, 2 + 3 * j + k, self.second(k))
        self.send(here, here, 15 + 4 * j, self.across)

    def pass_across(self, j, k):
        here = self.piece(j, k)
        arrived(here, self.rsem.at[2 + 3 * j + k], self.across)
        self.send(here, here, 15 + 4 * j + k, self.across)

    def pass_all_on(self):
        for j in (1, 3, 2):
            self.pass_on(j)

    def pass_all_across(self):
        for j in (0, 1, 3, 2):
            for k in (1, 3, 2):
                self.pass_across(j, k)

    def all_here(self):
        for j in range(4):
            for k in range(4):
                arrived(self.piece_across(j, k), self.rsem.at[15 + 4 * j + k], self.across)

    def done(self):
        for copy in self.sends:
            copy.wait_send()


def pack_wide(src, dst):
    cols = src.shape[-1]

    def rows(i, _):
        part = src[lax.div(i, 4), lax.rem(i, 4)].astype(F32).reshape(128, cols)
        dst[pl.ds(pl.multiple_of(i * 128, 128), 128)] = part.astype(BF)
        return 0

    lax.fori_loop(0, 8, rows, 0)


def pack_down(src, dst):
    def rows(i, _):
        part = src[lax.div(i, 4), pl.ds(lax.rem(i, 4) * 4, 4)].astype(F32).reshape(96, 1024)
        dst[pl.ds(pl.multiple_of(i * 96, 96), 96)] = part.astype(BF)
        return 0

    lax.fori_loop(0, 8, rows, 0)


def front_kernel(
    tok, cot, wq, wk, wv, gains, wo, low, ic, isn, oc, osn,
    att, cs, wof, wa, rows, xn, q, kvx, lse,
    sa, wal, xs, cos, sin, peak, total, acc, ssem, rsem, lsem, *sems,
):
    x, y, z, c = coords()
    ring = [device(x, wrap4(y + k), z, c) for k in range(1, 4)]
    for r in range(4):
        for g in range(2):
            h = g * 4 + r
            sa[r, :, g * 256 : g * 256 + 256] = wq[:, h * 256 : h * 256 + 256]
            sa[r, :, 512 + g * 128 : 640 + g * 128] = wk[:, h * 128 : h * 128 + 128]
            sa[r, :, 768 + g * 128 : 896 + g * 128] = wv[:, h * 128 : h * 128 + 128]
        sa[r, :, 1024:1152] = gains[...]
    a = Pieces(wal, True, *sems[:2])
    o = Pieces(wof, False, *sems[2:4])
    greet_all(True)
    sends = []

    def ring_send(n, k, src, dst):
        sends.append(send(src, dst, ssem.at[n, k - 1], rsem.at[n, k - 1], ring[k - 1]))

    a.to_ring(sa)
    for k in (2, 1, 3):
        ring_send(0, k, tok, xs.at[y])
    own_o = pltpu.make_async_copy(wo, o.piece(0, 0), lsem.at[0])
    own_o.start()
    own_c = pltpu.make_async_copy(cot, cs.at[y], lsem.at[1])
    own_c.start()
    xs[y] = tok[...]
    rope_here(ic, isn, oc, osn, cos, sin)
    a.from_ring()
    a.own()
    a.pass_all_on()
    o.own(wo)
    for k in (1, 3, 2):
        arrived(xs.at[wrap4(y - k)], rsem.at[0, k - 1], ring[0])
    for k in (2, 1, 3):
        ring_send(1, k, cot, cs.at[y])
    a.pass_all_across()
    o.pass_all_on()
    a.all_here()
    pack_wide(wal, wa)

    pick = lax.broadcasted_iota(jnp.int32, (8, 128), 0) == lax.broadcasted_iota(jnp.int32, (8, 128), 1)
    by_row = dot(pick.astype(F32).astype(BF), wa[:, 1024:1152], 1, 1)
    rows[:, :1024] = by_row
    every = lax.broadcasted_iota(jnp.int32, (1024, 128), 0) == 8 * lax.broadcasted_iota(jnp.int32, (1024, 128), 1)
    rows[:, 1024:] = dot(by_row.astype(BF), every.astype(F32).astype(BF), 1, 0)
    q_gain, k_gain = rows[2:3, 1024:], rows[3:4, 1024:]
    for r in range(4):
        block = xs[r].astype(F32)
        xn[r * 128 : r * 128 + 128] = (block * rms_scale(block) * rows[0:1, :1024]).astype(BF)

    raw = dot(xn[...], wa[:, 512:768], 1, 0)
    for g in range(2):
        k_raw = raw[:, g * 128 : g * 128 + 128]
        kvx[g, 2] = rope(k_raw * rms_scale(k_raw) * k_gain, cos[...], sin[...]).astype(BF)
    raw = dot(xn[...], wa[:, 768:1024], 1, 0)
    for g in range(2):
        kvx[2 + g, 2] = raw[:, g * 128 : g * 128 + 128].astype(BF)
    near = send(kvx.at[:, 2], kvx.at[:, 1], ssem.at[2, 0], rsem.at[2, 0], chunk_device(1))
    far = send(kvx.at[:, 2], kvx.at[:, 0], ssem.at[2, 1], rsem.at[2, 1], chunk_device(2))

    def queries(g, _):
        raw = dot(xn[...], wa[:, pl.ds(pl.multiple_of(g * 256, 256), 256)], 1, 0)
        for hd in range(2):
            q_raw = raw[:, hd * 128 : hd * 128 + 128]
            rot = rope(q_raw * rms_scale(q_raw) * q_gain, cos[...], sin[...]).astype(BF)
            for t in range(2):
                q[g, t, hd * 256 : hd * 256 + 256] = rot[t * 256 : t * 256 + 256]
        return 0

    lax.fori_loop(0, 2, queries, 0)
    attend(q, kvx, low, peak, total, acc, 2, True)
    o.pass_all_across()
    near.wait_recv()
    attend(q, kvx, low, peak, total, acc, 1, False)
    far.wait_recv()
    attend(q, kvx, low, peak, total, acc, 0, False)
    for g in range(2):
        for t in range(2):
            done = jnp.transpose(acc[g, t] / total[g, t]).astype(BF)
            lse[g, t] = peak[g, t] * EXP_SCALE + jnp.log(total[g, t]) * math.log2(math.e)
            for hd in range(2):
                cols = slice((g * 2 + hd) * 128, (g * 2 + hd) * 128 + 128)
                for half in range(2):
                    first = hd * 256 + half * 128
                    att[2 * t + half, :, cols] = done[first : first + 128]
    for k in (1, 3, 2):
        arrived(cs.at[wrap4(y - k)], rsem.at[1, k - 1], ring[0])
    o.all_here()
    own_o.wait()
    own_c.wait()
    for copy in sends + [near, far]:
        copy.wait_send()
    a.done()
    o.done()


def front(tok, cot, wq, wk, wv, gains, wo, low):
    sds = jax.ShapeDtypeStruct
    return pl.pallas_call(
        front_kernel,
        out_shape=(
            sds((4, 128, 512), BF),
            sds((4, 128, 1024), BF),
            sds((2, 16, 16, 1024), BF),
            sds((1024, 1152), BF),
            sds((8, 1152), F32),
            sds((CHUNK, 1024), BF),
            sds((2, 2, 512, 128), BF),
            sds((4, 3, CHUNK, 128), BF),
            sds((2, 2, 1, 512), F32),
        ),
        in_specs=[VMEM, HBM] + [VMEM] * 4 + [HBM] + [VMEM] * 5,
        out_specs=(VMEM, HBM, HBM) + (VMEM,) * 6,
        scratch_shapes=[
            pltpu.VMEM((4, 8, 1152), BF),
            pltpu.VMEM((2, 4, 16, 8, 1152), BF),
            pltpu.VMEM((4, 128, 1024), BF),
            pltpu.VMEM((CHUNK, 128), F32),
            pltpu.VMEM((CHUNK, 128), F32),
            pltpu.VMEM((2, 2, 1, 512), F32),
            pltpu.VMEM((2, 2, 1, 512), F32),
            pltpu.VMEM((2, 2, 128, 512), F32),
            DMA((3, 3)),
            DMA((3, 3)),
            DMA((2,)),
        ]
        + Pieces.semaphores() * 2,
        compiler_params=params(0),
        name="front",
    )(tok, cot, wq, wk, wv, gains, wo, low, *rope_tables())


class Sums:
    def __init__(self, grad, rows, cols, cut, refs):
        self.grad, self.rows, self.cols, self.cut = grad, rows, cols, cut
        (self.rc, self.sa, self.lb, self.sb, self.l2, self.sd, self.ry, self.ss, self.rs) = refs
        x, y, z, c = coords()
        self.y, self.c, self.d = y, c, 1 - c
        d = self.d
        self.across = device(x, y, z, d)
        self.ring = [device(x, wrap4(y + k), z, c) for k in range(1, 4)]
        self.to_first = [device(wrap4(x + k * d), y, wrap4(z + k * c), c) for k in range(1, 4)]
        self.to_second = [device(wrap4(x + k * c), y, wrap4(z + k * d), c) for k in range(1, 4)]
        self.p1 = x * d + z * c
        self.p2 = x * c + z * d
        self.sends = []

    @staticmethod
    def scratch(rows, cols, cut):
        buffers = [(16 * cut,), (4, 4, cut), (3, 4, cut), (4, cut), (3, cut), (cut,), (cut,)]
        return [pltpu.VMEM(lead + (rows, cols), BF) for lead in buffers] + [DMA((10,)), DMA((10,))]

    def start(self):
        self.over = send(self.grad.at[:, self.d], self.rc, self.ss.at[9], self.rs.at[9], self.across)
        self.sends.append(self.over)

    def cores(self):
        self.over.wait_recv()
        c, d, cut = self.c, self.d, self.cut

        def add(i, _):
            a2, a1, r = lax.div(i, 4 * cut), lax.rem(lax.div(i, cut), 4), lax.rem(i, cut)
            px, pz = a1 * d + a2 * c, a1 * c + a2 * d
            at = ((lax.div(px, 2) * cut + r) * 2 + lax.rem(px, 2)) * 4 + pz
            self.sa[a2, a1, r] = (self.rc[at].astype(F32) + self.grad[at, c].astype(F32)).astype(BF)
            return 0

        lax.fori_loop(0, 16 * cut, add, 0)
        self.hop = [
            send(self.sa.at[wrap4(self.p2 + k + 1)], self.lb.at[k], self.ss.at[k], self.rs.at[k], self.to_second[k])
            for k in range(3)
        ]
        self.sends += self.hop

    def second(self):
        for copy in self.hop:
            copy.wait_recv()

        def add(i, _):
            a1, r = lax.div(i, self.cut), lax.rem(i, self.cut)
            total = self.sa[self.p2, a1, r].astype(F32)
            for k in range(3):
                total = total + self.lb[k, a1, r].astype(F32)
            self.sb[a1, r] = total.astype(BF)
            return 0

        lax.fori_loop(0, 4 * self.cut, add, 0)
        self.hop = [
            send(self.sb.at[wrap4(self.p1 + k + 1)], self.l2.at[k], self.ss.at[3 + k], self.rs.at[3 + k], self.to_first[k])
            for k in range(3)
        ]
        self.sends += self.hop

    def first(self, out=None):
        for copy in self.hop:
            copy.wait_recv()
        for r in range(self.cut):
            total = self.sb[self.p1, r].astype(F32)
            for k in range(3):
                total = total + self.l2[k, r].astype(F32)
            if out is not None:
                out[...] = total
            else:
                self.sd[r] = total.astype(BF)
        if out is None:
            y = self.y
            self.hop = [
                send(self.sd.at[wrap4(y + k + 1)], self.ry.at[y], self.ss.at[6 + k], self.rs.at[6 + k], self.ring[k])
                for k in range(3)
            ]
            self.sends += self.hop
            self.ry[y] = self.sd[y]

    def owners(self):
        for copy in self.hop:
            copy.wait_recv()

    def done(self):
        for copy in self.sends:
            copy.wait_send()


def middle_kernel(
    att, tok, cot, wo, wg, wu, wdp, rows,
    out, dmid, datt, gffn, go, og, ou, od,
    part, land1, acc, unit, mid, dhid, dgu, hid, dpart, land2, dbr, opart, land3, gbs, gds,
    bparts, wbl, wdl, wb, wd, ssem, rsem, *scratch,
):
    x, y, z, c = coords()
    ring = [device(x, wrap4(y + k), z, c) for k in range(1, 4)]
    sb = Sums(gbs, 8, 1536, 4, scratch[:9])
    sd = Sums(gds, 24, 1024, 1, scratch[9:18])
    b = Pieces(wbl, True, *scratch[18:20])
    w = Pieces(wdl, False, *scratch[20:22])
    for r in range(4):
        for g in range(2):
            h = g * 4 + r
            bparts[r, :, g * 384 : g * 384 + 384] = wg[:, h * 384 : h * 384 + 384]
            bparts[r, :, 768 + g * 384 : 1152 + g * 384] = wu[:, h * 384 : h * 384 + 384]
    wdl[lax.div(x, 2), lax.rem(x, 2) * 8 + z * 2 + c] = wdp[...]
    gain = rows[1:2, :1024]
    greet_all()
    sends = []

    def ring_send(n, k, src, dst):
        sends.append(send(src, dst, ssem.at[n, k - 1], rsem.at[n, k - 1], ring[k - 1]))

    def ring_wait(n, k, dst):
        arrived(dst, rsem.at[n, k - 1], ring[0])

    b.to_ring(bparts)
    for k in (2, 1, 3, 0):
        p = dot(att[wrap4(y + k)], wo[...], 1, 0)
        if k:
            part[k - 1] = p.astype(BF)
            ring_send(0, k, part.at[k - 1], land1.at[k - 1])
        else:
            acc[...] = p + tok[...].astype(F32)
    b.from_ring()
    b.own()
    w.own()
    b.pass_all_on()
    w.pass_all_on()
    for k in (1, 3, 2):
        ring_wait(0, k, land1.at[k - 1])
    total = acc[...]
    for k in range(3):
        total = total + land1[k].astype(F32)
    acc[...] = total
    scale = rms_scale(total)
    unit[...] = total * scale
    mid[y] = (total * scale * gain).astype(BF)
    for k in (2, 1, 3):
        ring_send(1, k, mid.at[y], mid.at[y])
    b.pass_all_across()
    w.pass_all_across()
    w.all_here()
    pack_down(wdl, wd)
    for r in range(4):
        dhid[r] = dot(cot[r], wd[...], 1, 1)
    b.all_here()
    pack_wide(wbl, wb)

    for k in (0, 1, 3, 2):
        r = wrap4(y - k)
        if k:
            ring_wait(1, k, mid.at[r])
        gu = dot(mid[r], wb[...], 1, 0)
        gate, up = gu[:, :768], gu[:, 768:]
        sig = 1.0 / (1.0 + jnp.exp(-gate))
        act = gate * sig
        dh = dhid[r]
        hid[r] = (act * up).astype(BF)
        dgu[r, :, :768] = (dh * up * sig * (1.0 + gate * (1.0 - sig))).astype(BF)
        dgu[r, :, 768:] = (dh * act).astype(BF)
        p = dot(dgu[r], wb[...], 1, 1)
        if k:
            dpart[k - 1] = p.astype(BF)
            ring_send(2, 4 - k, dpart.at[k - 1], land2.at[3 - k])
        else:
            dmid[...] = p

    for k in (1, 3, 2):
        ring_wait(2, k, land2.at[k - 1])
    total = dmid[...]
    for k in range(3):
        total = total + land2[k].astype(F32)
    gffn[...] = jnp.sum(total * unit[...], axis=0, keepdims=True)
    total = total * gain
    mean = jnp.mean(total * unit[...], axis=-1, keepdims=True)
    total = cot[y].astype(F32) + rms_scale(acc[...]) * (total - unit[...] * mean)
    dmid[...] = total
    dbr[y] = total.astype(BF)
    for k in (2, 1, 3):
        ring_send(3, k, dbr.at[y], dbr.at[y])

    def gate_up_rows(f, _):
        cols = pl.ds(pl.multiple_of(f * 128, 128), 128)
        rows = mid[:, :, cols].reshape(CHUNK, 128)
        g = dot(rows, dgu[...].reshape(CHUNK, 1536), 0, 0)
        gbs[pl.ds(f * 8, 8)] = g.reshape(8, 2, 8, 1536).astype(BF)
        return 0

    lax.fori_loop(0, 8, gate_up_rows, 0)
    sb.start()

    def down_rows(f, _):
        cols = pl.ds(pl.multiple_of(f * 384, 384), 384)
        rows = hid[:, :, cols].reshape(CHUNK, 384)
        g = dot(rows, cot[...].reshape(CHUNK, 1024), 0, 0)
        gds[pl.ds(f * 8, 8)] = g.reshape(8, 2, 24, 1024).astype(BF)
        return 0

    lax.fori_loop(0, 2, down_rows, 0)
    sd.start()
    for k in (2, 1, 3, 0):
        p = dot(hid[wrap4(y + k)], wd[...], 1, 0)
        if k:
            opart[k - 1] = p.astype(BF)
            ring_send(4, k, opart.at[k - 1], land3.at[k - 1])
        else:
            acc[...] = acc[...] + p
    sb.cores()
    sd.cores()
    for k in (0, 1, 3, 2):
        r = wrap4(y - k)
        if k:
            ring_wait(3, k, dbr.at[r])
        datt[r] = dot(dbr[r], wo[...], 1, 1).astype(BF)

    def out_rows(f, _):
        cols = pl.ds(pl.multiple_of(f * 256, 256), 256)
        rows = att[:, :, cols].reshape(CHUNK, 256)
        g = dot(rows, dbr[...].reshape(CHUNK, 1024), 0, 0)
        go[pl.ds(f * 8, 8)] = g.reshape(8, 2, 16, 1024).astype(BF)
        return 0

    lax.fori_loop(0, 2, out_rows, 0)
    for k in (1, 3, 2):
        ring_wait(4, k, land3.at[k - 1])
    total = acc[...]
    for k in range(3):
        total = total + land3[k].astype(F32)
    out[...] = total.astype(BF)
    sb.second()
    sd.second()
    sb.first()
    sd.first(od)
    sb.owners()
    for r in range(4):
        for g in range(2):
            h = g * 4 + r
            og[:, h * 384 : h * 384 + 384] = sb.ry[r, :, g * 384 : g * 384 + 384].astype(F32)
            ou[:, h * 384 : h * 384 + 384] = sb.ry[r, :, 768 + g * 384 : 1152 + g * 384].astype(F32)
    for s in (sb, sd, b, w):
        s.done()
    for copy in sends:
        copy.wait_send()


def middle(att, tok, cot, wo, wg, wu, wd, rows):
    sds = jax.ShapeDtypeStruct
    block = (128, 1024)
    return pl.pallas_call(
        middle_kernel,
        out_shape=(
            sds(block, BF),
            sds(block, F32),
            sds((4, 128, 512), BF),
            sds((1, 1024), F32),
            sds((16, 2, 16, 1024), BF),
            sds((8, 3072), F32),
            sds((8, 3072), F32),
            sds((24, 1024), F32),
        ),
        in_specs=[VMEM] * 8,
        out_specs=(VMEM,) * 8,
        scratch_shapes=[
            pltpu.VMEM((3,) + block, BF),
            pltpu.VMEM((3,) + block, BF),
            pltpu.VMEM(block, F32),
            pltpu.VMEM(block, F32),
            pltpu.VMEM((4,) + block, BF),
            pltpu.VMEM((4, 128, 768), F32),
            pltpu.VMEM((4, 128, 1536), BF),
            pltpu.VMEM((4, 128, 768), BF),
            pltpu.VMEM((3,) + block, BF),
            pltpu.VMEM((3,) + block, BF),
            pltpu.VMEM((4,) + block, BF),
            pltpu.VMEM((3,) + block, BF),
            pltpu.VMEM((3,) + block, BF),
            pltpu.VMEM((64, 2, 8, 1536), BF),
            pltpu.VMEM((16, 2, 24, 1024), BF),
            pltpu.VMEM((4, 8, 1536), BF),
            pltpu.VMEM((2, 4, 16, 8, 1536), BF),
            pltpu.VMEM((2, 16, 24, 1024), BF),
            pltpu.VMEM((1024, 1536), BF),
            pltpu.VMEM((768, 1024), BF),
            DMA((5, 3)),
            DMA((5, 3)),
        ]
        + Sums.scratch(8, 1536, 4)
        + Sums.scratch(24, 1024, 1)
        + Pieces.semaphores() * 2,
        compiler_params=params(3),
        name="middle",
    )(att, tok, cot, wo, wg, wu, wd, rows)


def back_kernel(
    q, kvx, lse, att, datt, low, xn, wa, rows, go, dmid, tok, gffn, ic, isn, oc, osn,
    igrad, oq, ok, ov, oo, ogain,
    cos, sin, do, inner, dq, dkv, dkvb, land, raw, dqkv, gaq, gakv, grow, acc, dpart, landx, ssem, rsem, *scratch,
):
    x, y, z, c = coords()
    ring = [device(x, wrap4(y + k), z, c) for k in range(1, 4)]
    so = Sums(go, 16, 1024, 1, scratch[:9])
    sq = Sums(gaq, 8, 512, 4, scratch[9:18])
    sk = Sums(gakv, 8, 640, 4, scratch[18:27])
    q_gain, k_gain = rows[2:3, 1024:], rows[3:4, 1024:]
    greet_all(True)
    so.start()
    sends = []
    rope_here(ic, isn, oc, osn, cos, sin)
    ones = jnp.ones((8, 128), BF)
    for g in range(2):
        for t in range(2):
            for hd in range(2):
                cols = slice((g * 2 + hd) * 128, (g * 2 + hd) * 128 + 128)
                for half in range(2):
                    first = hd * 256 + half * 128
                    d = datt[2 * t + half, :, cols]
                    do[g, t, first : first + 128] = d
                    prod = d.astype(F32) * att[2 * t + half, :, cols].astype(F32)
                    high = prod.astype(BF)
                    rest = (prod - high.astype(F32)).astype(BF)
                    inner[g, t, :, first : first + 128] = (dot(ones, high, 1, 1) + dot(ones, rest, 1, 1))[:1]
    attend_back(q, kvx, low, lse, do, inner, dq, dkv, 0, True)
    dkvb[:, 0] = dkv[:, 0].astype(BF)
    sends.append(send(dkvb.at[:, 0], land.at[0], ssem.at[0, 0], rsem.at[0, 0], chunk_device(-2)))
    attend_back(q, kvx, low, lse, do, inner, dq, dkv, 1, False)
    dkvb[:, 1] = dkv[:, 1].astype(BF)
    sends.append(send(dkvb.at[:, 1], land.at[1], ssem.at[0, 1], rsem.at[0, 1], chunk_device(-1)))
    so.cores()
    attend_back(q, kvx, low, lse, do, inner, dq, dkv, 2, False)

    scale = HEAD_SIZE ** (-0.5)
    raw[...] = dot(xn[...], wa[:, :768], 1, 0)
    g_q = jnp.zeros((1, 128), F32)
    for g in range(2):
        for t in range(2):
            d = jnp.transpose(dq[g, t] * scale).astype(BF).astype(F32)
            span = slice(t * 256, t * 256 + 256)
            for hd in range(2):
                cols = slice((g * 2 + hd) * 128, (g * 2 + hd) * 128 + 128)
                d_raw, d_gain = prep_back(
                    d[hd * 256 : hd * 256 + 256], raw[span, cols], q_gain, cos[span], sin[span]
                )
                dqkv[span, cols] = d_raw.astype(BF)
                g_q = g_q + d_gain

    def query_rows(f, _):
        lhs = xn[:, pl.ds(pl.multiple_of(f * 128, 128), 128)]
        gaq[pl.ds(f * 8, 8)] = dot(lhs, dqkv[:, :512], 0, 0).reshape(8, 2, 8, 512).astype(BF)
        return 0

    lax.fori_loop(0, 8, query_rows, 0)
    sq.start()
    for copy in sends[:2]:
        copy.wait_recv()
    g_k = jnp.zeros((1, 128), F32)
    for g in range(2):
        d = dkv[g, 2] + land[0, g].astype(F32) + land[1, g].astype(F32)
        d = (d * scale).astype(BF).astype(F32)
        cols = slice(512 + g * 128, 640 + g * 128)
        d_raw, d_gain = prep_back(d, raw[:, cols], k_gain, cos[...], sin[...])
        dqkv[:, cols] = d_raw.astype(BF)
        g_k = g_k + d_gain
        d = dkv[2 + g, 2] + land[0, 2 + g].astype(F32) + land[1, 2 + g].astype(F32)
        dqkv[:, 768 + g * 128 : 896 + g * 128] = d.astype(BF)

    g_x = jnp.zeros((1, 1024), F32)
    for k in (2, 1, 3, 0):
        span = pl.ds(pl.multiple_of(wrap4(y + k) * 128, 128), 128)
        p = dot(dqkv[span], wa[:, :1024], 1, 1)
        g_x = g_x + jnp.sum(p * xn[span].astype(F32), axis=0, keepdims=True)
        if k:
            dpart[k - 1] = p.astype(BF)
            sends.append(send(dpart.at[k - 1], landx.at[k - 1], ssem.at[1, k - 1], rsem.at[1, k - 1], ring[k - 1]))
        else:
            acc[...] = p
    eight = lax.div(lax.broadcasted_iota(jnp.int32, (128, 1024), 1), 8) == lax.broadcasted_iota(jnp.int32, (128, 1024), 0)
    eight = eight.astype(F32).astype(BF)
    grow[...] = jnp.zeros_like(grow)
    grow[0:1] = g_x / rows[0:1, :1024]
    grow[1:2] = gffn[...]
    grow[2:3] = dot(jnp.broadcast_to(g_q, (8, 128)).astype(BF), eight, 1, 0)[:1]
    grow[3:4] = dot(jnp.broadcast_to(g_k, (8, 128)).astype(BF), eight, 1, 0)[:1]

    def key_rows(f, _):
        span = pl.ds(pl.multiple_of(f * 128, 128), 128)
        part = dot(xn[:, span], dqkv[:, 512:], 0, 0)
        gakv[pl.ds(f * 8, 8), :, :, :512] = part.reshape(8, 2, 8, 512).astype(BF)
        gakv[pl.ds(f * 8, 8), :, :, 512:] = jnp.transpose(grow[:, span]).reshape(8, 2, 8, 128).astype(BF)
        return 0

    lax.fori_loop(0, 8, key_rows, 0)
    sk.start()
    so.second()
    sq.cores()
    sk.cores()
    for k in (1, 3, 2):
        arrived(landx.at[k - 1], rsem.at[1, k - 1], ring[0])
    total = acc[...]
    for k in range(3):
        total = total + landx[k].astype(F32)
    own = tok[...].astype(F32)
    scale_own = rms_scale(own)
    unit = own * scale_own
    total = total * rows[0:1, :1024]
    mean = jnp.mean(total * unit, axis=-1, keepdims=True)
    igrad[...] = (dmid[...] + scale_own * (total - unit * mean)).astype(BF)
    sq.second()
    sk.second()
    so.first(oo)
    sq.first()
    sk.first()
    sq.owners()
    sk.owners()
    gain = jnp.zeros((8, 128), F32)
    for r in range(4):
        for g in range(2):
            h = g * 4 + r
            oq[:, h * 256 : h * 256 + 256] = sq.ry[r, :, g * 256 : g * 256 + 256].astype(F32)
            ok[:, h * 128 : h * 128 + 128] = sk.ry[r, :, g * 128 : g * 128 + 128].astype(F32)
            ov[:, h * 128 : h * 128 + 128] = sk.ry[r, :, 256 + g * 128 : 384 + g * 128].astype(F32)
        gain = gain + sk.ry[r, :, 512:640].astype(F32)
    ogain[...] = gain
    for copy in sends:
        copy.wait_send()
    for s in (so, sq, sk):
        s.done()


def back(q, kvx, lse, att, datt, low, xn, wa, rows, go, dmid, tok, gffn):
    sds = jax.ShapeDtypeStruct
    block = (128, 1024)
    return pl.pallas_call(
        back_kernel,
        out_shape=(
            sds(block, BF),
            sds((8, 2048), F32),
            sds((8, 1024), F32),
            sds((8, 1024), F32),
            sds((16, 1024), F32),
            sds((8, 128), F32),
        ),
        in_specs=[VMEM] * 17,
        out_specs=(VMEM,) * 6,
        scratch_shapes=[
            pltpu.VMEM((CHUNK, 128), F32),
            pltpu.VMEM((CHUNK, 128), F32),
            pltpu.VMEM((2, 2, 512, 128), BF),
            pltpu.VMEM((2, 2, 1, 512), F32),
            pltpu.VMEM((2, 2, 128, 512), F32),
            pltpu.VMEM((4, 3, CHUNK, 128), F32),
            pltpu.VMEM((4, 2, CHUNK, 128), BF),
            pltpu.VMEM((2, 4, CHUNK, 128), BF),
            pltpu.VMEM((CHUNK, 768), F32),
            pltpu.VMEM((CHUNK, 1024), BF),
            pltpu.VMEM((64, 2, 8, 512), BF),
            pltpu.VMEM((64, 2, 8, 640), BF),
            pltpu.VMEM((128, 1024), F32),
            pltpu.VMEM(block, F32),
            pltpu.VMEM((3,) + block, BF),
            pltpu.VMEM((3,) + block, BF),
            DMA((2, 3)),
            DMA((2, 3)),
        ]
        + Sums.scratch(16, 1024, 1)
        + Sums.scratch(8, 512, 4)
        + Sums.scratch(8, 640, 4),
        compiler_params=params(1),
        name="back",
    )(q, kvx, lse, att, datt, low, xn, wa, rows, go, dmid, tok, gffn, *rope_tables())


def first_keys(segments):
    padded = jnp.concatenate([jnp.full((2 * CHUNK,), -1, jnp.int32), segments])
    keys = lax.dynamic_slice_in_dim(padded, chunk_number() * CHUNK, 3 * CHUNK, 0)
    begins = jnp.sum((keys[:, None] < keys[None, 2 * CHUNK :]).astype(jnp.int32), axis=0)
    low = jnp.maximum(begins, jnp.arange(1, CHUNK + 1, dtype=jnp.int32)).reshape(2, 1, 256)
    return jnp.concatenate([low, low], axis=2)


def local(
    tokens, cotangent, segments, attn_gain, w_query, key_matrix, value_matrix, query_gain, key_gain,
    w_out, ffn_gain, w_gate, w_up, w_down,
):
    low = first_keys(segments)
    gains = jnp.stack(
        [attn_gain, ffn_gain, jnp.broadcast_to(query_gain, (8,)), jnp.broadcast_to(key_gain, (8,))], axis=1
    )
    gains = jnp.pad(gains, ((0, 0), (0, 124)))
    att, cs, wo, wa, rows, xn, q, kvx, lse = front(
        tokens, cotangent, w_query, key_matrix, value_matrix, gains, w_out, low
    )
    output, d_mid, d_att, g_ffn, go, g_gate, g_up, g_down = middle(
        att, tokens, cs, wo.reshape(512, 1024), w_gate, w_up, w_down, rows
    )
    input_grad, g_query, g_key, g_value, g_out, g_gains = back(
        q, kvx, lse, att, d_att, low, xn, wa, rows, go, d_mid, tokens, g_ffn
    )
    return (
        output,
        input_grad,
        g_gains[:, 0],
        g_query,
        g_key,
        g_value,
        g_gains[0, 2:3],
        g_gains[0, 3:4],
        g_out,
        g_gains[:, 1],
        g_gate,
        g_up,
        g_down,
    )


def solution(mesh):
    rows = P(("blk", "head"), None)
    cut = P(("head", "blk"), None)
    vec = P(("head", "blk"))
    return jax.shard_map(
        local,
        mesh=mesh,
        in_specs=(rows, rows, P(), vec, cut, cut, cut, vec, vec, cut, vec, cut, cut, cut),
        out_specs=(rows, rows, vec, cut, cut, cut, vec, vec, cut, vec, cut, cut, cut),
        check_vma=False,
    )
```

time: 358 us -> 227 us (0.63)
  matrix products: 42.9 us -> 0 us
  other arithmetic: 34.4 us -> 1.07 us
  local copies, waits for them, and re-layouts: 48.2 us -> 16.6 us
  Pallas kernels: 223 us -> 204 us
    dot_general x8 -> x0, matrix products: 31.7 us -> none  [the longest x1 7.73 us: local(): d_v = jnp.einsum('kgqc,qkgd->ckd', probs, d4, preferred_element_type=F32)]
    convert_element_type x9 -> x0, other arithmetic: 16.2 us -> none  [the longest x1 7.16 us: local(): d_scores = (soft * (d_probs - inner)).astype(BF)]
    pallas_call x5 -> x2, Pallas kernels: 131 us -> 116 us  [the longest x1 59.4 us: front(): pl.pallas_call(front_kernel, out_shape=(sds((4, 128, 512), BF), sds((4, 1...]
    concatenate x5 -> x0, local copies, waits for them, and re-layouts: 13.1 us -> none  [the longest x2 10.5 us: local(): jnp.concatenate([dot(x_normed, d_qkv, 0, 0).astype(BF), g_gains], axis=1)]
    sub x1 -> x0, matrix products: 11.1 us -> none  [local(): weight = jnp.exp(scores - peak)]
    reduce_sum x8 -> x1, other arithmetic: 7.48 us -> 0.38 us  [first_keys(): jnp.sum((keys[:, None] < keys[None, 2 * CHUNK:]).astype(jnp.int32), axis=0)]
    slice x14 -> x3, local copies, waits for them, and re-layouts: 8.3 us -> 3.59 us  [the longest x1 1.48 us: local(): g_gains[:, 1]]
    pallas_call x1, Pallas kernels: 92.1 us -> 87.9 us  [middle(): pl.pallas_call(middle_kernel, out_shape=(sds(block, BF), sds(block, F32),...]
where the time goes in v3:
time: 227 us; the launch traced here: 223 us
  Pallas kernels  204 us (90%)
  local copies, waits for them, and re-layouts  16.6 us (7%)
    pallas_call x1, Pallas kernels, middle(): pl.pallas_call(middle_kernel, out_shape=(sds(block, BF), sds(block, F32),...  87.9 us
    pallas_call x1, Pallas kernels, front(): pl.pallas_call(front_kernel, out_shape=(sds((4, 128, 512), BF), sds((4, 1...  59.4 us
    pallas_call x1, Pallas kernels, back(): pl.pallas_call(back_kernel, out_shape=(sds(block, BF), sds((8, 2048), F32...  56.5 us
    unnamed x17, local copies, waits for them, and re-layouts  10 us

profile of v3, /device:TPU:0, one launch (start us, length us, event | category | flops | bytes accessed | tf_op | source)
XLA Modules:
  0.0 223.5 jit_solution(2035171254500714829)
XLA Ops:
  2.0 0.1 pad.10.clone
  2.0 0.1 pad.11.clone
  2.1 0.8 pad_dynamic-slice_fusion
  2.9 0.7 copy.39
  3.6 0.7 copy.40
  4.4 0.1 maximum_maximum_fusion
  4.4 0.6 pad.5.gains
  5.0 0.8 pad_dynamic-slice_fusion.1
  5.8 0.4 convert_reduce_fusion
  6.2 0.6 pad_add_fusion.low
  6.8 59.4 %front.1 = (bf16[4,128,512]{2,1,0:T(8,128)(2,1)}, bf16[4,128,1024]{2,1,0:T(8,128)(2,1)}, bf16[2,16,16,1024]{3,2,1,0:T(8,128)(2,1)}, bf16[1024,1152]{1,0:T(8,128)...) custom-call(bf16[128,1024]{1,0:T(8,128)(2,1)} %tok.5, ...), custom_call_target="tpu_custom_call" | custom-call | tf_op jit(solution)/shard_map/front/pallas_call | solution.py:417
  66.2 87.9 %middle.1 = (bf16[128,1024]{1,0:T(8,128)(2,1)}, f32[128,1024]{1,0:T(8,128)}, bf16[4,128,512]{2,1,0:T(8,128)(2,1)}, f32[1,1024]{1,0:T(1,128)}, bf16[16,2,16,1024]...) custom-call(bf16[4,128,512]{2,1,0:T(8,128)(2,1)} %get-tuple-element.36.att, ...), custom_call_target="tpu_custom_call" | custom-call | tf_op jit(solution)/shard_map/middle/pallas_call | solution.py:702
  154.1 0.0 copy-start
  154.1 0.0 copy-start.3
  154.1 0.0 copy-start.2
  154.1 0.0 copy-start.1
  154.1 56.5 %back.1 = (bf16[128,1024]{1,0:T(8,128)(2,1)}, f32[8,2048]{1,0:T(8,128)}, f32[8,1024]{1,0:T(8,128)}, f32[8,1024]{1,0:T(8,128)}, f32[16,1024]{1,0:T(8,128)}, /*index=5*/f32[8,128]{1,0:T(8,128)}) custom-call(bf16[2,2,512,128]{3,2,1,0:T(8,128)(2,1)} %get-tuple-element.41.q, bf16[4,3,512,128]{3,2,1,0:T(8,128)(2,1)} %get-tuple-element.42.kvx, ...), custom_call_target="tpu_custom_call" | custom-call | tf_op jit(solution)/shard_map/back/pallas_call | solution.py:886
  210.7 1.3 fusion
  212.0 1.5 slice_reduce_fusion
  213.5 0.0 copy-done
  213.5 0.7 copy.52
  214.2 1.7 copy.53
  215.9 1.5 copy.54
  217.3 1.4 copy.55
  218.7 1.4 copy.56
  220.1 1.5 copy.57
  221.6 0.0 copy-done.3
  221.6 0.6 copy.58
  222.2 0.0 copy-done.2
  222.2 0.6 copy.59
  222.9 0.0 copy-done.1
  222.9 0.6 copy.60
  (1 shorter events, 0.0 us)
Async XLA Ops:
  154.1 59.4 %copy-start = (bf16[128,1024]{1,0:T(8,128)(2,1)S(1)}, bf16[128,1024]{1,0:T(8,128)(2,1)}, u32[]{:S(2)}) copy-start(bf16[128,1024]{1,0:T(8,128)(2,1)} %get-tuple-element.76) | copy-start | bytes 786436
  154.1 67.5 %copy-start.3 = (f32[8,3072]{1,0:T(8,128)S(1)}, f32[8,3072]{1,0:T(8,128)}, u32[]{:S(2)}) copy-start(f32[8,3072]{1,0:T(8,128)} %get-tuple-element.86) | copy-start | bytes 294916
  154.1 68.1 %copy-start.2 = (f32[8,3072]{1,0:T(8,128)S(1)}, f32[8,3072]{1,0:T(8,128)}, u32[]{:S(2)}) copy-start(f32[8,3072]{1,0:T(8,128)} %get-tuple-element.87) | copy-start | bytes 294916
  154.1 68.7 %copy-start.1 = (f32[24,1024]{1,0:T(8,128)S(1)}, f32[24,1024]{1,0:T(8,128)}, u32[]{:S(2)}) copy-start(f32[24,1024]{1,0:T(8,128)} %get-tuple-element.88) | copy-start | bytes 294916

commit v4 on v3

v4 whole, which is shorter than its diff:
```python
import math

import jax
import jax.numpy as jnp
import numpy as np
from jax import lax
from jax.experimental import pallas as pl
from jax.experimental.pallas import tpu as pltpu
from jax.sharding import PartitionSpec as P

HEAD_SIZE = 128
SPAN = 1024
CHUNK = 512
EPS = 1e-06
ROPE_BASE = 1000000.0
MASKED = -1e30
MESH = pl.DeviceIdType.MESH
BF = jnp.bfloat16
F32 = jnp.float32
VMEM = pl.BlockSpec(memory_space=pltpu.VMEM)
DMA = pltpu.SemaphoreType.DMA
VMEM_LIMIT = 62 * 2**20


def coords():
    h = lax.axis_index("head")
    b = lax.axis_index("blk")
    x = 2 * lax.div(h, 4) + lax.div(b, 8)
    return x, lax.rem(h, 4), lax.rem(lax.div(b, 2), 4), lax.rem(b, 2)


def device(x, y, z, c):
    return (lax.div(x, 2) * 4 + y, lax.rem(x, 2) * 8 + z * 2 + c)


def wrap4(v):
    return lax.rem(v + 8, 4)


def send(src, dst, send_sem, recv_sem, to):
    copy = pltpu.make_async_remote_copy(
        src_ref=src, dst_ref=dst, send_sem=send_sem, recv_sem=recv_sem, device_id=to, device_id_type=MESH
    )
    copy.start()
    return copy


def arrived(dst, sem, anyone):
    pltpu.make_async_remote_copy(
        src_ref=dst, dst_ref=dst, send_sem=sem, recv_sem=sem, device_id=anyone, device_id_type=MESH
    ).wait_recv()


def meet(peers):
    barrier = pltpu.get_barrier_semaphore()
    for peer in peers:
        pl.semaphore_signal(barrier, inc=1, device_id=peer, device_id_type=MESH)
    pl.semaphore_wait(barrier, len(peers))


def params(collective_id):
    return pltpu.CompilerParams(
        collective_id=collective_id, has_side_effects=True, vmem_limit_bytes=VMEM_LIMIT
    )


def chunk_number():
    return 2 * lax.axis_index("blk") + lax.div(lax.axis_index("head"), 4)


def chunk_device(step):
    chunk = lax.rem(chunk_number() + step + 32, 32)
    return (lax.rem(chunk, 2) * 4 + lax.rem(lax.axis_index("head"), 4), lax.div(chunk, 2))


def greet_all(chunks=False):
    x, y, z, c = coords()
    peers = [device(x, wrap4(y + k), z, c) for k in range(1, 4)]
    peers += [device(wrap4(x + k), y, z, c) for k in range(1, 4)]
    peers += [device(x, y, wrap4(z + k), c) for k in range(1, 4)]
    peers += [device(x, y, z, 1 - c)]
    if chunks:
        peers += [chunk_device(s) for s in (-2, -1, 1, 2)]
    meet(peers)


def dot(a, b, ca, cb):
    return lax.dot_general(a, b, (((ca,), (cb,)), ((), ())), preferred_element_type=F32)


def rms_scale(rows):
    return lax.rsqrt(jnp.mean(rows * rows, axis=-1, keepdims=True) + EPS)


def rope_tables():
    freq = ROPE_BASE ** (-np.arange(0, HEAD_SIZE, 2, dtype=np.float64) / HEAD_SIZE)
    freq = np.concatenate([freq, freq])
    sign = np.where(np.arange(HEAD_SIZE) < 64, -1.0, 1.0)
    inner = np.arange(CHUNK)[:, None] * freq[None, :]
    outer = (np.arange(32) * CHUNK)[:, None] * freq[None, :]
    tables = [f(a) * s for a in (inner, outer) for f, s in ((np.cos, 1.0), (np.sin, sign))]
    return [jnp.asarray(t.astype(np.float32)) for t in tables]


def rope_here(ic, isn, oc, osn, cos, sin):
    n = chunk_number()
    c0, s0 = oc[pl.ds(n, 1), :], osn[pl.ds(n, 1), :]
    cos[...] = c0 * ic[...] - s0 * isn[...]
    sin[...] = s0 * ic[...] + c0 * isn[...]


def rope(rows, cos, sin):
    return rows * cos + pltpu.roll(rows, 64, 1) * sin


def rope_back(rows, cos, sin):
    return rows * cos + pltpu.roll(rows * sin, 64, 1)


def prep_back(d, raw, gain, cos, sin):
    scale = rms_scale(raw)
    unit = raw * scale
    d = rope_back(d, cos, sin)
    d_gain = jnp.sum(d * unit, axis=0, keepdims=True)
    d = d * gain
    return scale * (d - unit * jnp.mean(d * unit, axis=-1, keepdims=True)), d_gain


REACH = (((0, 512), (256, 256)), ((0, 512), (0, 512)), ((0, 256), (0, 512)))
EXP_SCALE = HEAD_SIZE ** (-0.5) * math.log2(math.e)


def allowed(low, slot, t):
    first, count = REACH[slot][t]
    place = lax.broadcasted_iota(jnp.int32, (count, 512), 0) + (slot * CHUNK + first)
    ok = place >= low[t]
    if slot == 2:
        query = lax.rem(lax.broadcasted_iota(jnp.int32, (1, 512), 1), 256) + (t * 256 + SPAN)
        ok = ok & (place <= query)
    return ok


def attend(q, kvx, low, peak, total, acc, slot, fresh):
    def group(g, _):
        for t in range(2):
            first, count = REACH[slot][t]
            keys = kvx[g, slot, first : first + count]
            values = kvx[2 + g, slot, first : first + count]
            s = dot(keys, q[g, t], 1, 1)
            s = jnp.where(allowed(low, slot, t), s, MASKED)
            top = jnp.max(s, axis=0, keepdims=True)
            if not fresh:
                before = peak[g, t]
                top = jnp.maximum(top, before)
                fade = jnp.exp2((before - top) * EXP_SCALE)
            p = jnp.exp2((s - top) * EXP_SCALE)
            add = jnp.sum(p, axis=0, keepdims=True)
            o = dot(values, p.astype(BF), 0, 0)
            if not fresh:
                add = add + total[g, t] * fade
                o = o + acc[g, t] * fade
            peak[g, t] = top
            total[g, t] = add
            acc[g, t] = o
        return 0

    lax.fori_loop(0, 2, group, 0)


def attend_back(q, kvx, low, lse, do, inner, dq, dkv, slot, fresh):
    def group(g, _):
        for t in range(2):
            first, count = REACH[slot][t]
            rows = slice(first, first + count)
            keys = kvx[g, slot, rows]
            values = kvx[2 + g, slot, rows]
            s = dot(keys, q[g, t], 1, 1)
            p = jnp.where(allowed(low, slot, t), jnp.exp2(s * EXP_SCALE - lse[g, t]), 0.0)
            dp = dot(values, do[g, t], 1, 1)
            ds = (p * (dp - inner[g, t])).astype(BF)
            dv = dot(p.astype(BF), do[g, t], 1, 0)
            dk = dot(ds, q[g, t], 1, 0)
            whole = count == CHUNK
            if whole and (t == 0 or slot == 2):
                other = slice(0, 256)
                if t == 0:
                    dkv[g, slot] = dk
                    dkv[2 + g, slot] = dv
                else:
                    dkv[g, slot, other] = dkv[g, slot, other] + dk[other]
                    dkv[2 + g, slot, other] = dkv[2 + g, slot, other] + dv[other]
                    dkv[g, slot, 256:] = dk[256:]
                    dkv[2 + g, slot, 256:] = dv[256:]
            elif t == 0:
                dkv[g, slot, rows] = dk
                dkv[2 + g, slot, rows] = dv
            else:
                dkv[g, slot, rows] = dkv[g, slot, rows] + dk
                dkv[2 + g, slot, rows] = dkv[2 + g, slot, rows] + dv
            d = dot(keys, ds, 0, 0)
            dq[g, t] = d if fresh else dq[g, t] + d
        return 0

    lax.fori_loop(0, 2, group, 0)


class Pieces:
    def __init__(self, ref, wide, ssem, rsem):
        self.ref, self.wide, self.ssem, self.rsem = ref, wide, ssem, rsem
        self.x, self.y, self.z, self.c = x, y, z, c = coords()
        self.d = 1 - c
        self.across = device(x, y, z, 1 - c)
        self.ring = [device(x, wrap4(y + k), z, c) for k in range(1, 4)]
        self.sends = []

    @staticmethod
    def semaphores():
        return [DMA((34,)), DMA((34,))]

    def slot(self, px, pz, core):
        place = lax.rem(px, 2) * 4 + pz
        if self.wide:
            return self.ref.at[lax.div(px, 2), :, place, core]
        return self.ref.at[lax.div(px, 2), 0, place, core]

    def piece(self, j, k):
        c, d = self.c, self.d
        return self.slot(wrap4(self.x - j * d - k * c), wrap4(self.z - j * c - k * d), c)

    def piece_across(self, j, k):
        c, d = self.c, self.d
        return self.slot(wrap4(self.x - j * c - k * d), wrap4(self.z - j * d - k * c), d)

    def send(self, src, dst, n, to):
        self.sends.append(send(src, dst, self.ssem.at[n], self.rsem.at[n], to))

    def first(self, k):
        return device(wrap4(self.x + k * self.d), self.y, wrap4(self.z + k * self.c), self.c)

    def second(self, k):
        return device(wrap4(self.x + k * self.c), self.y, wrap4(self.z + k * self.d), self.c)

    def to_ring(self, parts):
        place = lax.rem(self.x, 2) * 4 + self.z
        xh = lax.div(self.x, 2)
        self.at_ring = lambda r: self.ref.at[xh, r, place, self.c]
        for k in range(1, 4):
            self.send(parts.at[wrap4(self.y + k)], self.at_ring(self.y), 30 + k, self.ring[k - 1])
        self.ref[xh, self.y, place, self.c] = parts[self.y]

    def from_ring(self):
        for k in range(1, 4):
            arrived(self.at_ring(wrap4(self.y - k)), self.rsem.at[30 + k], self.across)

    def own(self, src=None):
        src = self.piece(0, 0) if src is None else src
        for k in (2, 1, 3):
            self.send(src, self.piece(0, 0), k - 1, self.first(k))
        for k in (2, 1, 3):
            self.send(src, self.piece(0, 0), 2 + k, self.second(k))
        self.send(src, self.piece(0, 0), 15, self.across)

    def pass_on(self, j):
        here = self.piece(j, 0)
        arrived(here, self.rsem.at[j - 1], self.across)
        for k in (2, 1, 3):
            self.send(here, here, 2 + 3 * j + k, self.second(k))
        self.send(here, here, 15 + 4 * j, self.across)

    def pass_across(self, j, k):
        here = self.piece(j, k)
        arrived(here, self.rsem.at[2 + 3 * j + k], self.across)
        self.send(here, here, 15 + 4 * j + k, self.across)

    def pass_all_on(self):
        for j in (1, 3, 2):
            self.pass_on(j)

    def pass_all_across(self):
        for j in (0, 1, 3, 2):
            for k in (1, 3, 2):
                self.pass_across(j, k)

    def all_here(self):
        for j in range(4):
            for k in range(4):
                arrived(self.piece_across(j, k), self.rsem.at[15 + 4 * j + k], self.across)

    def done(self):
        for copy in self.sends:
            copy.wait_send()


def pack_wide(src, dst):
    cols = src.shape[-1]

    def rows(i, _):
        part = src[lax.div(i, 4), lax.rem(i, 4)].astype(F32).reshape(128, cols)
        dst[pl.ds(pl.multiple_of(i * 128, 128), 128)] = part.astype(BF)
        return 0

    lax.fori_loop(0, 8, rows, 0)


def pack_down(src, dst):
    def rows(i, _):
        part = src[lax.div(i, 4), 0, pl.ds(lax.rem(i, 4) * 2, 2)].astype(F32).reshape(96, 1024)
        dst[pl.ds(pl.multiple_of(i * 96, 96), 96)] = part.astype(BF)
        return 0

    lax.fori_loop(0, 8, rows, 0)


class Sums:
    def __init__(self, grad, cols, refs):
        self.grad, self.cols, self.cut = grad, cols, grad.shape[1]
        (self.rc, self.sa, self.lb, self.sb, self.l2, self.sd, self.ry, self.ss, self.rs) = refs
        x, y, z, c = coords()
        self.y, self.c, self.d = y, c, 1 - c
        d = self.d
        self.across = device(x, y, z, d)
        self.ring = [device(x, wrap4(y + k), z, c) for k in range(1, 4)]
        self.to_first = [device(wrap4(x + k * d), y, wrap4(z + k * c), c) for k in range(1, 4)]
        self.to_second = [device(wrap4(x + k * c), y, wrap4(z + k * d), c) for k in range(1, 4)]
        self.p1 = x * d + z * c
        self.p2 = x * c + z * d
        self.sends = []

    @staticmethod
    def scratch(rows, cols, cut):
        buffers = [(2, cut, 8), (4, 4, cut), (3, 4, cut), (4, cut), (3, cut), (cut,), (cut,)]
        return [pltpu.VMEM(lead + (rows, cols), BF) for lead in buffers] + [DMA((10,)), DMA((10,))]

    def start(self):
        self.over = send(self.grad.at[:, :, :, self.d, :, self.cols], self.rc, self.ss.at[9], self.rs.at[9], self.across)
        self.sends.append(self.over)

    def cores(self):
        self.over.wait_recv()
        c, d, cut = self.c, self.d, self.cut

        def add(i, _):
            a2, a1, r = lax.div(i, 4 * cut), lax.rem(lax.div(i, cut), 4), lax.rem(i, cut)
            px, pz = a1 * d + a2 * c, a1 * c + a2 * d
            xh, place = lax.div(px, 2), lax.rem(px, 2) * 4 + pz
            total = self.rc[xh, r, place].astype(F32) + self.grad[xh, r, place, c, :, self.cols].astype(F32)
            self.sa[a2, a1, r] = total.astype(BF)
            return 0

        lax.fori_loop(0, 16 * cut, add, 0)
        self.hop = [
            send(self.sa.at[wrap4(self.p2 + k + 1)], self.lb.at[k], self.ss.at[k], self.rs.at[k], self.to_second[k])
            for k in range(3)
        ]
        self.sends += self.hop

    def second(self):
        for copy in self.hop:
            copy.wait_recv()

        def add(i, _):
            a1, r = lax.div(i, self.cut), lax.rem(i, self.cut)
            total = self.sa[self.p2, a1, r].astype(F32)
            for k in range(3):
                total = total + self.lb[k, a1, r].astype(F32)
            self.sb[a1, r] = total.astype(BF)
            return 0

        lax.fori_loop(0, 4 * self.cut, add, 0)
        self.hop = [
            send(self.sb.at[wrap4(self.p1 + k + 1)], self.l2.at[k], self.ss.at[3 + k], self.rs.at[3 + k], self.to_first[k])
            for k in range(3)
        ]
        self.sends += self.hop

    def first(self, out=None):
        for copy in self.hop:
            copy.wait_recv()
        for r in range(self.cut):
            total = self.sb[self.p1, r].astype(F32)
            for k in range(3):
                total = total + self.l2[k, r].astype(F32)
            if out is not None:
                out[...] = total
            else:
                self.sd[r] = total.astype(BF)
        if out is None:
            y = self.y
            self.hop = [
                send(self.sd.at[wrap4(y + k + 1)], self.ry.at[y], self.ss.at[6 + k], self.rs.at[6 + k], self.ring[k])
                for k in range(3)
            ]
            self.sends += self.hop
            self.ry[y] = self.sd[y]

    def owners(self):
        for copy in self.hop:
            copy.wait_recv()

    def done(self):
        for copy in self.sends:
            copy.wait_send()


def layer_kernel(
    tok, cot, wq, wk, wv, wg, wu, gains, wop, wdp, low, ic, isn, oc, osn,
    out, igrad, oq, ok, ov, og, ou, oo, od, ogain,
    aparts, bparts, wal, wbl, wdl, wol, wa, wb, wd, xs, cs, cos, sin, rows, xn, q, kvx, lse, peak, total, wide, att,
    part, land1, acc, unit, dhid, dgu, hid, dpart, land2, dbr, opart, land3, dmid, datt, go,
    do, inner, dkv, dkvb, land, dqkv, grow, ssem, rsem, hsem, hrem, *scratch,
):
    x, y, z, c = coords()
    ring = [device(x, wrap4(y + k), z, c) for k in range(1, 4)]
    take = lambda n: [scratch.pop(0) for _ in range(n)]
    scratch = list(scratch)
    a, b, o, w = [Pieces(ref, n < 2, *take(2)) for n, ref in enumerate((wal, wbl, wol, wdl))]
    sq = Sums(wal, slice(0, 512), take(9))
    sk = Sums(wal, slice(512, 1152), take(9))
    sb = Sums(wbl, slice(0, 1536), take(9))
    so = Sums(go, slice(0, 1024), take(9))
    sd = Sums(wdl, slice(0, 1024), take(9))
    sends = []

    def ring_send(n, k, src, dst):
        sends.append(send(src, dst, ssem.at[n, k - 1], rsem.at[n, k - 1], ring[k - 1]))
        return sends[-1]

    def ring_wait(n, k, dst):
        arrived(dst, rsem.at[n, k - 1], ring[0])

    for r in range(4):
        for g in range(2):
            h = g * 4 + r
            aparts[r, :, g * 256 : g * 256 + 256] = wq[:, h * 256 : h * 256 + 256]
            aparts[r, :, 512 + g * 128 : 640 + g * 128] = wk[:, h * 128 : h * 128 + 128]
            aparts[r, :, 768 + g * 128 : 896 + g * 128] = wv[:, h * 128 : h * 128 + 128]
            bparts[r, :, g * 384 : g * 384 + 384] = wg[:, h * 384 : h * 384 + 384]
            bparts[r, :, 768 + g * 384 : 1152 + g * 384] = wu[:, h * 384 : h * 384 + 384]
        aparts[r, :, 1024:1152] = gains[...]
    greet_all(True)
    a.to_ring(aparts)
    for k in (2, 1, 3):
        ring_send(0, k, tok, xs.at[y])
    place = lax.rem(x, 2) * 4 + z
    wol[lax.div(x, 2), 0, place, c] = wop[...]
    wdl[lax.div(x, 2), 0, place, c] = wdp[...]
    xs[y] = tok[...]
    cs[y] = cot[...]
    rope_here(ic, isn, oc, osn, cos, sin)
    a.from_ring()
    a.own()
    a.pass_all_on()
    o.own()
    for k in (1, 3, 2):
        ring_wait(0, k, xs.at[wrap4(y - k)])
    b.to_ring(bparts)
    for k in (2, 1, 3):
        ring_send(1, k, cot, cs.at[y])
    a.pass_all_across()
    o.pass_all_on()
    a.all_here()
    pack_wide(wal, wa)

    pick = lax.broadcasted_iota(jnp.int32, (8, 128), 0) == lax.broadcasted_iota(jnp.int32, (8, 128), 1)
    by_row = dot(pick.astype(F32).astype(BF), wa[:, 1024:1152], 1, 1)
    rows[:, :1024] = by_row
    every = lax.broadcasted_iota(jnp.int32, (1024, 128), 0) == 8 * lax.broadcasted_iota(jnp.int32, (1024, 128), 1)
    rows[:, 1024:] = dot(by_row.astype(BF), every.astype(F32).astype(BF), 1, 0)
    attn_gain, ffn_gain = rows[0:1, :1024], rows[1:2, :1024]
    q_gain, k_gain = rows[2:3, 1024:], rows[3:4, 1024:]

    for r in range(4):
        block = xs[r].astype(F32)
        xn[r * 128 : r * 128 + 128] = (block * rms_scale(block) * attn_gain).astype(BF)
    raw = dot(xn[...], wa[:, 512:768], 1, 0)
    for g in range(2):
        k_raw = raw[:, g * 128 : g * 128 + 128]
        kvx[g, 2] = rope(k_raw * rms_scale(k_raw) * k_gain, cos[...], sin[...]).astype(BF)
    raw = dot(xn[...], wa[:, 768:1024], 1, 0)
    for g in range(2):
        kvx[2 + g, 2] = raw[:, g * 128 : g * 128 + 128].astype(BF)
    near = send(kvx.at[:, 2], kvx.at[:, 1], hsem.at[0], hrem.at[0], chunk_device(1))
    far = send(kvx.at[:, 2], kvx.at[:, 0], hsem.at[1], hrem.at[1], chunk_device(2))
    sends += [near, far]

    def queries(g, _):
        raw = dot(xn[...], wa[:, pl.ds(pl.multiple_of(g * 256, 256), 256)], 1, 0)
        for hd in range(2):
            q_raw = raw[:, hd * 128 : hd * 128 + 128]
            rot = rope(q_raw * rms_scale(q_raw) * q_gain, cos[...], sin[...]).astype(BF)
            for t in range(2):
                q[g, t, hd * 256 : hd * 256 + 256] = rot[t * 256 : t * 256 + 256]
        return 0

    lax.fori_loop(0, 2, queries, 0)

    o.pass_all_across()
    b.from_ring()
    b.own()
    w.own()
    attend(q, kvx, low, peak, total, wide, 2, True)
    near.wait_recv()
    attend(q, kvx, low, peak, total, wide, 1, False)
    b.pass_all_on()
    w.pass_all_on()
    far.wait_recv()
    attend(q, kvx, low, peak, total, wide, 0, False)
    for g in range(2):
        for t in range(2):
            done = jnp.transpose(wide[g, t] / total[g, t]).astype(BF)
            lse[g, t] = peak[g, t] * EXP_SCALE + jnp.log(total[g, t]) * math.log2(math.e)
            for hd in range(2):
                cols = slice((g * 2 + hd) * 128, (g * 2 + hd) * 128 + 128)
                for half in range(2):
                    first = hd * 256 + half * 128
                    att[2 * t + half, :, cols] = done[first : first + 128]

    o.all_here()
    wo = lambda: wol[...].reshape(512, 1024)
    first_sends = []
    for k in (2, 1, 3, 0):
        p = dot(att[wrap4(y + k)], wo(), 1, 0)
        if k:
            part[k - 1] = p.astype(BF)
            first_sends.append(ring_send(2, k, part.at[k - 1], land1.at[k - 1]))
        else:
            acc[...] = p + tok[...].astype(F32)
    b.pass_all_across()
    w.pass_all_across()
    w.all_here()
    pack_down(wdl, wd)
    for k in (1, 3, 2):
        ring_wait(1, k, cs.at[wrap4(y - k)])
    for k in (1, 3, 2):
        ring_wait(2, k, land1.at[k - 1])
    s = acc[...]
    for k in range(3):
        s = s + land1[k].astype(F32)
    acc[...] = s
    scale = rms_scale(s)
    unit[...] = s * scale
    mid = xs
    mid[y] = (s * scale * ffn_gain).astype(BF)
    for k in (2, 1, 3):
        ring_send(3, k, mid.at[y], mid.at[y])
    for r in range(4):
        dhid[r] = dot(cs[r], wd[...], 1, 1)
    b.all_here()
    pack_wide(wbl, wb)

    for k in (0, 1, 3, 2):
        r = wrap4(y - k)
        if k:
            ring_wait(3, k, mid.at[r])
        gu = dot(mid[r], wb[...], 1, 0)
        gate, up = gu[:, :768], gu[:, 768:]
        sig = 1.0 / (1.0 + jnp.exp(-gate))
        act = gate * sig
        dh = dhid[r]
        hid[r] = (act * up).astype(BF)
        dgu[r, :, :768] = (dh * up * sig * (1.0 + gate * (1.0 - sig))).astype(BF)
        dgu[r, :, 768:] = (dh * act).astype(BF)
        p = dot(dgu[r], wb[...], 1, 1)
        if k:
            dpart[k - 1] = p.astype(BF)
            ring_send(4, 4 - k, dpart.at[k - 1], land2.at[3 - k])
        else:
            dmid[...] = p
    b.done()
    w.done()

    def gate_up_rows(f, _):
        span = pl.ds(pl.multiple_of(f * 128, 128), 128)
        lhs = mid[:, :, span].reshape(CHUNK, 128)
        g = dot(lhs, dgu[...].reshape(CHUNK, 1536), 0, 0)
        wbl[lax.div(f, 4), lax.rem(f, 4)] = g.reshape(8, 2, 8, 1536).astype(BF)
        return 0

    lax.fori_loop(0, 8, gate_up_rows, 0)
    sb.start()

    for k in (1, 3, 2):
        ring_wait(4, k, land2.at[k - 1])
    s = dmid[...]
    for k in range(3):
        s = s + land2[k].astype(F32)
    grow[...] = jnp.zeros_like(grow)
    grow[1:2] = jnp.sum(s * unit[...], axis=0, keepdims=True)
    s = s * ffn_gain
    mean = jnp.mean(s * unit[...], axis=-1, keepdims=True)
    s = cs[y].astype(F32) + rms_scale(acc[...]) * (s - unit[...] * mean)
    dmid[...] = s
    dbr[y] = s.astype(BF)
    for k in (2, 1, 3):
        ring_send(5, k, dbr.at[y], dbr.at[y])

    def down_rows(f, _):
        span = pl.ds(pl.multiple_of(f * 384, 384), 384)
        lhs = hid[:, :, span].reshape(CHUNK, 384)
        g = dot(lhs, cs[...].reshape(CHUNK, 1024), 0, 0)
        wdl[f, 0] = g.reshape(8, 2, 24, 1024).astype(BF)
        return 0

    lax.fori_loop(0, 2, down_rows, 0)
    sd.start()
    sb.cores()
    for k in (2, 1, 3, 0):
        p = dot(hid[wrap4(y + k)], wd[...], 1, 0)
        if k:
            opart[k - 1] = p.astype(BF)
        else:
            acc[...] = acc[...] + p
    sd.cores()
    for k in (0, 1, 3, 2):
        r = wrap4(y - k)
        if k:
            ring_wait(5, k, dbr.at[r])
        datt[r] = dot(dbr[r], wo(), 1, 1).astype(BF)
    for k in (2, 1, 3):
        ring_send(6, k, opart.at[k - 1], land3.at[k - 1])

    ones = jnp.ones((8, 128), BF)
    for g in range(2):
        for t in range(2):
            for hd in range(2):
                cols = slice((g * 2 + hd) * 128, (g * 2 + hd) * 128 + 128)
                for half in range(2):
                    first = hd * 256 + half * 128
                    d = datt[2 * t + half, :, cols]
                    do[g, t, first : first + 128] = d
                    prod = d.astype(F32) * att[2 * t + half, :, cols].astype(F32)
                    high = prod.astype(BF)
                    rest = (prod - high.astype(F32)).astype(BF)
                    inner[g, t, :, first : first + 128] = (dot(ones, high, 1, 1) + dot(ones, rest, 1, 1))[:1]
    dq = wide
    attend_back(q, kvx, low, lse, do, inner, dq, dkv, 0, True)
    dkvb[:, 0] = dkv[:, 0].astype(BF)
    back_far = send(dkvb.at[:, 0], land.at[0], hsem.at[2], hrem.at[2], chunk_device(-2))
    attend_back(q, kvx, low, lse, do, inner, dq, dkv, 1, False)
    dkvb[:, 1] = dkv[:, 1].astype(BF)
    back_near = send(dkvb.at[:, 1], land.at[1], hsem.at[3], hrem.at[3], chunk_device(-1))
    sends += [back_far, back_near]

    def out_rows(f, _):
        span = pl.ds(pl.multiple_of(f * 256, 256), 256)
        lhs = att[:, :, span].reshape(CHUNK, 256)
        g = dot(lhs, dbr[...].reshape(CHUNK, 1024), 0, 0)
        go[f, 0] = g.reshape(8, 2, 16, 1024).astype(BF)
        return 0

    lax.fori_loop(0, 2, out_rows, 0)
    so.start()
    sb.second()
    sd.second()
    attend_back(q, kvx, low, lse, do, inner, dq, dkv, 2, False)

    scale = HEAD_SIZE ** (-0.5)
    raw = dhid
    raw[...] = dot(xn[...], wa[:, :768], 1, 0).reshape(4, 128, 768)
    a.done()
    g_q = jnp.zeros((1, 128), F32)
    for g in range(2):
        for t in range(2):
            d = jnp.transpose(dq[g, t] * scale).astype(BF).astype(F32)
            span = slice(t * 256, t * 256 + 256)
            for hd in range(2):
                cols = slice((g * 2 + hd) * 128, (g * 2 + hd) * 128 + 128)
                q_raw = raw[2 * t : 2 * t + 2, :, cols].reshape(256, 128)
                d_raw, d_gain = prep_back(d[hd * 256 : hd * 256 + 256], q_raw, q_gain, cos[span], sin[span])
                dqkv[span, cols] = d_raw.astype(BF)
                g_q = g_q + d_gain

    def query_rows(f, _):
        lhs = xn[:, pl.ds(pl.multiple_of(f * 128, 128), 128)]
        g = dot(lhs, dqkv[:, :512], 0, 0)
        wal[lax.div(f, 4), lax.rem(f, 4), :, :, :, :512] = g.reshape(8, 2, 8, 512).astype(BF)
        return 0

    lax.fori_loop(0, 8, query_rows, 0)
    sq.start()
    so.cores()
    sb.first()
    sd.first(od)
    for k in (1, 3, 2):
        ring_wait(6, k, land3.at[k - 1])
    s = acc[...]
    for k in range(3):
        s = s + land3[k].astype(F32)
    out[...] = s.astype(BF)
    back_far.wait_recv()
    back_near.wait_recv()
    g_k = jnp.zeros((1, 128), F32)
    for g in range(2):
        d = dkv[g, 2] + land[0, g].astype(F32) + land[1, g].astype(F32)
        d = (d * scale).astype(BF).astype(F32)
        cols = slice(512 + g * 128, 640 + g * 128)
        k_raw = raw[:, :, cols].reshape(CHUNK, 128)
        d_raw, d_gain = prep_back(d, k_raw, k_gain, cos[...], sin[...])
        dqkv[:, cols] = d_raw.astype(BF)
        g_k = g_k + d_gain
        d = dkv[2 + g, 2] + land[0, 2 + g].astype(F32) + land[1, 2 + g].astype(F32)
        dqkv[:, 768 + g * 128 : 896 + g * 128] = d.astype(BF)

    for copy in first_sends:
        copy.wait_send()
    sends[:] = [copy for copy in sends if all(copy is not s for s in first_sends)]
    g_x = jnp.zeros((1, 1024), F32)
    for k in (2, 1, 3, 0):
        span = pl.ds(pl.multiple_of(wrap4(y + k) * 128, 128), 128)
        p = dot(dqkv[span], wa[:, :1024], 1, 1)
        g_x = g_x + jnp.sum(p * xn[span].astype(F32), axis=0, keepdims=True)
        if k:
            part[k - 1] = p.astype(BF)
            ring_send(7, k, part.at[k - 1], land1.at[k - 1])
        else:
            acc[...] = p
    eight = lax.div(lax.broadcasted_iota(jnp.int32, (128, 1024), 1), 8) == lax.broadcasted_iota(jnp.int32, (128, 1024), 0)
    eight = eight.astype(F32).astype(BF)
    grow[0:1] = g_x / attn_gain
    grow[2:3] = dot(jnp.broadcast_to(g_q, (8, 128)).astype(BF), eight, 1, 0)[:1]
    grow[3:4] = dot(jnp.broadcast_to(g_k, (8, 128)).astype(BF), eight, 1, 0)[:1]

    def key_rows(f, _):
        span = pl.ds(pl.multiple_of(f * 128, 128), 128)
        g = dot(xn[:, span], dqkv[:, 512:], 0, 0)
        at = (lax.div(f, 4), lax.rem(f, 4))
        wal[at[0], at[1], :, :, :, 512:1024] = g.reshape(8, 2, 8, 512).astype(BF)
        wal[at[0], at[1], :, :, :, 1024:] = jnp.transpose(grow[:, span]).reshape(8, 2, 8, 128).astype(BF)
        return 0

    lax.fori_loop(0, 8, key_rows, 0)
    sk.start()
    sq.cores()
    sk.cores()
    so.second()
    sb.owners()
    for r in range(4):
        for g in range(2):
            h = g * 4 + r
            og[:, h * 384 : h * 384 + 384] = sb.ry[r, :, g * 384 : g * 384 + 384].astype(F32)
            ou[:, h * 384 : h * 384 + 384] = sb.ry[r, :, 768 + g * 384 : 1152 + g * 384].astype(F32)
    sq.second()
    sk.second()
    so.first(oo)
    for k in (1, 3, 2):
        ring_wait(7, k, land1.at[k - 1])
    s = acc[...]
    for k in range(3):
        s = s + land1[k].astype(F32)
    own = tok[...].astype(F32)
    scale_own = rms_scale(own)
    own = own * scale_own
    s = s * attn_gain
    mean = jnp.mean(s * own, axis=-1, keepdims=True)
    igrad[...] = (dmid[...] + scale_own * (s - own * mean)).astype(BF)
    sq.first()
    sk.first()
    sq.owners()
    sk.owners()
    gain = jnp.zeros((8, 128), F32)
    for r in range(4):
        for g in range(2):
            h = g * 4 + r
            oq[:, h * 256 : h * 256 + 256] = sq.ry[r, :, g * 256 : g * 256 + 256].astype(F32)
            ok[:, h * 128 : h * 128 + 128] = sk.ry[r, :, g * 128 : g * 128 + 128].astype(F32)
            ov[:, h * 128 : h * 128 + 128] = sk.ry[r, :, 256 + g * 128 : 384 + g * 128].astype(F32)
        gain = gain + sk.ry[r, :, 512:640].astype(F32)
    ogain[...] = gain
    for copy in sends:
        copy.wait_send()
    for s in (o, sq, sk, sb, so, sd):
        s.done()


def whole_layer(tok, cot, wq, wk, wv, wg, wu, gains, wo, wd, low):
    sds = jax.ShapeDtypeStruct
    block = (128, 1024)
    mem = lambda *shape: pltpu.VMEM(shape, BF)
    mem32 = lambda *shape: pltpu.VMEM(shape, F32)
    return pl.pallas_call(
        layer_kernel,
        out_shape=(
            sds(block, BF),
            sds(block, BF),
            sds((8, 2048), F32),
            sds((8, 1024), F32),
            sds((8, 1024), F32),
            sds((8, 3072), F32),
            sds((8, 3072), F32),
            sds((16, 1024), F32),
            sds((24, 1024), F32),
            sds((8, 128), F32),
        ),
        in_specs=[VMEM] * 15,
        out_specs=(VMEM,) * 10,
        scratch_shapes=[
            mem(4, 8, 1152),
            mem(4, 8, 1536),
            mem(2, 4, 8, 2, 8, 1152),
            mem(2, 4, 8, 2, 8, 1536),
            mem(2, 1, 8, 2, 24, 1024),
            mem(2, 1, 8, 2, 16, 1024),
            mem(1024, 1152),
            mem(1024, 1536),
            mem(768, 1024),
            mem(4, *block),
            mem(4, *block),
            mem32(CHUNK, 128),
            mem32(CHUNK, 128),
            mem32(8, 1152),
            mem(CHUNK, 1024),
            mem(2, 2, 512, 128),
            mem(4, 3, CHUNK, 128),
            mem32(2, 2, 1, 512),
            mem32(2, 2, 1, 512),
            mem32(2, 2, 1, 512),
            mem32(2, 2, 128, 512),
            mem(4, 128, 512),
            mem(3, *block),
            mem(3, *block),
            mem32(*block),
            mem32(*block),
            mem32(4, 128, 768),
            mem(4, 128, 1536),
            mem(4, 128, 768),
            mem(3, *block),
            mem(3, *block),
            mem(4, *block),
            mem(3, *block),
            mem(3, *block),
            mem32(*block),
            mem(4, 128, 512),
            mem(2, 1, 8, 2, 16, 1024),
            mem(2, 2, 512, 128),
            mem32(2, 2, 1, 512),
            mem32(4, 3, CHUNK, 128),
            mem(4, 2, CHUNK, 128),
            mem(2, 4, CHUNK, 128),
            mem(CHUNK, 1024),
            mem32(128, 1024),
            DMA((8, 3)),
            DMA((8, 3)),
            DMA((4,)),
            DMA((4,)),
        ]
        + Pieces.semaphores() * 4
        + Sums.scratch(8, 512, 4)
        + Sums.scratch(8, 640, 4)
        + Sums.scratch(8, 1536, 4)
        + Sums.scratch(16, 1024, 1)
        + Sums.scratch(24, 1024, 1),
        compiler_params=params(0),
        name="whole_layer",
    )(tok, cot, wq, wk, wv, wg, wu, gains, wo, wd, low, *rope_tables())


def results_kernel(*refs):
    half = len(refs) // 2
    for src, dst in zip(refs[:half], refs[half:]):
        dst[...] = src[...]


def results(*arrays):
    return pl.pallas_call(
        results_kernel,
        out_shape=tuple(jax.ShapeDtypeStruct(r.shape, r.dtype) for r in arrays),
        in_specs=[VMEM] * len(arrays),
        out_specs=(VMEM,) * len(arrays),
        name="results",
    )(*arrays)


def first_keys(segments):
    padded = jnp.concatenate([jnp.full((2 * CHUNK,), -1, jnp.int32), segments])
    keys = lax.dynamic_slice_in_dim(padded, chunk_number() * CHUNK, 3 * CHUNK, 0)
    begins = jnp.sum((keys[:, None] < keys[None, 2 * CHUNK :]).astype(jnp.int32), axis=0)
    low = jnp.maximum(begins, jnp.arange(1, CHUNK + 1, dtype=jnp.int32)).reshape(2, 1, 256)
    return jnp.concatenate([low, low], axis=2)


def local(
    tokens, cotangent, segments, attn_gain, w_query, key_matrix, value_matrix, query_gain, key_gain,
    w_out, ffn_gain, w_gate, w_up, w_down,
):
    low = first_keys(segments)
    gains = jnp.stack(
        [attn_gain, ffn_gain, jnp.broadcast_to(query_gain, (8,)), jnp.broadcast_to(key_gain, (8,))], axis=1
    )
    gains = jnp.pad(gains, ((0, 0), (0, 124)))
    output, input_grad, g_query, g_key, g_value, g_gate, g_up, g_out, g_down, g_gains = results(
        *whole_layer(
            tokens, cotangent, w_query, key_matrix, value_matrix, w_gate, w_up, gains, w_out, w_down, low
        )
    )
    return (
        output,
        input_grad,
        g_gains[:, 0],
        g_query,
        g_key,
        g_value,
        g_gains[0, 2:3],
        g_gains[0, 3:4],
        g_out,
        g_gains[:, 1],
        g_gate,
        g_up,
        g_down,
    )


def solution(mesh):
    rows = P(("blk", "head"), None)
    cut = P(("head", "blk"), None)
    vec = P(("head", "blk"))
    return jax.shard_map(
        local,
        mesh=mesh,
        in_specs=(rows, rows, P(), vec, cut, cut, cut, vec, vec, cut, vec, cut, cut, cut),
        out_specs=(rows, rows, vec, cut, cut, cut, vec, vec, cut, vec, cut, cut, cut),
        check_vma=False,
    )
```

time: 227 us -> 184 us (0.81); the launches traced: 223 us -> 184 us
  Pallas kernels: 204 us -> 174 us
  local copies, waits for them, and re-layouts: 16.6 us -> 6.56 us
    pallas_call x3 -> x2, Pallas kernels: 204 us -> 174 us  [the longest x1 172 us: whole_layer(): pl.pallas_call(layer_kernel, out_shape=(sds(block, BF), sds(block, BF), s...]
    unnamed x17 -> x0, local copies, waits for them, and re-layouts: 10 us -> none
where the time goes in v4:
time: 184 us
  Pallas kernels  174 us (95%)
  local copies, waits for them, and re-layouts  6.56 us (4%)
  between operations  1.98 us (1%)
    pallas_call x1, Pallas kernels, whole_layer(): pl.pallas_call(layer_kernel, out_shape=(sds(block, BF), sds(block, BF), s...  172 us

profile of v4, /device:TPU:0, one launch (start us, length us, event | category | flops | bytes accessed | tf_op | source)
XLA Modules:
  0.0 183.6 jit_solution(13725498812496924889)
XLA Ops:
  2.0 0.1 pad.10.clone
  2.0 0.1 pad.11.clone
  2.1 0.8 pad_dynamic-slice_fusion
  2.9 0.7 copy.35
  3.6 0.7 copy.36
  4.4 0.1 maximum_maximum_fusion
  4.4 0.6 pad.5.gains
  5.0 0.8 pad_dynamic-slice_fusion.1
  5.8 0.4 convert_reduce_fusion
  6.2 0.6 pad_add_fusion.low
  6.8 171.7 %whole_layer.1 = (bf16[128,1024]{1,0:T(8,128)(2,1)}, bf16[128,1024]{1,0:T(8,128)(2,1)}, f32[8,2048]{1,0:T(8,128)}, f32[8,1024]{1,0:T(8,128)}, f32[8,1024]{1,0:T(...) custom-call(bf16[128,1024]{1,0:T(8,128)(2,1)} %tok.1, ...), custom_call_target="tpu_custom_call" | custom-call | tf_op jit(solution)/shard_map/whole_layer/pallas_call | solution.py:780
  178.5 2.2 %results.1 = (bf16[128,1024]{1,0:T(8,128)(2,1)}, bf16[128,1024]{1,0:T(8,128)(2,1)}, f32[8,2048]{1,0:T(8,128)}, f32[8,1024]{1,0:T(8,128)}, f32[8,1024]{1,0:T(8,12...) custom-call(bf16[128,1024]{1,0:T(8,128)(2,1)} %get-tuple-element.33., ...), custom_call_target="tpu_custom_call" | custom-call | tf_op jit(solution)/shard_map/results/pallas_call | solution.py:864
  180.7 1.3 fusion
  182.1 1.5 slice_reduce_fusion
  (1 shorter events, 0.0 us)

commit v5 on v4

v5 whole, which is shorter than its diff:
```python
import math

import jax
import jax.numpy as jnp
import numpy as np
from jax import lax
from jax.experimental import pallas as pl
from jax.experimental.pallas import tpu as pltpu
from jax.sharding import PartitionSpec as P

HEAD_SIZE = 128
SPAN = 1024
CHUNK = 512
EPS = 1e-06
ROPE_BASE = 1000000.0
MASKED = -1e30
MESH = pl.DeviceIdType.MESH
BF = jnp.bfloat16
F32 = jnp.float32
VMEM = pl.BlockSpec(memory_space=pltpu.VMEM)
SMEM = pl.BlockSpec(memory_space=pltpu.SMEM)
DMA = pltpu.SemaphoreType.DMA
VMEM_LIMIT = 62 * 2**20


def coords():
    h = lax.axis_index("head")
    b = lax.axis_index("blk")
    x = 2 * lax.div(h, 4) + lax.div(b, 8)
    return x, lax.rem(h, 4), lax.rem(lax.div(b, 2), 4), lax.rem(b, 2)


def device(x, y, z, c):
    return (lax.div(x, 2) * 4 + y, lax.rem(x, 2) * 8 + z * 2 + c)


def wrap4(v):
    return lax.rem(v + 8, 4)


def send(src, dst, send_sem, recv_sem, to):
    copy = pltpu.make_async_remote_copy(
        src_ref=src, dst_ref=dst, send_sem=send_sem, recv_sem=recv_sem, device_id=to, device_id_type=MESH
    )
    copy.start()
    return copy


def arrived(dst, sem, anyone):
    pltpu.make_async_remote_copy(
        src_ref=dst, dst_ref=dst, send_sem=sem, recv_sem=sem, device_id=anyone, device_id_type=MESH
    ).wait_recv()


def greet(peers):
    barrier = pltpu.get_barrier_semaphore()
    for peer in peers:
        pl.semaphore_signal(barrier, inc=1, device_id=peer, device_id_type=MESH)
    return lambda: pl.semaphore_wait(barrier, len(peers))


def params(collective_id):
    return pltpu.CompilerParams(
        collective_id=collective_id, has_side_effects=True, vmem_limit_bytes=VMEM_LIMIT
    )


def chunk_number():
    return 2 * lax.axis_index("blk") + lax.div(lax.axis_index("head"), 4)


def chunk_device(step):
    chunk = lax.rem(chunk_number() + step + 32, 32)
    return (lax.rem(chunk, 2) * 4 + lax.rem(lax.axis_index("head"), 4), lax.div(chunk, 2))


def greet_all():
    x, y, z, c = coords()
    peers = [device(x, y, z, 1 - c)]
    for j in range(4):
        for r in range(4):
            if j or r:
                peers.append(device(wrap4(x + j * (1 - c)), wrap4(y + r), wrap4(z + j * c), c))
    peers += [device(wrap4(x + k * c), y, wrap4(z + k * (1 - c)), c) for k in range(1, 4)]
    return greet(peers + [chunk_device(s) for s in (-2, -1, 1, 2)])


def dot(a, b, ca, cb):
    return lax.dot_general(a, b, (((ca,), (cb,)), ((), ())), preferred_element_type=F32)


def rms_scale(rows):
    return lax.rsqrt(jnp.mean(rows * rows, axis=-1, keepdims=True) + EPS)


def rope_tables():
    freq = ROPE_BASE ** (-np.arange(0, HEAD_SIZE, 2, dtype=np.float64) / HEAD_SIZE)
    freq = np.concatenate([freq, freq])
    sign = np.where(np.arange(HEAD_SIZE) < 64, -1.0, 1.0)
    inner = np.arange(CHUNK)[:, None] * freq[None, :]
    outer = (np.arange(32) * CHUNK)[:, None] * freq[None, :]
    tables = [f(a) * s for a in (inner, outer) for f, s in ((np.cos, 1.0), (np.sin, sign))]
    return [jnp.asarray(t.astype(np.float32)) for t in tables]


def rope_here(ic, isn, oc, osn, cos, sin):
    n = chunk_number()
    c0, s0 = oc[pl.ds(n, 1), :], osn[pl.ds(n, 1), :]
    cos[...] = c0 * ic[...] - s0 * isn[...]
    sin[...] = s0 * ic[...] + c0 * isn[...]


def rope(rows, cos, sin):
    return rows * cos + pltpu.roll(rows, 64, 1) * sin


def rope_back(rows, cos, sin):
    return rows * cos + pltpu.roll(rows * sin, 64, 1)


def prep_back(d, raw, gain, cos, sin):
    scale = rms_scale(raw)
    unit = raw * scale
    d = rope_back(d, cos, sin)
    d_gain = jnp.sum(d * unit, axis=0, keepdims=True)
    d = d * gain
    return scale * (d - unit * jnp.mean(d * unit, axis=-1, keepdims=True)), d_gain


def first_keys(seg, low):
    start = chunk_number() * 4 - 8
    rows = []
    for i in range(12):
        row = seg[pl.ds(jnp.maximum(start + i, 0), 1), :].astype(F32)
        rows.append(jnp.where(start + i < 0, -1.0, row))
    keys = jnp.transpose(jnp.concatenate(rows + [jnp.zeros((116, 128), F32)], axis=0))
    for t in range(2):
        for half in range(2):
            query = rows[8 + 2 * t + half]
            begins = jnp.zeros((1, 128), F32)
            for i in range(12):
                before = jnp.where(keys[:, i : i + 1] < query, 1.0, 0.0)
                begins = begins + jnp.sum(before, axis=0, keepdims=True)
            row = lax.broadcasted_iota(jnp.int32, (1, 128), 1) + (t * 256 + half * 128 + 1)
            for hd in range(2):
                at = hd * 256 + half * 128
                low[t, :, at : at + 128] = jnp.maximum(begins.astype(jnp.int32), row)


def gain_tile(gains):
    row = lax.broadcasted_iota(jnp.int32, (8, 128), 0)
    col = lax.broadcasted_iota(jnp.int32, (8, 128), 1)
    tile = jnp.where(col == 2, gains[16], jnp.where(col == 3, gains[17], 0.0))
    for i in range(8):
        tile = jnp.where((row == i) & (col == 0), gains[i], tile)
        tile = jnp.where((row == i) & (col == 1), gains[8 + i], tile)
    return tile.astype(BF)


REACH = (((0, 512), (256, 256)), ((0, 512), (0, 512)), ((0, 256), (0, 512)))
EXP_SCALE = HEAD_SIZE ** (-0.5) * math.log2(math.e)


def allowed(low, slot, t):
    first, count = REACH[slot][t]
    place = lax.broadcasted_iota(jnp.int32, (count, 512), 0) + (slot * CHUNK + first)
    ok = place >= low[t]
    if slot == 2:
        query = lax.rem(lax.broadcasted_iota(jnp.int32, (1, 512), 1), 256) + (t * 256 + SPAN)
        ok = ok & (place <= query)
    return ok


def attend(q, kvx, low, peak, total, acc, slot, fresh):
    def group(g, _):
        for t in range(2):
            first, count = REACH[slot][t]
            keys = kvx[2 * g, slot, first : first + count]
            values = kvx[2 * g + 1, slot, first : first + count]
            s = dot(keys, q[g, t], 1, 1)
            s = jnp.where(allowed(low, slot, t), s, MASKED)
            top = jnp.max(s, axis=0, keepdims=True)
            if not fresh:
                before = peak[g, t]
                top = jnp.maximum(top, before)
                fade = jnp.exp2((before - top) * EXP_SCALE)
            p = jnp.exp2((s - top) * EXP_SCALE)
            add = jnp.sum(p, axis=0, keepdims=True)
            o = dot(values, p.astype(BF), 0, 0)
            if not fresh:
                add = add + total[g, t] * fade
                o = o + acc[g, t] * fade
            peak[g, t] = top
            total[g, t] = add
            acc[g, t] = o
        return 0

    lax.fori_loop(0, 2, group, 0)


def attend_back(q, kvx, low, lse, do, inner, dq, dkv, slot, fresh, after=None):
    def group(g, _):
        for t in range(2):
            first, count = REACH[slot][t]
            rows = slice(first, first + count)
            keys = kvx[2 * g, slot, rows]
            values = kvx[2 * g + 1, slot, rows]
            s = dot(keys, q[g, t], 1, 1)
            p = jnp.where(allowed(low, slot, t), jnp.exp2(s * EXP_SCALE - lse[g, t]), 0.0)
            dp = dot(values, do[g, t], 1, 1)
            ds = (p * (dp - inner[g, t])).astype(BF)
            dv = dot(p.astype(BF), do[g, t], 1, 0)
            dk = dot(ds, q[g, t], 1, 0)
            for n, d in ((2 * g, dk), (2 * g + 1, dv)):
                if t == 0:
                    dkv[n, slot, rows] = d
                elif slot == 2:
                    dkv[n, slot, :256] = dkv[n, slot, :256] + d[:256]
                    dkv[n, slot, 256:] = d[256:]
                else:
                    dkv[n, slot, rows] = dkv[n, slot, rows] + d
            d = dot(keys, ds, 0, 0)
            dq[g, t] = d if fresh else dq[g, t] + d
        return 0

    if after is None:
        lax.fori_loop(0, 2, group, 0)
    else:
        for g in range(2):
            group(g, 0)
            after(g)


LOW, HIGH = pl.ds(0, 64), pl.ds(64, 64)


class Ring:
    def __init__(self, ssem, rsem):
        x, self.y, z, c = coords()
        self.next = device(x, wrap4(self.y + 1), z, c)
        self.last = device(x, wrap4(self.y + 3), z, c)
        self.ssem, self.rsem = ssem, rsem
        self.sends = []

    def send(self, n, src, dst, to):
        self.sends.append(send(src, dst, self.ssem.at[n], self.rsem.at[n], to))

    def wait(self, n, dst):
        arrived(dst, self.rsem.at[n], self.next)

    def done(self):
        for copy in self.sends:
            copy.wait_send()
        self.sends = []


class RingGather(Ring):
    def __init__(self, ref, ssem, rsem):
        super().__init__(ssem, rsem)
        self.ref = ref

    def half(self, back, rows):
        return self.ref.at[wrap4(self.y - back), rows]

    def start(self):
        low, high = self.half(0, LOW), self.half(0, HIGH)
        self.send(0, low, low, self.next)
        self.send(1, high, high, self.last)
        self.send(2, high, high, self.next)
        self.send(3, low, low, self.last)

    def pass_on(self):
        low, high = self.half(1, LOW), self.half(3, HIGH)
        self.wait(0, low)
        self.send(4, low, low, self.next)
        self.wait(1, high)
        self.send(5, high, high, self.last)

    def block(self, back):
        if back == 1:
            self.wait(2, self.half(1, HIGH))
        elif back == 3:
            self.wait(3, self.half(3, LOW))
        elif back == 2:
            self.wait(4, self.half(2, LOW))
            self.wait(5, self.half(2, HIGH))


class RingSum(Ring):
    def __init__(self, part, relayed, landed, ssem, rsem):
        super().__init__(ssem, rsem)
        self.part, self.relayed, self.landed = part, relayed, landed

    def give(self, k):
        part = self.part.at[k - 1]
        if k == 2:
            self.send(0, part.at[LOW], self.relayed.at[0], self.next)
            self.send(1, part.at[HIGH], self.relayed.at[1], self.last)
        elif k == 1:
            self.send(2, part.at[HIGH], self.landed.at[0, HIGH], self.next)
        else:
            self.send(3, part.at[LOW], self.landed.at[1, LOW], self.last)

    def relay(self):
        part, relayed, landed = self.part, self.relayed, self.landed
        self.wait(0, relayed.at[0])
        part[0, :64] = (part[0, :64].astype(F32) + relayed[0].astype(F32)).astype(BF)
        self.send(4, part.at[0, LOW], landed.at[0, LOW], self.next)
        self.wait(1, relayed.at[1])
        part[2, 64:] = (part[2, 64:].astype(F32) + relayed[1].astype(F32)).astype(BF)
        self.send(5, part.at[2, HIGH], landed.at[1, HIGH], self.last)

    def total(self, own):
        landed = self.landed
        self.wait(2, landed.at[0, HIGH])
        self.wait(3, landed.at[1, LOW])
        self.wait(4, landed.at[0, LOW])
        self.wait(5, landed.at[1, HIGH])
        return own + landed[0].astype(F32) + landed[1].astype(F32)


class Pieces:
    def __init__(self, ref, ssem, rsem):
        self.ref, self.wide, self.ssem, self.rsem = ref, ref.shape[1] == 4, ssem, rsem
        self.x, self.y, self.z, self.c = x, y, z, c = coords()
        self.d = 1 - c
        self.across = device(x, y, z, 1 - c)
        self.sends = []

    @staticmethod
    def semaphores():
        return [DMA((44,)), DMA((44,))]

    def slot(self, px, pz, core):
        place = lax.rem(px, 2) * 4 + pz
        if self.wide:
            return self.ref.at[lax.div(px, 2), :, place, core]
        return self.ref.at[lax.div(px, 2), 0, place, core]

    def back(self, j, k):
        c, d = self.c, self.d
        return wrap4(self.x - j * d - k * c), wrap4(self.z - j * c - k * d)

    def piece(self, j, k):
        return self.slot(*self.back(j, k), self.c)

    def piece_across(self, j, k):
        c, d = self.c, self.d
        return self.slot(wrap4(self.x - j * c - k * d), wrap4(self.z - j * d - k * c), d)

    def send(self, src, dst, n, to):
        self.sends.append(send(src, dst, self.ssem.at[n], self.rsem.at[n], to))

    def ahead(self, j, k, r=0):
        px, pz = self.back(-j, -k)
        return device(px, wrap4(self.y + r), pz, self.c)

    def from_source(self, j, r):
        px, pz = self.back(j, 0)
        return self.ref.at[lax.div(px, 2), wrap4(self.y - r) if self.wide else 0, lax.rem(px, 2) * 4 + pz, self.c]

    def start(self, parts):
        here = self.from_source(0, 0)
        for j in (2, 1, 3, 0):
            for r in (2, 1, 3, 0) if self.wide else (0,):
                if j or r:
                    src = parts.at[wrap4(self.y + r)] if self.wide else parts
                    self.send(src, here, 4 * j + r, self.ahead(j, 0, r))
        px, pz = self.back(0, 0)
        if self.wide:
            self.ref[lax.div(px, 2), self.y, lax.rem(px, 2) * 4 + pz, self.c] = parts[self.y]
        else:
            self.ref[lax.div(px, 2), 0, lax.rem(px, 2) * 4 + pz, self.c] = parts[...]

    def pass_on(self, j):
        for r in range(4) if self.wide else (0,):
            if j or r:
                arrived(self.from_source(j, r), self.rsem.at[4 * j + r], self.across)
        here = self.piece(j, 0)
        for k in (2, 1, 3):
            self.send(here, here, 15 + 3 * j + k, self.ahead(0, k))
        self.send(here, here, 28 + 4 * j, self.across)

    def pass_across(self, j, k):
        here = self.piece(j, k)
        arrived(here, self.rsem.at[15 + 3 * j + k], self.across)
        self.send(here, here, 28 + 4 * j + k, self.across)

    def pass_all_on(self):
        for j in (0, 1, 3, 2):
            self.pass_on(j)

    def pass_all_across(self):
        for j in (0, 1, 3, 2):
            for k in (1, 3, 2):
                self.pass_across(j, k)

    def all_here(self):
        for j in range(4):
            for k in range(4):
                arrived(self.piece_across(j, k), self.rsem.at[28 + 4 * j + k], self.across)

    def done(self):
        for copy in self.sends:
            copy.wait_send()


def pack_wide(src, dst):
    cols = src.shape[-1]

    def rows(i, _):
        part = src[lax.div(i, 4), lax.rem(i, 4)].astype(F32).reshape(128, cols)
        dst[pl.ds(pl.multiple_of(i * 128, 128), 128)] = part.astype(BF)
        return 0

    lax.fori_loop(0, 8, rows, 0)


def pack_down(src, dst):
    def rows(i, _):
        part = src[lax.div(i, 4), 0, pl.ds(lax.rem(i, 4) * 2, 2)].astype(F32).reshape(96, 1024)
        dst[pl.ds(pl.multiple_of(i * 96, 96), 96)] = part.astype(BF)
        return 0

    lax.fori_loop(0, 8, rows, 0)


class Sums:
    def __init__(self, grad, refs):
        self.grad, self.cut = grad, grad.shape[1]
        (self.rc, self.sa, self.lb, self.sb, self.lg, self.ss, self.rs) = refs
        x, y, z, c = coords()
        self.y, self.c, self.d = y, c, 1 - c
        d = self.d
        self.across = device(x, y, z, d)
        self.ahead = lambda j, k, r: device(wrap4(x + j * d + k * c), wrap4(y + r), wrap4(z + j * c + k * d), c)
        self.p1 = x * d + z * c
        self.p2 = x * c + z * d
        self.sends = []

    @staticmethod
    def scratch(rows, cols, cut):
        buffers = [(2, cut, 8), (4, 4, cut), (3, 4, cut), (4, cut), (4, cut)]
        return [pltpu.VMEM(lead + (rows, cols), BF) for lead in buffers] + [DMA((20,)), DMA((20,))]

    def send(self, src, dst, n, to):
        self.sends.append(send(src, dst, self.ss.at[n], self.rs.at[n], to))

    def start(self):
        self.send(self.grad.at[:, :, :, self.d], self.rc, 0, self.across)

    def cores(self):
        arrived(self.rc, self.rs.at[0], self.across)
        c, d, cut = self.c, self.d, self.cut

        def add(i, _):
            a2, a1, r = lax.div(i, 4 * cut), lax.rem(lax.div(i, cut), 4), lax.rem(i, cut)
            px, pz = a1 * d + a2 * c, a1 * c + a2 * d
            xh, place = lax.div(px, 2), lax.rem(px, 2) * 4 + pz
            total = self.rc[xh, r, place].astype(F32) + self.grad[xh, r, place, c].astype(F32)
            self.sa[a2, a1, r] = total.astype(BF)
            return 0

        lax.fori_loop(0, 16 * cut, add, 0)
        for k in (2, 1, 3):
            self.send(self.sa.at[wrap4(self.p2 + k)], self.lb.at[k - 1], k, self.ahead(0, k, 0))

    def second(self):
        for k in (1, 3, 2):
            arrived(self.lb.at[k - 1], self.rs.at[k], self.across)

        def add(i, _):
            a1, r = lax.div(i, self.cut), lax.rem(i, self.cut)
            total = self.sa[self.p2, a1, r].astype(F32)
            for k in range(3):
                total = total + self.lb[k, a1, r].astype(F32)
            self.sb[a1, r] = total.astype(BF)
            return 0

        lax.fori_loop(0, 4 * self.cut, add, 0)
        for j in (2, 1, 3, 0):
            for r in (2, 1, 3, 0) if self.cut > 1 else (0,):
                if j or r:
                    src = self.sb.at[wrap4(self.p1 + j), wrap4(self.y + r) if self.cut > 1 else 0]
                    self.send(src, self.lg.at[j, r], 4 + 4 * j + r, self.ahead(j, 0, r))
        if self.cut > 1:
            self.lg[0, 0] = self.sb[self.p1, self.y]
        else:
            self.lg[0, 0] = self.sb[self.p1, 0]

    def last(self, r=0):
        total = 0.0
        for j in range(4):
            if j or r:
                arrived(self.lg.at[j, r], self.rs.at[4 + 4 * j + r], self.across)
            total = total + self.lg[j, r].astype(F32)
        return total

    def done(self):
        for copy in self.sends:
            copy.wait_send()


def layer_kernel(
    tok, cot, wq, wk, wv, wg, wu, gains, wop, wdp, seg, ic, isn, oc, osn,
    out, igrad, oq, ok, ov, og, ou, oo, od, ogain,
    kparts, qparts, bparts, wkl, wql, wbl, wdl, wol, wkv, wqs, wb, wd, low, xs, cs, cos, sin, rows, xn, q, kvx, lse,
    peak, total, wide, att, part, relay1, land1, acc, unit, dhid, dgu, hid, dpart, relay2, land2, dbr, opart, scale_two, land3,
    dmid, datt, go, do, inner, dkv, dkvb, land, dqkv, grow, dxq, rsend, rrecv, ssem, rsem, hsem, hrem, *scratch,
):
    x, y, z, c = coords()
    ring = [device(x, wrap4(y + k), z, c) for k in range(1, 4)]
    take = lambda n: [scratch.pop(0) for _ in range(n)]
    scratch = list(scratch)
    kv, qw, b, o, w = [Pieces(ref, *take(2)) for ref in (wkl, wql, wbl, wol, wdl)]
    sq, sk, sb, so, sd = [Sums(ref, take(7)) for ref in (wql, wkl, wbl, go, wdl)]
    sends = []

    def ring_send(n, k, src, dst):
        sends.append(send(src, dst, ssem.at[n, k - 1], rsem.at[n, k - 1], ring[k - 1]))
        return sends[-1]

    def ring_wait(n, k, dst):
        arrived(dst, rsem.at[n, k - 1], ring[0])

    mid = xs
    tokens_in = RingGather(xs, rsend.at[0], rrecv.at[0])
    sum_out = RingSum(part, relay1, land1, rsend.at[1], rrecv.at[1])
    mid_in = RingGather(mid, rsend.at[2], rrecv.at[2])
    sum_mid = RingSum(dpart, relay2, land2, rsend.at[3], rrecv.at[3])
    branch_in = RingGather(dbr, rsend.at[4], rrecv.at[4])
    sum_x = RingSum(part, relay1, land1, rsend.at[5], rrecv.at[5])

    everyone = greet_all()
    for r in range(4):
        for g in range(2):
            h = g * 4 + r
            kparts[r, :, g * 256 : 128 + g * 256] = wk[:, h * 128 : h * 128 + 128]
            kparts[r, :, 128 + g * 256 : 256 + g * 256] = wv[:, h * 128 : h * 128 + 128]
            qparts[r, :, g * 256 : g * 256 + 256] = wq[:, h * 256 : h * 256 + 256]
        kparts[r, :, 512:] = gain_tile(gains)
    xs[y] = tok[...]
    everyone()
    kv.start(kparts)
    tokens_in.start()
    qw.start(qparts)
    for r in range(4):
        for g in range(2):
            h = g * 4 + r
            bparts[r, :, g * 384 : g * 384 + 384] = wg[:, h * 384 : h * 384 + 384]
            bparts[r, :, 768 + g * 384 : 1152 + g * 384] = wu[:, h * 384 : h * 384 + 384]
    o.start(wop)
    cs[y] = cot[...]
    first_keys(seg, low)
    rope_here(ic, isn, oc, osn, cos, sin)
    kv.pass_all_on()
    tokens_in.pass_on()
    qw.pass_all_on()
    kv.pass_all_across()
    kv.all_here()
    o.pass_all_on()
    b.start(bparts)
    w.start(wdp)
    pack_wide(wkl, wkv)
    for back in (1, 3, 2):
        tokens_in.block(back)

    pick = lax.broadcasted_iota(jnp.int32, (8, 128), 0) == lax.broadcasted_iota(jnp.int32, (8, 128), 1)
    by_row = dot(pick.astype(F32).astype(BF), wkv[:, 512:], 1, 1)
    rows[:, :1024] = by_row
    every = lax.broadcasted_iota(jnp.int32, (1024, 128), 0) == 8 * lax.broadcasted_iota(jnp.int32, (1024, 128), 1)
    rows[:, 1024:] = dot(by_row.astype(BF), every.astype(F32).astype(BF), 1, 0)
    attn_gain, ffn_gain = rows[0:1, :1024], rows[1:2, :1024]
    q_gain, k_gain = rows[2:3, 1024:], rows[3:4, 1024:]

    for r in range(4):
        block = xs[r].astype(F32)
        xn[r * 128 : r * 128 + 128] = (block * rms_scale(block) * attn_gain).astype(BF)
    near, far = [], []
    for g in range(2):
        raw = dot(xn[...], wkv[:, g * 256 : g * 256 + 256], 1, 0)
        k_raw = raw[:, :128]
        kvx[2 * g, 2] = rope(k_raw * rms_scale(k_raw) * k_gain, cos[...], sin[...]).astype(BF)
        kvx[2 * g + 1, 2] = raw[:, 128:].astype(BF)
        pair = pl.ds(2 * g, 2)
        near.append(send(kvx.at[pair, 2], kvx.at[pair, 1], hsem.at[g], hrem.at[g], chunk_device(1)))
        far.append(send(kvx.at[pair, 2], kvx.at[pair, 0], hsem.at[2 + g], hrem.at[2 + g], chunk_device(2)))
    sends += near + far
    for n in (2, 1, 3):
        ring_send(1, n, cot, cs.at[y])
    qw.pass_all_across()
    qw.all_here()
    pack_wide(wql, wqs)

    def queries(g, _):
        raw = dot(xn[...], wqs[:, pl.ds(pl.multiple_of(g * 256, 256), 256)], 1, 0)
        for hd in range(2):
            q_raw = raw[:, hd * 128 : hd * 128 + 128]
            rot = rope(q_raw * rms_scale(q_raw) * q_gain, cos[...], sin[...]).astype(BF)
            for t in range(2):
                q[g, t, hd * 256 : hd * 256 + 256] = rot[t * 256 : t * 256 + 256]
        return 0

    lax.fori_loop(0, 2, queries, 0)

    attend(q, kvx, low, peak, total, wide, 2, True)
    o.pass_all_across()
    for copy in far:
        copy.wait_recv()
    attend(q, kvx, low, peak, total, wide, 0, False)
    for copy in near:
        copy.wait_recv()
    b.pass_all_on()
    w.pass_all_on()
    attend(q, kvx, low, peak, total, wide, 1, False)
    for g in range(2):
        for t in range(2):
            done = jnp.transpose(wide[g, t] / total[g, t]).astype(BF)
            lse[g, t] = peak[g, t] * EXP_SCALE + jnp.log(total[g, t]) * math.log2(math.e)
            for hd in range(2):
                cols = slice((g * 2 + hd) * 128, (g * 2 + hd) * 128 + 128)
                for half in range(2):
                    first = hd * 256 + half * 128
                    att[2 * t + half, :, cols] = done[first : first + 128]

    o.all_here()
    wo = lambda: wol[...].reshape(512, 1024)
    tokens_in.done()
    for n in (2, 1, 3, 0):
        p = dot(att[wrap4(y + n)], wo(), 1, 0)
        if n:
            part[n - 1] = p.astype(BF)
            sum_out.give(n)
        else:
            acc[...] = p + tok[...].astype(F32)
    sum_out.relay()
    b.pass_all_across()
    s = sum_out.total(acc[...])
    acc[...] = s
    scale = rms_scale(s)
    scale_two[...] = scale
    unit[...] = s * scale
    mid[y] = (s * scale * ffn_gain).astype(BF)
    mid_in.start()
    b.all_here()
    pack_wide(wbl, wb)
    mid_in.pass_on()
    w.pass_all_across()
    w.all_here()
    pack_down(wdl, wd)
    for n in (1, 3, 2):
        ring_wait(1, n, cs.at[wrap4(y - n)])
    for r in range(4):
        dhid[r] = dot(cs[r], wd[...], 1, 1)

    for k in (0, 1, 3, 2):
        r = wrap4(y - k)
        if k:
            mid_in.block(k)
        gu = dot(mid[r], wb[...], 1, 0)
        gate, up = gu[:, :768], gu[:, 768:]
        sig = 1.0 / (1.0 + jnp.exp(-gate))
        act = gate * sig
        dh = dhid[r]
        hid[r] = (act * up).astype(BF)
        dgu[r, :, :768] = (dh * up * sig * (1.0 + gate * (1.0 - sig))).astype(BF)
        dgu[r, :, 768:] = (dh * act).astype(BF)
        p = dot(dgu[r], wb[...], 1, 1)
        if k:
            dpart[3 - k] = p.astype(BF)
            sum_mid.give(4 - k)
        else:
            dmid[...] = p
    b.done()
    w.done()

    def gate_up_rows(f, _):
        span = pl.ds(pl.multiple_of(f * 128, 128), 128)
        lhs = mid[:, :, span].reshape(CHUNK, 128)
        g = dot(lhs, dgu[...].reshape(CHUNK, 1536), 0, 0)
        wbl[lax.div(f, 4), lax.rem(f, 4)] = g.reshape(8, 2, 8, 1536).astype(BF)
        return 0

    lax.fori_loop(0, 8, gate_up_rows, 0)
    sb.start()

    def down_rows(f, _):
        span = pl.ds(pl.multiple_of(f * 384, 384), 384)
        lhs = hid[:, :, span].reshape(CHUNK, 384)
        g = dot(lhs, cs[...].reshape(CHUNK, 1024), 0, 0)
        wdl[f, 0] = g.reshape(8, 2, 24, 1024).astype(BF)
        return 0

    lax.fori_loop(0, 2, down_rows, 0)
    sd.start()
    sum_mid.relay()
    sb.cores()
    for n in (2, 1, 3, 0):
        p = dot(hid[wrap4(y + n)], wd[...], 1, 0)
        if n:
            opart[n - 1] = p.astype(BF)
        else:
            acc[...] = acc[...] + p
    sd.cores()

    s = sum_mid.total(dmid[...])
    grow[...] = jnp.zeros_like(grow)
    grow[1:2] = jnp.sum(s * unit[...], axis=0, keepdims=True)
    s = s * ffn_gain
    mean = jnp.mean(s * unit[...], axis=-1, keepdims=True)
    s = cs[y].astype(F32) + scale_two[...] * (s - unit[...] * mean)
    dmid[...] = s
    dbr[y] = s.astype(BF)
    branch_in.start()

    branch_in.pass_on()
    sb.second()
    sd.second()
    for k in (0, 1, 3, 2):
        r = wrap4(y - k)
        if k:
            branch_in.block(k)
        datt[r] = dot(dbr[r], wo(), 1, 1).astype(BF)
    for k in (2, 1, 3):
        ring_send(0, k, opart.at[k - 1], land3.at[k - 1])

    ones = jnp.ones((8, 128), BF)
    for g in range(2):
        for t in range(2):
            for hd in range(2):
                cols = slice((g * 2 + hd) * 128, (g * 2 + hd) * 128 + 128)
                for half in range(2):
                    first = hd * 256 + half * 128
                    d = datt[2 * t + half, :, cols]
                    do[g, t, first : first + 128] = d
                    prod = d.astype(F32) * att[2 * t + half, :, cols].astype(F32)
                    high = prod.astype(BF)
                    rest = (prod - high.astype(F32)).astype(BF)
                    inner[g, t, :, first : first + 128] = (dot(ones, high, 1, 1) + dot(ones, rest, 1, 1))[:1]
    dq = wide
    back_near, back_far = [], []

    def give_back(g, slot, step, copies):
        pair = pl.ds(2 * g, 2)
        dkvb[2 * g : 2 * g + 2, slot] = dkv[2 * g : 2 * g + 2, slot].astype(BF)
        n = 4 + 2 * slot + g
        copies.append(send(dkvb.at[pair, slot], land.at[slot, pair], hsem.at[n], hrem.at[n], chunk_device(step)))

    attend_back(q, kvx, low, lse, do, inner, dq, dkv, 1, True, lambda g: give_back(g, 1, -1, back_near))
    attend_back(q, kvx, low, lse, do, inner, dq, dkv, 0, False, lambda g: give_back(g, 0, -2, back_far))
    sends += back_near + back_far

    def out_rows(f, _):
        span = pl.ds(pl.multiple_of(f * 256, 256), 256)
        lhs = att[:, :, span].reshape(CHUNK, 256)
        g = dot(lhs, dbr[...].reshape(CHUNK, 1024), 0, 0)
        go[f, 0] = g.reshape(8, 2, 16, 1024).astype(BF)
        return 0

    lax.fori_loop(0, 2, out_rows, 0)
    so.start()
    attend_back(q, kvx, low, lse, do, inner, dq, dkv, 2, False)

    scale = HEAD_SIZE ** (-0.5)
    raw = dhid
    raw[:, :, :512] = dot(xn[...], wqs[...], 1, 0).reshape(4, 128, 512)
    for g in range(2):
        raw[:, :, 512 + g * 128 : 640 + g * 128] = dot(xn[...], wkv[:, g * 256 : g * 256 + 128], 1, 0).reshape(4, 128, 128)
    kv.done()
    qw.done()
    g_q = jnp.zeros((1, 128), F32)
    for g in range(2):
        for t in range(2):
            d = jnp.transpose(dq[g, t] * scale).astype(BF).astype(F32)
            span = slice(t * 256, t * 256 + 256)
            for hd in range(2):
                cols = slice((g * 2 + hd) * 128, (g * 2 + hd) * 128 + 128)
                q_raw = raw[2 * t : 2 * t + 2, :, cols].reshape(256, 128)
                d_raw, d_gain = prep_back(d[hd * 256 : hd * 256 + 256], q_raw, q_gain, cos[span], sin[span])
                dqkv[span, cols] = d_raw.astype(BF)
                g_q = g_q + d_gain

    def query_rows(f, _):
        span = pl.ds(pl.multiple_of(f * 128, 128), 128)
        g = dot(xn[:, span], dqkv[:, :512], 0, 0)
        wql[lax.div(f, 4), lax.rem(f, 4)] = g.reshape(8, 2, 8, 512).astype(BF)
        of_gain = jnp.sum(g * wqs[span].astype(F32), axis=1, keepdims=True)
        grow[4:5, span] = jnp.transpose(jnp.broadcast_to(of_gain, (128, 128)))[:1]
        return 0

    lax.fori_loop(0, 8, query_rows, 0)
    sq.start()
    for r in range(4):
        dxq[r] = dot(dqkv[r * 128 : r * 128 + 128, :512], wqs[...], 1, 1)
    so.cores()
    sq.cores()
    for n in (1, 3, 2):
        ring_wait(0, n, land3.at[n - 1])
    s = acc[...]
    for n in range(3):
        s = s + land3[n].astype(F32)
    out[...] = s.astype(BF)
    for r in range(4):
        gate_up = sb.last(r)
        h = wrap4(y - r)
        for g in range(2):
            span = pl.ds(pl.multiple_of((g * 4 + h) * 384, 128), 384)
            og[:, span] = gate_up[:, g * 384 : g * 384 + 384]
            ou[:, span] = gate_up[:, 768 + g * 384 : 1152 + g * 384]
    od[...] = sd.last()
    sum_out.done()
    for copy in back_near + back_far:
        copy.wait_recv()
    g_k = jnp.zeros((1, 128), F32)
    for g in range(2):
        d = dkv[2 * g, 2] + land[0, 2 * g].astype(F32) + land[1, 2 * g].astype(F32)
        d = (d * scale).astype(BF).astype(F32)
        cols = slice(512 + g * 256, 640 + g * 256)
        k_raw = raw[:, :, 512 + g * 128 : 640 + g * 128].reshape(CHUNK, 128)
        d_raw, d_gain = prep_back(d, k_raw, k_gain, cos[...], sin[...])
        dqkv[:, cols] = d_raw.astype(BF)
        g_k = g_k + d_gain
        d = dkv[2 * g + 1, 2] + land[0, 2 * g + 1].astype(F32) + land[1, 2 * g + 1].astype(F32)
        dqkv[:, 640 + g * 256 : 768 + g * 256] = d.astype(BF)

    eight = lax.div(lax.broadcasted_iota(jnp.int32, (128, 1024), 1), 8) == lax.broadcasted_iota(jnp.int32, (128, 1024), 0)
    eight = eight.astype(F32).astype(BF)
    grow[2:3] = dot(jnp.broadcast_to(g_q, (8, 128)).astype(BF), eight, 1, 0)[:1]
    grow[3:4] = dot(jnp.broadcast_to(g_k, (8, 128)).astype(BF), eight, 1, 0)[:1]

    def key_rows(f, _):
        span = pl.ds(pl.multiple_of(f * 128, 128), 128)
        g = dot(xn[:, span], dqkv[:, 512:], 0, 0)
        at = (lax.div(f, 4), lax.rem(f, 4))
        wkl[at[0], at[1], :, :, :, :512] = g.reshape(8, 2, 8, 512).astype(BF)
        w_rows = wkv[span].astype(F32)
        tile = jnp.transpose(jnp.concatenate([grow[:, span], jnp.zeros((120, 128), F32)], axis=0))
        d_gain = (tile[:, 4:5] + jnp.sum(g * w_rows[:, :512], axis=1, keepdims=True)) / w_rows[:, 512:513]
        lane = lax.broadcasted_iota(jnp.int32, (128, 128), 1)
        tile = jnp.where(lane == 0, d_gain, tile)
        wkl[at[0], at[1], :, :, :, 512:] = tile.reshape(8, 2, 8, 128).astype(BF)
        return 0

    lax.fori_loop(0, 8, key_rows, 0)
    sk.start()

    for n in (2, 1, 3, 0):
        r = wrap4(y + n)
        span = pl.ds(pl.multiple_of(r * 128, 128), 128)
        if n == 0:
            sk.cores()
            sum_x.relay()
        p = dxq[r] + dot(dqkv[span, 512:], wkv[:, :512], 1, 1)
        if n:
            part[n - 1] = p.astype(BF)
            sum_x.give(n)
        else:
            acc[...] = p
    so.second()
    sq.second()
    sk.second()
    s = sum_x.total(acc[...])
    own = tok[...].astype(F32)
    scale_own = rms_scale(own)
    own = own * scale_own
    s = s * attn_gain
    mean = jnp.mean(s * own, axis=-1, keepdims=True)
    igrad[...] = (dmid[...] + scale_own * (s - own * mean)).astype(BF)
    oo[...] = so.last()
    gain = jnp.zeros((8, 128), F32)
    for r in range(4):
        h = wrap4(y - r)
        queries_ = sq.last(r)
        keys_ = sk.last(r)
        for g in range(2):
            span = pl.ds(pl.multiple_of((g * 4 + h) * 128, 128), 128)
            oq[:, pl.ds(pl.multiple_of((g * 4 + h) * 256, 128), 256)] = queries_[:, g * 256 : g * 256 + 256]
            ok[:, span] = keys_[:, g * 256 : g * 256 + 128]
            ov[:, span] = keys_[:, g * 256 + 128 : g * 256 + 256]
        gain = gain + keys_[:, 512:640]
    ogain[...] = gain
    for copy in sends:
        copy.wait_send()
    for s in (o, sq, sk, sb, so, sd, tokens_in, mid_in, sum_mid, branch_in, sum_x):
        s.done()


def whole_layer(tok, cot, wq, wk, wv, wg, wu, gains, wo, wd, segments):
    sds = jax.ShapeDtypeStruct
    block = (128, 1024)
    mem = lambda *shape: pltpu.VMEM(shape, BF)
    mem32 = lambda *shape: pltpu.VMEM(shape, F32)
    return pl.pallas_call(
        layer_kernel,
        out_shape=(
            sds(block, BF),
            sds(block, BF),
            sds((8, 2048), F32),
            sds((8, 1024), F32),
            sds((8, 1024), F32),
            sds((8, 3072), F32),
            sds((8, 3072), F32),
            sds((16, 1024), F32),
            sds((24, 1024), F32),
            sds((8, 128), F32),
        ),
        in_specs=[VMEM] * 7 + [SMEM] + [VMEM] * 7,
        out_specs=(VMEM,) * 10,
        scratch_shapes=[
            mem(4, 8, 640),
            mem(4, 8, 512),
            mem(4, 8, 1536),
            mem(2, 4, 8, 2, 8, 640),
            mem(2, 4, 8, 2, 8, 512),
            mem(2, 4, 8, 2, 8, 1536),
            mem(2, 1, 8, 2, 24, 1024),
            mem(2, 1, 8, 2, 16, 1024),
            mem(1024, 640),
            mem(1024, 512),
            mem(1024, 1536),
            mem(768, 1024),
            pltpu.VMEM((2, 1, 512), jnp.int32),
            mem(4, *block),
            mem(4, *block),
            mem32(CHUNK, 128),
            mem32(CHUNK, 128),
            mem32(8, 1152),
            mem(CHUNK, 1024),
            mem(2, 2, 512, 128),
            mem(4, 3, CHUNK, 128),
            mem32(2, 2, 1, 512),
            mem32(2, 2, 1, 512),
            mem32(2, 2, 1, 512),
            mem32(2, 2, 128, 512),
            mem(4, 128, 512),
            mem(3, *block),
            mem(2, 64, 1024),
            mem(2, *block),
            mem32(*block),
            mem32(*block),
            mem32(4, 128, 768),
            mem(4, 128, 1536),
            mem(4, 128, 768),
            mem(3, *block),
            mem(2, 64, 1024),
            mem(2, *block),
            mem(4, *block),
            mem(3, *block),
            mem32(128, 1),
            mem(3, *block),
            mem32(*block),
            mem(4, 128, 512),
            mem(2, 1, 8, 2, 16, 1024),
            mem(2, 2, 512, 128),
            mem32(2, 2, 1, 512),
            mem32(4, 3, CHUNK, 128),
            mem(4, 2, CHUNK, 128),
            mem(2, 4, CHUNK, 128),
            mem(CHUNK, 1024),
            mem32(8, 1024),
            mem32(4, *block),
            DMA((6, 6)),
            DMA((6, 6)),
            DMA((2, 3)),
            DMA((2, 3)),
            DMA((8,)),
            DMA((8,)),
        ]
        + Pieces.semaphores() * 5
        + Sums.scratch(8, 512, 4)
        + Sums.scratch(8, 640, 4)
        + Sums.scratch(8, 1536, 4)
        + Sums.scratch(16, 1024, 1)
        + Sums.scratch(24, 1024, 1),
        compiler_params=params(0),
        name="whole_layer",
    )(tok, cot, wq, wk, wv, wg, wu, gains, wo, wd, segments.reshape(128, 128), *rope_tables())


def results_kernel(*refs):
    ins, outs = refs[:10], refs[10:]
    for src, dst in zip(ins[:9], outs):
        dst[...] = src[...]
    gains = ins[9][...]
    row = lax.broadcasted_iota(jnp.int32, (8, 128), 0)
    col = lax.broadcasted_iota(jnp.int32, (8, 128), 1)
    for kind, dst in enumerate(outs[9:]):
        for i in range(dst.shape[0]):
            dst[i] = jnp.sum(jnp.where((row == i) & (col == kind), gains, 0.0))


def results(*arrays):
    vectors = [jax.ShapeDtypeStruct((n,), F32) for n in (8, 8, 1, 1)]
    return pl.pallas_call(
        results_kernel,
        out_shape=tuple(jax.ShapeDtypeStruct(r.shape, r.dtype) for r in arrays[:9]) + tuple(vectors),
        in_specs=[VMEM] * 10,
        out_specs=(VMEM,) * 9 + (SMEM,) * 4,
        name="results",
    )(*arrays)


def local(
    tokens, cotangent, segments, attn_gain, w_query, key_matrix, value_matrix, query_gain, key_gain,
    w_out, ffn_gain, w_gate, w_up, w_down,
):
    gains = jnp.concatenate([attn_gain, ffn_gain, query_gain, key_gain]).astype(F32)
    output, input_grad, g_query, g_key, g_value, g_gate, g_up, g_out, g_down, g_attn, g_ffn, g_qg, g_kg = results(
        *whole_layer(
            tokens, cotangent, w_query, key_matrix, value_matrix, w_gate, w_up, gains, w_out, w_down, segments
        )
    )
    return (
        output, input_grad, g_attn, g_query, g_key, g_value, g_qg, g_kg, g_out, g_ffn, g_gate, g_up, g_down,
    )


def solution(mesh):
    rows = P(("blk", "head"), None)
    cut = P(("head", "blk"), None)
    vec = P(("head", "blk"))
    return jax.shard_map(
        local,
        mesh=mesh,
        in_specs=(rows, rows, P(), vec, cut, cut, cut, vec, vec, cut, vec, cut, cut, cut),
        out_specs=(rows, rows, vec, cut, cut, cut, vec, vec, cut, vec, cut, cut, cut),
        check_vma=False,
    )
```

time: 184 us -> 162 us (0.88)
  Pallas kernels: 174 us -> 158 us
  local copies, waits for them, and re-layouts: 6.56 us -> 0.01 us
    pallas_call x1, Pallas kernels: 172 us -> 156 us  [whole_layer(): pl.pallas_call(layer_kernel, out_shape=(sds(block, BF), sds(block, BF), s...]
    slice x3 -> x0, local copies, waits for them, and re-layouts: 3.57 us -> none  [the longest x1 1.48 us: local(): g_gains[:, 1]]
where the time goes in v5:
time: 162 us; the launch traced here: 161 us
  Pallas kernels  158 us (98%)
  between operations  2.21 us (1%)
    pallas_call x1, Pallas kernels, whole_layer(): pl.pallas_call(layer_kernel, out_shape=(sds(block, BF), sds(block, BF), s...  156 us

profile of v5, /device:TPU:0, one launch (start us, length us, event | category | flops | bytes accessed | tf_op | source)
XLA Modules:
  0.0 161.2 jit_solution(16008999461429796570)
XLA Ops:
  1.3 0.0 copy-start
  1.3 0.0 copy-start.1
  2.0 0.0 copy-done
  2.0 0.0 copy-done.1
  2.0 0.6 maximum_convert_fusion.gains
  2.6 156.2 %whole_layer.1 = (bf16[128,1024]{1,0:T(8,128)(2,1)}, bf16[128,1024]{1,0:T(8,128)(2,1)}, f32[8,2048]{1,0:T(8,128)}, f32[8,1024]{1,0:T(8,128)}, f32[8,1024]{1,0:T(...) custom-call(bf16[128,1024]{1,0:T(8,128)(2,1)} %tok.1, ...), custom_call_target="tpu_custom_call" | custom-call | tf_op jit(solution)/shard_map/whole_layer/pallas_call | solution.py:893
  158.8 2.2 %results.1 = (bf16[128,1024]{1,0:T(8,128)(2,1)}, bf16[128,1024]{1,0:T(8,128)(2,1)}, f32[8,2048]{1,0:T(8,128)}, f32[8,1024]{1,0:T(8,128)}, f32[8,1024]{1,0:T(8,12...) custom-call(bf16[128,1024]{1,0:T(8,128)(2,1)} %get-tuple-element.36., ...), custom_call_target="tpu_custom_call" | custom-call | tf_op jit(solution)/shard_map/results/pallas_call | solution.py:994
Async XLA Ops:
  1.3 0.7 copy-start
  1.3 0.7 copy-start.1

commit v6 on v5

--- a/solution.py
+++ b/solution.py
@@ -103,8 +103,8 @@
     return [jnp.asarray(t.astype(np.float32)) for t in tables]
 
 
-def rope_here(ic, isn, oc, osn, cos, sin):
-    n = chunk_number()
+def rope_of(step, ic, isn, oc, osn, cos, sin):
+    n = lax.rem(chunk_number() + step + 32, 32)
     c0, s0 = oc[pl.ds(n, 1), :], osn[pl.ds(n, 1), :]
     cos[...] = c0 * ic[...] - s0 * isn[...]
     sin[...] = s0 * ic[...] + c0 * isn[...]
@@ -321,43 +321,31 @@
 
 class Pieces:
     def __init__(self, ref, ssem, rsem):
-        self.ref, self.wide, self.ssem, self.rsem = ref, ref.shape[1] == 4, ssem, rsem
+        self.ref, self.wide, self.ssem, self.rsem = ref, ref.shape[3] == 4, ssem, rsem
         self.x, self.y, self.z, self.c = x, y, z, c = coords()
         self.d = 1 - c
+        self.p1 = x * self.d + z * c
+        self.p2 = x * c + z * self.d
         self.across = device(x, y, z, 1 - c)
         self.sends = []
+        self.whole = False
 
     @staticmethod
     def semaphores():
-        return [DMA((44,)), DMA((44,))]
-
-    def slot(self, px, pz, core):
-        place = lax.rem(px, 2) * 4 + pz
-        if self.wide:
-            return self.ref.at[lax.div(px, 2), :, place, core]
-        return self.ref.at[lax.div(px, 2), 0, place, core]
-
-    def back(self, j, k):
-        c, d = self.c, self.d
-        return wrap4(self.x - j * d - k * c), wrap4(self.z - j * c - k * d)
+        return [DMA((32,)), DMA((32,))]
 
     def piece(self, j, k):
-        return self.slot(*self.back(j, k), self.c)
-
-    def piece_across(self, j, k):
-        c, d = self.c, self.d
-        return self.slot(wrap4(self.x - j * c - k * d), wrap4(self.z - j * d - k * c), d)
+        return self.ref.at[self.c, wrap4(self.p2 - k), wrap4(self.p1 - j)]
 
     def send(self, src, dst, n, to):
         self.sends.append(send(src, dst, self.ssem.at[n], self.rsem.at[n], to))
 
     def ahead(self, j, k, r=0):
-        px, pz = self.back(-j, -k)
-        return device(px, wrap4(self.y + r), pz, self.c)
+        c, d = self.c, self.d
+        return device(wrap4(self.x + j * d + k * c), wrap4(self.y + r), wrap4(self.z + j * c + k * d), c)
 
     def from_source(self, j, r):
-        px, pz = self.back(j, 0)
-        return self.ref.at[lax.div(px, 2), wrap4(self.y - r) if self.wide else 0, lax.rem(px, 2) * 4 + pz, self.c]
+        return self.ref.at[self.c, self.p2, wrap4(self.p1 - j), wrap4(self.y - r) if self.wide else 0]
 
     def start(self, parts):
         here = self.from_source(0, 0)
@@ -366,69 +354,80 @@
                 if j or r:
                     src = parts.at[wrap4(self.y + r)] if self.wide else parts
                     self.send(src, here, 4 * j + r, self.ahead(j, 0, r))
-        px, pz = self.back(0, 0)
         if self.wide:
-            self.ref[lax.div(px, 2), self.y, lax.rem(px, 2) * 4 + pz, self.c] = parts[self.y]
+            self.ref[self.c, self.p2, self.p1, self.y] = parts[self.y]
         else:
-            self.ref[lax.div(px, 2), 0, lax.rem(px, 2) * 4 + pz, self.c] = parts[...]
-
-    def pass_on(self, j):
-        for r in range(4) if self.wide else (0,):
-            if j or r:
-                arrived(self.from_source(j, r), self.rsem.at[4 * j + r], self.across)
-        here = self.piece(j, 0)
-        for k in (2, 1, 3):
-            self.send(here, here, 15 + 3 * j + k, self.ahead(0, k))
-        self.send(here, here, 28 + 4 * j, self.across)
-
-    def pass_across(self, j, k):
-        here = self.piece(j, k)
-        arrived(here, self.rsem.at[15 + 3 * j + k], self.across)
-        self.send(here, here, 28 + 4 * j + k, self.across)
+            self.ref[self.c, self.p2, self.p1, 0] = parts[...]
+
+    def start_ring(self, parts):
+        here = self.from_source(0, 0)
+        for r in (2, 1, 3):
+            self.send(parts.at[wrap4(self.y + r)], here, r, self.ahead(0, 0, r))
+        self.ref[self.c, self.p2, self.p1, self.y] = parts[self.y]
+
+    def pass_first(self):
+        for r in (1, 3, 2):
+            arrived(self.from_source(0, r), self.rsem.at[r], self.across)
+        here = self.piece(0, 0)
+        for j in (2, 1, 3):
+            self.send(here, here, 4 * j, self.ahead(j, 0))
+        self.whole = True
 
     def pass_all_on(self):
         for j in (0, 1, 3, 2):
-            self.pass_on(j)
+            if self.whole:
+                if j:
+                    arrived(self.piece(j, 0), self.rsem.at[4 * j], self.across)
+            else:
+                for r in range(4) if self.wide else (0,):
+                    if j or r:
+                        arrived(self.from_source(j, r), self.rsem.at[4 * j + r], self.across)
+            here = self.piece(j, 0)
+            for k in (2, 1, 3):
+                self.send(here, here, 15 + 3 * j + k, self.ahead(0, k))
 
     def pass_all_across(self):
         for j in (0, 1, 3, 2):
             for k in (1, 3, 2):
-                self.pass_across(j, k)
+                arrived(self.piece(j, k), self.rsem.at[15 + 3 * j + k], self.across)
+            here = self.ref.at[self.c, :, wrap4(self.p1 - j)]
+            self.send(here, here, 28 + j, self.across)
 
     def all_here(self):
         for j in range(4):
-            for k in range(4):
-                arrived(self.piece_across(j, k), self.rsem.at[28 + 4 * j + k], self.across)
+            arrived(self.ref.at[self.d, :, wrap4(self.p2 - j)], self.rsem.at[28 + j], self.across)
 
     def done(self):
         for copy in self.sends:
             copy.wait_send()
 
 
-def pack_wide(src, dst):
-    cols = src.shape[-1]
-
-    def rows(i, _):
-        part = src[lax.div(i, 4), lax.rem(i, 4)].astype(F32).reshape(128, cols)
-        dst[pl.ds(pl.multiple_of(i * 128, 128), 128)] = part.astype(BF)
+def pack(src, dst):
+    _, _, _, cut, rows, cols = src.shape
+
+    def block(i, _):
+        px, r = lax.div(i, cut), lax.rem(i, cut)
+        both = jnp.stack([src[0, :, px, r].astype(F32), src[1, px, :, r].astype(F32)], axis=1)
+        first = lax.div(px, 2) * (16 * cut * rows) + r * (16 * rows) + lax.rem(px, 2) * (8 * rows)
+        dst[pl.ds(pl.multiple_of(first, 8 * rows), 8 * rows)] = both.reshape(8 * rows, cols).astype(BF)
         return 0
 
-    lax.fori_loop(0, 8, rows, 0)
-
-
-def pack_down(src, dst):
-    def rows(i, _):
-        part = src[lax.div(i, 4), 0, pl.ds(lax.rem(i, 4) * 2, 2)].astype(F32).reshape(96, 1024)
-        dst[pl.ds(pl.multiple_of(i * 96, 96), 96)] = part.astype(BF)
-        return 0
-
-    lax.fori_loop(0, 8, rows, 0)
+    lax.fori_loop(0, 4 * cut, block, 0)
+
+
+def unpack(part, dst, xh, r):
+    _, _, _, _, rows, cols = dst.shape
+    part = part.reshape(2, 4, 2, rows, cols).astype(BF)
+    for xl in range(2):
+        px = 2 * xh + xl
+        dst[0, :, px, r] = part[xl, :, 0]
+        dst[1, px, :, r] = part[xl, :, 1]
 
 
 class Sums:
     def __init__(self, grad, refs):
-        self.grad, self.cut = grad, grad.shape[1]
-        (self.rc, self.sa, self.lb, self.sb, self.lg, self.ss, self.rs) = refs
+        self.grad, self.cut = grad, grad.shape[3]
+        (self.rc, self.lb, self.lg, self.ss, self.rs) = refs
         x, y, z, c = coords()
         self.y, self.c, self.d = y, c, 1 - c
         d = self.d
@@ -440,53 +439,36 @@
 
     @staticmethod
     def scratch(rows, cols, cut):
-        buffers = [(2, cut, 8), (4, 4, cut), (3, 4, cut), (4, cut), (4, cut)]
+        buffers = [(4, 4, cut), (3, 4, cut), (4, cut)]
         return [pltpu.VMEM(lead + (rows, cols), BF) for lead in buffers] + [DMA((20,)), DMA((20,))]
 
     def send(self, src, dst, n, to):
         self.sends.append(send(src, dst, self.ss.at[n], self.rs.at[n], to))
 
     def start(self):
-        self.send(self.grad.at[:, :, :, self.d], self.rc, 0, self.across)
+        self.send(self.grad.at[self.d], self.rc, 0, self.across)
 
     def cores(self):
         arrived(self.rc, self.rs.at[0], self.across)
-        c, d, cut = self.c, self.d, self.cut
-
-        def add(i, _):
-            a2, a1, r = lax.div(i, 4 * cut), lax.rem(lax.div(i, cut), 4), lax.rem(i, cut)
-            px, pz = a1 * d + a2 * c, a1 * c + a2 * d
-            xh, place = lax.div(px, 2), lax.rem(px, 2) * 4 + pz
-            total = self.rc[xh, r, place].astype(F32) + self.grad[xh, r, place, c].astype(F32)
-            self.sa[a2, a1, r] = total.astype(BF)
-            return 0
-
-        lax.fori_loop(0, 16 * cut, add, 0)
-        for k in (2, 1, 3):
-            self.send(self.sa.at[wrap4(self.p2 + k)], self.lb.at[k - 1], k, self.ahead(0, k, 0))
+        for k in (2, 1, 3, 0):
+            a2 = wrap4(self.p2 + k)
+            self.rc[a2] = (self.rc[a2].astype(F32) + self.grad[self.c, a2].astype(F32)).astype(BF)
+            if k:
+                self.send(self.rc.at[a2], self.lb.at[k - 1], k, self.ahead(0, k, 0))
 
     def second(self):
         for k in (1, 3, 2):
             arrived(self.lb.at[k - 1], self.rs.at[k], self.across)
-
-        def add(i, _):
-            a1, r = lax.div(i, self.cut), lax.rem(i, self.cut)
-            total = self.sa[self.p2, a1, r].astype(F32)
-            for k in range(3):
-                total = total + self.lb[k, a1, r].astype(F32)
-            self.sb[a1, r] = total.astype(BF)
-            return 0
-
-        lax.fori_loop(0, 4 * self.cut, add, 0)
+        total = self.rc[self.p2].astype(F32)
+        for k in range(3):
+            total = total + self.lb[k].astype(F32)
+        self.rc[self.p2] = total.astype(BF)
         for j in (2, 1, 3, 0):
             for r in (2, 1, 3, 0) if self.cut > 1 else (0,):
                 if j or r:
-                    src = self.sb.at[wrap4(self.p1 + j), wrap4(self.y + r) if self.cut > 1 else 0]
+                    src = self.rc.at[self.p2, wrap4(self.p1 + j), wrap4(self.y + r) if self.cut > 1 else 0]
                     self.send(src, self.lg.at[j, r], 4 + 4 * j + r, self.ahead(j, 0, r))
-        if self.cut > 1:
-            self.lg[0, 0] = self.sb[self.p1, self.y]
-        else:
-            self.lg[0, 0] = self.sb[self.p1, 0]
+        self.lg[0, 0] = self.rc[self.p2, self.p1, self.y if self.cut > 1 else 0]
 
     def last(self, r=0):
         total = 0.0
@@ -504,16 +486,16 @@
 def layer_kernel(
     tok, cot, wq, wk, wv, wg, wu, gains, wop, wdp, seg, ic, isn, oc, osn,
     out, igrad, oq, ok, ov, og, ou, oo, od, ogain,
-    kparts, qparts, bparts, wkl, wql, wbl, wdl, wol, wkv, wqs, wb, wd, low, xs, cs, cos, sin, rows, xn, q, kvx, lse,
+    kparts, qparts, bparts, wkl, wql, wbl, wdl, wol, wkv, wqs, wb, wd, wo, low, xs, xs_near, cs, cos, sin, cos_near, sin_near, rows, xn, xnt, q, kvx, lse,
     peak, total, wide, att, part, relay1, land1, acc, unit, dhid, dgu, hid, dpart, relay2, land2, dbr, opart, scale_two, land3,
-    dmid, datt, go, do, inner, dkv, dkvb, land, dqkv, grow, dxq, rsend, rrecv, ssem, rsem, hsem, hrem, *scratch,
+    dmid, datt, do, inner, dkv, dkvb, land, dqkv, grow, dxq, rsend, rrecv, ssem, rsem, hsem, hrem, *scratch,
 ):
     x, y, z, c = coords()
     ring = [device(x, wrap4(y + k), z, c) for k in range(1, 4)]
     take = lambda n: [scratch.pop(0) for _ in range(n)]
     scratch = list(scratch)
     kv, qw, b, o, w = [Pieces(ref, *take(2)) for ref in (wkl, wql, wbl, wol, wdl)]
-    sq, sk, sb, so, sd = [Sums(ref, take(7)) for ref in (wql, wkl, wbl, go, wdl)]
+    sq, sk, sb, so, sd = [Sums(ref, take(5)) for ref in (wql, wkl, wbl, wol, wdl)]
     sends = []
 
     def ring_send(n, k, src, dst):
@@ -530,6 +512,8 @@
     sum_mid = RingSum(dpart, relay2, land2, rsend.at[3], rrecv.at[3])
     branch_in = RingGather(dbr, rsend.at[4], rrecv.at[4])
     sum_x = RingSum(part, relay1, land1, rsend.at[5], rrecv.at[5])
+    near_in = RingGather(xs_near, rsend.at[6], rrecv.at[6])
+    cot_in = RingGather(cs, rsend.at[7], rrecv.at[7])
 
     everyone = greet_all()
     for r in range(4):
@@ -542,6 +526,8 @@
     xs[y] = tok[...]
     everyone()
     kv.start(kparts)
+    near_tok = send(tok, xs_near.at[y], hsem.at[0], hrem.at[0], chunk_device(1))
+    sends.append(near_tok)
     tokens_in.start()
     qw.start(qparts)
     for r in range(4):
@@ -549,19 +535,22 @@
             h = g * 4 + r
             bparts[r, :, g * 384 : g * 384 + 384] = wg[:, h * 384 : h * 384 + 384]
             bparts[r, :, 768 + g * 384 : 1152 + g * 384] = wu[:, h * 384 : h * 384 + 384]
+    b.start_ring(bparts)
     o.start(wop)
+    w.start(wdp)
     cs[y] = cot[...]
     first_keys(seg, low)
-    rope_here(ic, isn, oc, osn, cos, sin)
+    rope_of(0, ic, isn, oc, osn, cos, sin)
     kv.pass_all_on()
     tokens_in.pass_on()
+    near_tok.wait_recv()
+    near_in.start()
+    kv.pass_all_across()
     qw.pass_all_on()
-    kv.pass_all_across()
+    o.pass_all_on()
+    b.pass_first()
     kv.all_here()
-    o.pass_all_on()
-    b.start(bparts)
-    w.start(wdp)
-    pack_wide(wkl, wkv)
+    pack(wkl, wkv)
     for back in (1, 3, 2):
         tokens_in.block(back)
 
@@ -576,21 +565,28 @@
     for r in range(4):
         block = xs[r].astype(F32)
         xn[r * 128 : r * 128 + 128] = (block * rms_scale(block) * attn_gain).astype(BF)
-    near, far = [], []
+
+    def keys_values(rows_in, slot, cos_, sin_, g):
+        raw = dot(rows_in, wkv[:, g * 256 : g * 256 + 256], 1, 0)
+        k_raw = raw[:, :128]
+        kvx[2 * g, slot] = rope(k_raw * rms_scale(k_raw) * k_gain, cos_[...], sin_[...]).astype(BF)
+        kvx[2 * g + 1, slot] = raw[:, 128:].astype(BF)
+
+    far = []
     for g in range(2):
-        raw = dot(xn[...], wkv[:, g * 256 : g * 256 + 256], 1, 0)
-        k_raw = raw[:, :128]
-        kvx[2 * g, 2] = rope(k_raw * rms_scale(k_raw) * k_gain, cos[...], sin[...]).astype(BF)
-        kvx[2 * g + 1, 2] = raw[:, 128:].astype(BF)
+        keys_values(xn[...], 2, cos, sin, g)
         pair = pl.ds(2 * g, 2)
-        near.append(send(kvx.at[pair, 2], kvx.at[pair, 1], hsem.at[g], hrem.at[g], chunk_device(1)))
         far.append(send(kvx.at[pair, 2], kvx.at[pair, 0], hsem.at[2 + g], hrem.at[2 + g], chunk_device(2)))
-    sends += near + far
-    for n in (2, 1, 3):
-        ring_send(1, n, cot, cs.at[y])
+    sends += far
+    near_in.pass_on()
+    w.pass_all_on()
     qw.pass_all_across()
+    rope_of(-1, ic, isn, oc, osn, cos_near, sin_near)
     qw.all_here()
-    pack_wide(wql, wqs)
+    pack(wql, wqs)
+
+    for f in range(8):
+        xnt[f * 128 : f * 128 + 128] = jnp.transpose(xn[:, f * 128 : f * 128 + 128])
 
     def queries(g, _):
         raw = dot(xn[...], wqs[:, pl.ds(pl.multiple_of(g * 256, 256), 256)], 1, 0)
@@ -605,14 +601,21 @@
 
     attend(q, kvx, low, peak, total, wide, 2, True)
     o.pass_all_across()
+    for back in (1, 3, 2):
+        near_in.block(back)
+    cot_in.start()
+    near_in.done()
+    for r in range(4):
+        block = xs_near[r].astype(F32)
+        xs_near[r] = (block * rms_scale(block) * attn_gain).astype(BF)
+    for g in range(2):
+        keys_values(xs_near[...].reshape(CHUNK, 1024), 1, cos_near, sin_near, g)
+    attend(q, kvx, low, peak, total, wide, 1, False)
+    b.pass_all_on()
+    cot_in.pass_on()
     for copy in far:
         copy.wait_recv()
     attend(q, kvx, low, peak, total, wide, 0, False)
-    for copy in near:
-        copy.wait_recv()
-    b.pass_all_on()
-    w.pass_all_on()
-    attend(q, kvx, low, peak, total, wide, 1, False)
     for g in range(2):
         for t in range(2):
             done = jnp.transpose(wide[g, t] / total[g, t]).astype(BF)
@@ -624,10 +627,10 @@
                     att[2 * t + half, :, cols] = done[first : first + 128]
 
     o.all_here()
-    wo = lambda: wol[...].reshape(512, 1024)
+    pack(wol, wo)
     tokens_in.done()
     for n in (2, 1, 3, 0):
-        p = dot(att[wrap4(y + n)], wo(), 1, 0)
+        p = dot(att[wrap4(y + n)], wo[...], 1, 0)
         if n:
             part[n - 1] = p.astype(BF)
             sum_out.give(n)
@@ -635,6 +638,7 @@
             acc[...] = p + tok[...].astype(F32)
     sum_out.relay()
     b.pass_all_across()
+    w.pass_all_across()
     s = sum_out.total(acc[...])
     acc[...] = s
     scale = rms_scale(s)
@@ -643,13 +647,12 @@
     mid[y] = (s * scale * ffn_gain).astype(BF)
     mid_in.start()
     b.all_here()
-    pack_wide(wbl, wb)
+    pack(wbl, wb)
     mid_in.pass_on()
-    w.pass_all_across()
     w.all_here()
-    pack_down(wdl, wd)
-    for n in (1, 3, 2):
-        ring_wait(1, n, cs.at[wrap4(y - n)])
+    pack(wdl, wd)
+    for back in (1, 3, 2):
+        cot_in.block(back)
     for r in range(4):
         dhid[r] = dot(cs[r], wd[...], 1, 1)
 
@@ -673,12 +676,13 @@
             dmid[...] = p
     b.done()
     w.done()
+    o.done()
 
     def gate_up_rows(f, _):
         span = pl.ds(pl.multiple_of(f * 128, 128), 128)
         lhs = mid[:, :, span].reshape(CHUNK, 128)
         g = dot(lhs, dgu[...].reshape(CHUNK, 1536), 0, 0)
-        wbl[lax.div(f, 4), lax.rem(f, 4)] = g.reshape(8, 2, 8, 1536).astype(BF)
+        unpack(g, wbl, lax.div(f, 4), lax.rem(f, 4))
         return 0
 
     lax.fori_loop(0, 8, gate_up_rows, 0)
@@ -688,7 +692,7 @@
         span = pl.ds(pl.multiple_of(f * 384, 384), 384)
         lhs = hid[:, :, span].reshape(CHUNK, 384)
         g = dot(lhs, cs[...].reshape(CHUNK, 1024), 0, 0)
-        wdl[f, 0] = g.reshape(8, 2, 24, 1024).astype(BF)
+        unpack(g, wdl, f, 0)
         return 0
 
     lax.fori_loop(0, 2, down_rows, 0)
@@ -720,7 +724,7 @@
         r = wrap4(y - k)
         if k:
             branch_in.block(k)
-        datt[r] = dot(dbr[r], wo(), 1, 1).astype(BF)
+        datt[r] = dot(dbr[r], wo[...], 1, 1).astype(BF)
     for k in (2, 1, 3):
         ring_send(0, k, opart.at[k - 1], land3.at[k - 1])
 
@@ -754,7 +758,7 @@
         span = pl.ds(pl.multiple_of(f * 256, 256), 256)
         lhs = att[:, :, span].reshape(CHUNK, 256)
         g = dot(lhs, dbr[...].reshape(CHUNK, 1024), 0, 0)
-        go[f, 0] = g.reshape(8, 2, 16, 1024).astype(BF)
+        unpack(g, wol, f, 0)
         return 0
 
     lax.fori_loop(0, 2, out_rows, 0)
@@ -782,8 +786,8 @@
 
     def query_rows(f, _):
         span = pl.ds(pl.multiple_of(f * 128, 128), 128)
-        g = dot(xn[:, span], dqkv[:, :512], 0, 0)
-        wql[lax.div(f, 4), lax.rem(f, 4)] = g.reshape(8, 2, 8, 512).astype(BF)
+        g = dot(xnt[span], dqkv[:, :512], 1, 0)
+        unpack(g, wql, lax.div(f, 4), lax.rem(f, 4))
         of_gain = jnp.sum(g * wqs[span].astype(F32), axis=1, keepdims=True)
         grow[4:5, span] = jnp.transpose(jnp.broadcast_to(of_gain, (128, 128)))[:1]
         return 0
@@ -830,15 +834,13 @@
 
     def key_rows(f, _):
         span = pl.ds(pl.multiple_of(f * 128, 128), 128)
-        g = dot(xn[:, span], dqkv[:, 512:], 0, 0)
-        at = (lax.div(f, 4), lax.rem(f, 4))
-        wkl[at[0], at[1], :, :, :, :512] = g.reshape(8, 2, 8, 512).astype(BF)
+        g = dot(xnt[span], dqkv[:, 512:], 1, 0)
         w_rows = wkv[span].astype(F32)
         tile = jnp.transpose(jnp.concatenate([grow[:, span], jnp.zeros((120, 128), F32)], axis=0))
         d_gain = (tile[:, 4:5] + jnp.sum(g * w_rows[:, :512], axis=1, keepdims=True)) / w_rows[:, 512:513]
         lane = lax.broadcasted_iota(jnp.int32, (128, 128), 1)
         tile = jnp.where(lane == 0, d_gain, tile)
-        wkl[at[0], at[1], :, :, :, 512:] = tile.reshape(8, 2, 8, 128).astype(BF)
+        unpack(jnp.concatenate([g, tile], axis=1), wkl, lax.div(f, 4), lax.rem(f, 4))
         return 0
 
     lax.fori_loop(0, 8, key_rows, 0)
@@ -881,7 +883,7 @@
     ogain[...] = gain
     for copy in sends:
         copy.wait_send()
-    for s in (o, sq, sk, sb, so, sd, tokens_in, mid_in, sum_mid, branch_in, sum_x):
+    for s in (sq, sk, sb, so, sd, tokens_in, mid_in, sum_mid, branch_in, sum_x, cot_in):
         s.done()
 
 
@@ -910,22 +912,27 @@
             mem(4, 8, 640),
             mem(4, 8, 512),
             mem(4, 8, 1536),
-            mem(2, 4, 8, 2, 8, 640),
-            mem(2, 4, 8, 2, 8, 512),
-            mem(2, 4, 8, 2, 8, 1536),
-            mem(2, 1, 8, 2, 24, 1024),
-            mem(2, 1, 8, 2, 16, 1024),
+            mem(2, 4, 4, 4, 8, 640),
+            mem(2, 4, 4, 4, 8, 512),
+            mem(2, 4, 4, 4, 8, 1536),
+            mem(2, 4, 4, 1, 24, 1024),
+            mem(2, 4, 4, 1, 16, 1024),
             mem(1024, 640),
             mem(1024, 512),
             mem(1024, 1536),
             mem(768, 1024),
+            mem(512, 1024),
             pltpu.VMEM((2, 1, 512), jnp.int32),
+            mem(4, *block),
             mem(4, *block),
             mem(4, *block),
             mem32(CHUNK, 128),
             mem32(CHUNK, 128),
+            mem32(CHUNK, 128),
+            mem32(CHUNK, 128),
             mem32(8, 1152),
             mem(CHUNK, 1024),
+            mem(1024, CHUNK),
             mem(2, 2, 512, 128),
             mem(4, 3, CHUNK, 128),
             mem32(2, 2, 1, 512),
@@ -950,7 +957,6 @@
             mem(3, *block),
             mem32(*block),
             mem(4, 128, 512),
-            mem(2, 1, 8, 2, 16, 1024),
             mem(2, 2, 512, 128),
             mem32(2, 2, 1, 512),
             mem32(4, 3, CHUNK, 128),
@@ -959,8 +965,8 @@
             mem(CHUNK, 1024),
             mem32(8, 1024),
             mem32(4, *block),
-            DMA((6, 6)),
-            DMA((6, 6)),
+            DMA((8, 6)),
+            DMA((8, 6)),
             DMA((2, 3)),
             DMA((2, 3)),
             DMA((8,)),

time: 162 us -> 151 us (0.932)
  Pallas kernels: 158 us -> 148 us
    pallas_call x1, Pallas kernels: 156 us -> 146 us  [whole_layer(): pl.pallas_call(layer_kernel, out_shape=(sds(block, BF), sds(block, BF), s...]
where the time goes in v6:
time: 151 us
  Pallas kernels  148 us (98%)
  between operations  2.21 us (1%)
    pallas_call x1, Pallas kernels, whole_layer(): pl.pallas_call(layer_kernel, out_shape=(sds(block, BF), sds(block, BF), s...  146 us

profile of v6, /device:TPU:0, one launch (start us, length us, event | category | flops | bytes accessed | tf_op | source)
XLA Modules:
  0.0 150.9 jit_solution(4072575615700187594)
XLA Ops:
  1.3 0.0 copy-start
  1.3 0.0 copy-start.1
  2.0 0.0 copy-done
  2.0 0.0 copy-done.1
  2.0 0.6 maximum_convert_fusion.gains
  2.6 145.9 %whole_layer.1 = (bf16[128,1024]{1,0:T(8,128)(2,1)}, bf16[128,1024]{1,0:T(8,128)(2,1)}, f32[8,2048]{1,0:T(8,128)}, f32[8,1024]{1,0:T(8,128)}, f32[8,1024]{1,0:T(...) custom-call(bf16[128,1024]{1,0:T(8,128)(2,1)} %tok.1, ...), custom_call_target="tpu_custom_call" | custom-call | tf_op jit(solution)/shard_map/whole_layer/pallas_call | solution.py:895
  148.5 2.2 %results.1 = (bf16[128,1024]{1,0:T(8,128)(2,1)}, bf16[128,1024]{1,0:T(8,128)(2,1)}, f32[8,2048]{1,0:T(8,128)}, f32[8,1024]{1,0:T(8,128)}, f32[8,1024]{1,0:T(8,12...) custom-call(bf16[128,1024]{1,0:T(8,128)(2,1)} %get-tuple-element.36., ...), custom_call_target="tpu_custom_call" | custom-call | tf_op jit(solution)/shard_map/results/pallas_call | solution.py:1000
Async XLA Ops:
  1.3 0.7 copy-start
  1.3 0.7 copy-start.1

commit v7 on v6

--- a/solution.py
+++ b/solution.py
@@ -486,7 +486,7 @@
 def layer_kernel(
     tok, cot, wq, wk, wv, wg, wu, gains, wop, wdp, seg, ic, isn, oc, osn,
     out, igrad, oq, ok, ov, og, ou, oo, od, ogain,
-    kparts, qparts, bparts, wkl, wql, wbl, wdl, wol, wkv, wqs, wb, wd, wo, low, xs, xs_near, cs, cos, sin, cos_near, sin_near, rows, xn, xnt, q, kvx, lse,
+    kparts, qparts, bparts, wkl, wql, wbl, wdl, wol, wkv, wqs, wb, wd, wo, low, xs, xs_near, scales, cs, cos, sin, cos_near, sin_near, rows, xn, xnt, q, kvx, lse,
     peak, total, wide, att, part, relay1, land1, acc, unit, dhid, dgu, hid, dpart, relay2, land2, dbr, opart, scale_two, land3,
     dmid, datt, do, inner, dkv, dkvb, land, dqkv, grow, dxq, rsend, rrecv, ssem, rsem, hsem, hrem, *scratch,
 ):
@@ -549,10 +549,13 @@
     qw.pass_all_on()
     o.pass_all_on()
     b.pass_first()
+    for back in (0, 1, 3, 2):
+        tokens_in.block(back)
+        r = wrap4(y - back)
+        block = xs[r].astype(F32)
+        scales[r] = rms_scale(block)
     kv.all_here()
     pack(wkl, wkv)
-    for back in (1, 3, 2):
-        tokens_in.block(back)
 
     pick = lax.broadcasted_iota(jnp.int32, (8, 128), 0) == lax.broadcasted_iota(jnp.int32, (8, 128), 1)
     by_row = dot(pick.astype(F32).astype(BF), wkv[:, 512:], 1, 1)
@@ -563,8 +566,7 @@
     q_gain, k_gain = rows[2:3, 1024:], rows[3:4, 1024:]
 
     for r in range(4):
-        block = xs[r].astype(F32)
-        xn[r * 128 : r * 128 + 128] = (block * rms_scale(block) * attn_gain).astype(BF)
+        xn[r * 128 : r * 128 + 128] = (xs[r].astype(F32) * scales[r] * attn_gain).astype(BF)
 
     def keys_values(rows_in, slot, cos_, sin_, g):
         raw = dot(rows_in, wkv[:, g * 256 : g * 256 + 256], 1, 0)
@@ -584,9 +586,6 @@
     rope_of(-1, ic, isn, oc, osn, cos_near, sin_near)
     qw.all_here()
     pack(wql, wqs)
-
-    for f in range(8):
-        xnt[f * 128 : f * 128 + 128] = jnp.transpose(xn[:, f * 128 : f * 128 + 128])
 
     def queries(g, _):
         raw = dot(xn[...], wqs[:, pl.ds(pl.multiple_of(g * 256, 256), 256)], 1, 0)
@@ -636,6 +635,8 @@
             sum_out.give(n)
         else:
             acc[...] = p + tok[...].astype(F32)
+    for f in range(8):
+        xnt[f * 128 : f * 128 + 128] = jnp.transpose(xn[:, f * 128 : f * 128 + 128])
     sum_out.relay()
     b.pass_all_across()
     w.pass_all_across()
@@ -699,13 +700,6 @@
     sd.start()
     sum_mid.relay()
     sb.cores()
-    for n in (2, 1, 3, 0):
-        p = dot(hid[wrap4(y + n)], wd[...], 1, 0)
-        if n:
-            opart[n - 1] = p.astype(BF)
-        else:
-            acc[...] = acc[...] + p
-    sd.cores()
 
     s = sum_mid.total(dmid[...])
     grow[...] = jnp.zeros_like(grow)
@@ -716,10 +710,16 @@
     dmid[...] = s
     dbr[y] = s.astype(BF)
     branch_in.start()
+    for n in (2, 1, 3, 0):
+        p = dot(hid[wrap4(y + n)], wd[...], 1, 0)
+        if n:
+            opart[n - 1] = p.astype(BF)
+        else:
+            acc[...] = acc[...] + p
+    sd.cores()
 
     branch_in.pass_on()
     sb.second()
-    sd.second()
     for k in (0, 1, 3, 2):
         r = wrap4(y - k)
         if k:
@@ -752,6 +752,7 @@
 
     attend_back(q, kvx, low, lse, do, inner, dq, dkv, 1, True, lambda g: give_back(g, 1, -1, back_near))
     attend_back(q, kvx, low, lse, do, inner, dq, dkv, 0, False, lambda g: give_back(g, 0, -2, back_far))
+    sd.second()
     sends += back_near + back_far
 
     def out_rows(f, _):
@@ -796,8 +797,6 @@
     sq.start()
     for r in range(4):
         dxq[r] = dot(dqkv[r * 128 : r * 128 + 128, :512], wqs[...], 1, 1)
-    so.cores()
-    sq.cores()
     for n in (1, 3, 2):
         ring_wait(0, n, land3.at[n - 1])
     s = acc[...]
@@ -815,6 +814,8 @@
     sum_out.done()
     for copy in back_near + back_far:
         copy.wait_recv()
+    sq.cores()
+    so.cores()
     g_k = jnp.zeros((1, 128), F32)
     for g in range(2):
         d = dkv[2 * g, 2] + land[0, 2 * g].astype(F32) + land[1, 2 * g].astype(F32)
@@ -858,9 +859,9 @@
             sum_x.give(n)
         else:
             acc[...] = p
+    sk.second()
+    sq.second()
     so.second()
-    sq.second()
-    sk.second()
     s = sum_x.total(acc[...])
     own = tok[...].astype(F32)
     scale_own = rms_scale(own)
@@ -925,6 +926,7 @@
             pltpu.VMEM((2, 1, 512), jnp.int32),
             mem(4, *block),
             mem(4, *block),
+            mem32(4, 128, 1),
             mem(4, *block),
             mem32(CHUNK, 128),
             mem32(CHUNK, 128),

time: 151 us -> 148 us (0.980)
  Pallas kernels: 148 us -> 145 us
    pallas_call x1, Pallas kernels: 146 us -> 143 us  [whole_layer(): pl.pallas_call(layer_kernel, out_shape=(sds(block, BF), sds(block, BF), s...]
where the time goes in v7:
time: 148 us
  Pallas kernels  145 us (98%)
  between operations  2.19 us (1%)
    pallas_call x1, Pallas kernels, whole_layer(): pl.pallas_call(layer_kernel, out_shape=(sds(block, BF), sds(block, BF), s...  143 us

profile of v7, /device:TPU:0, one launch (start us, length us, event | category | flops | bytes accessed | tf_op | source)
XLA Modules:
  0.0 148.0 jit_solution(16910607169940287036)
XLA Ops:
  1.3 0.0 copy-start
  1.3 0.0 copy-start.1
  2.0 0.0 copy-done
  2.0 0.0 copy-done.1
  2.0 0.6 maximum_convert_fusion.gains
  2.6 143.0 %whole_layer.1 = (bf16[128,1024]{1,0:T(8,128)(2,1)}, bf16[128,1024]{1,0:T(8,128)(2,1)}, f32[8,2048]{1,0:T(8,128)}, f32[8,1024]{1,0:T(8,128)}, f32[8,1024]{1,0:T(...) custom-call(bf16[128,1024]{1,0:T(8,128)(2,1)} %tok.1, ...), custom_call_target="tpu_custom_call" | custom-call | tf_op jit(solution)/shard_map/whole_layer/pallas_call | solution.py:896
  145.6 2.2 %results.1 = (bf16[128,1024]{1,0:T(8,128)(2,1)}, bf16[128,1024]{1,0:T(8,128)(2,1)}, f32[8,2048]{1,0:T(8,128)}, f32[8,1024]{1,0:T(8,128)}, f32[8,1024]{1,0:T(8,12...) custom-call(bf16[128,1024]{1,0:T(8,128)(2,1)} %get-tuple-element.36., ...), custom_call_target="tpu_custom_call" | custom-call | tf_op jit(solution)/shard_map/results/pallas_call | solution.py:1002
Async XLA Ops:
  1.3 0.7 copy-start
  1.3 0.7 copy-start.1

commit v8 on v7

--- a/solution.py
+++ b/solution.py
@@ -729,7 +729,8 @@
         ring_send(0, k, opart.at[k - 1], land3.at[k - 1])
 
     ones = jnp.ones((8, 128), BF)
-    for g in range(2):
+
+    def prepare(g):
         for t in range(2):
             for hd in range(2):
                 cols = slice((g * 2 + hd) * 128, (g * 2 + hd) * 128 + 128)
@@ -741,6 +742,8 @@
                     high = prod.astype(BF)
                     rest = (prod - high.astype(F32)).astype(BF)
                     inner[g, t, :, first : first + 128] = (dot(ones, high, 1, 1) + dot(ones, rest, 1, 1))[:1]
+
+    prepare(0)
     dq = wide
     back_near, back_far = [], []
 
@@ -750,7 +753,12 @@
         n = 4 + 2 * slot + g
         copies.append(send(dkvb.at[pair, slot], land.at[slot, pair], hsem.at[n], hrem.at[n], chunk_device(step)))
 
-    attend_back(q, kvx, low, lse, do, inner, dq, dkv, 1, True, lambda g: give_back(g, 1, -1, back_near))
+    def near_done(g):
+        give_back(g, 1, -1, back_near)
+        if g == 0:
+            prepare(1)
+
+    attend_back(q, kvx, low, lse, do, inner, dq, dkv, 1, True, near_done)
     attend_back(q, kvx, low, lse, do, inner, dq, dkv, 0, False, lambda g: give_back(g, 0, -2, back_far))
     sd.second()
     sends += back_near + back_far

time: 148 us -> 148 us (level)
  no operation moved by 1% of the time
where the time goes in v8:
time: 148 us
  Pallas kernels  145 us (98%)
  between operations  2.19 us (1%)
    pallas_call x1, Pallas kernels, whole_layer(): pl.pallas_call(layer_kernel, out_shape=(sds(block, BF), sds(block, BF), s...  143 us

profile of v8, /device:TPU:0, one launch (start us, length us, event | category | flops | bytes accessed | tf_op | source)
XLA Modules:
  0.0 148.0 jit_solution(11122550472563560265)
XLA Ops:
  1.3 0.0 copy-start
  1.3 0.0 copy-start.1
  2.0 0.0 copy-done
  2.0 0.0 copy-done.1
  2.0 0.6 maximum_convert_fusion.gains
  2.6 143.0 %whole_layer.1 = (bf16[128,1024]{1,0:T(8,128)(2,1)}, bf16[128,1024]{1,0:T(8,128)(2,1)}, f32[8,2048]{1,0:T(8,128)}, f32[8,1024]{1,0:T(8,128)}, f32[8,1024]{1,0:T(...) custom-call(bf16[128,1024]{1,0:T(8,128)(2,1)} %tok.1, ...), custom_call_target="tpu_custom_call" | custom-call | tf_op jit(solution)/shard_map/whole_layer/pallas_call | solution.py:904
  145.6 2.2 %results.1 = (bf16[128,1024]{1,0:T(8,128)(2,1)}, bf16[128,1024]{1,0:T(8,128)(2,1)}, f32[8,2048]{1,0:T(8,128)}, f32[8,1024]{1,0:T(8,128)}, f32[8,1024]{1,0:T(8,12...) custom-call(bf16[128,1024]{1,0:T(8,128)(2,1)} %get-tuple-element.36., ...), custom_call_target="tpu_custom_call" | custom-call | tf_op jit(solution)/shard_map/results/pallas_call | solution.py:1010
Async XLA Ops:
  1.3 0.7 copy-start
  1.3 0.7 copy-start.1
